TPU v7x, 32 devices: a whole 2x2x4 slice. The times are simulated.
32 devices in a mesh: img: 8 (over z, x), proto: 4 (over y, core).
Axes of the slice: x: 2, y: 2, z: 4, core: 2. Of those that a mesh axis runs over, the one named last changes fastest.
Arguments:
- student_feats: bfloat16 [8, 128, 384], P('img'), may hold values from -1 to 1
- teacher_feats: bfloat16 [8, 128, 384], P('img'), may hold values from -1 to 1
- student_weight: bfloat16 [384, 131072], P(None, ('img', 'proto')), may hold values from -1 to 1
- teacher_weight: bfloat16 [384, 131072], P(None, ('img', 'proto')), may hold values from -1 to 1
- patch_masks: int32 [8, 128], P('img'), may hold values from 0 to 1, as said below
Outputs:
- patch_loss: float32 [], replicated
- grad_weight: float32 [384, 131072], P(None, ('img', 'proto'))
- grad_rows: float32 [512, 384], P(('img', 'proto'))
Inputs may be any that keep to these rules, and one draw needn't show every extreme that they name: `patch_masks`: exactly 4 images have masked patches, chosen at random; a quarter of these each have 128 / 8, 32, 48 and 64 masked patches at random positions, so 160 patches are masked in all.
All inputs are finite; a program needn't handle non-finite values.
Results may differ from a plain program's by a relative error of at most 0.0085.
Values may be sent and summed in bfloat16 or wider, within the bound.
No kernel may reach another device: no remote copies, remote signals or barrier semaphores. Data moves between devices by JAX's collectives and lax.ppermute only.
A program may use at most 64 MiB of HBM per device.

v0:
```python
import jax
import jax.numpy as jnp
from jax import lax
from jax.sharding import PartitionSpec as P

P_SIZE = 131072
PATCH = 128
ITERS = 3


TEACHER_TEMP = 0.07
STUDENT_TEMP = 0.1
NORM_EPS = 1e-06


def slot_rows(features, mask_rows, slot_count):
    rank_of = jnp.cumsum(mask_rows, axis=1) - 1
    slot_ids = jnp.arange(slot_count, dtype=jnp.int32)
    select = (
        (mask_rows[:, None, :] == 1) & (rank_of[:, None, :] == slot_ids[None, :, None])
    ).astype(jnp.bfloat16)
    return jnp.einsum("isp,ipe->ise", select, features, preferred_element_type=jnp.float32)


def unit_rows(slot_data):
    norm_rows = jnp.sqrt(jnp.sum(slot_data * slot_data, axis=-1) + NORM_EPS)
    return ((slot_data / norm_rows[..., None]).astype(jnp.bfloat16), norm_rows)


def unit_columns(weight):
    w_float = weight.astype(jnp.float32)
    norm_cols = jnp.sqrt(jnp.sum(w_float * w_float, axis=0) + NORM_EPS)
    return ((w_float / norm_cols[None, :]).astype(jnp.bfloat16), norm_cols)


def summed_mass(row_part):
    return lax.psum(row_part, ("img", "proto"))


def shards(student_feats, teacher_feats, student_weight, teacher_weight, patch_masks):
    slot_count = PATCH // 2
    stu_local, stu_norm = unit_rows(slot_rows(student_feats, patch_masks, slot_count))
    tea_local, _ = unit_rows(slot_rows(teacher_feats, patch_masks, slot_count))
    local_counts = jnp.sum(patch_masks, axis=1).astype(jnp.bfloat16)
    stu_all, tea_all, count_all = (
        lax.all_gather(stu_local, "img", axis=0, tiled=True),
        lax.all_gather(tea_local, "img", axis=0, tiled=True),
        lax.all_gather(local_counts, "img", axis=0, tiled=True),
    )
    feature_width = stu_all.shape[-1]
    stu_flat = stu_all.reshape(-1, feature_width)
    tea_flat = tea_all.reshape(-1, feature_width)
    slot_total = stu_flat.shape[0]
    rows_total = slot_total * 5 // 16
    count_f = count_all.astype(jnp.float32)
    masked_images = jnp.sum((count_f > 0).astype(jnp.float32))
    valid_slot = (jnp.arange(slot_count, dtype=jnp.float32)[None, :] < count_f[:, None]).reshape(-1)
    slot_weight = jnp.where(
        valid_slot, 1.0 / (jnp.repeat(jnp.maximum(count_f, 1.0), slot_count) * masked_images), 0.0
    )
    w_unit, w_norm = unit_columns(student_weight)
    tea_w_unit, _ = unit_columns(teacher_weight)
    packed_ids = jnp.nonzero(valid_slot, size=rows_total)[0].astype(jnp.int32)
    stu_use = stu_flat[packed_ids]
    tea_use = tea_flat[packed_ids]
    row_weight = slot_weight[packed_ids]
    live_rows = jnp.ones((rows_total,), jnp.float32)
    logits = jnp.dot(stu_use, w_unit, preferred_element_type=jnp.float32) / STUDENT_TEMP
    stu_exp = jnp.exp(logits)
    kernel = jnp.exp(
        jnp.dot(tea_use, tea_w_unit, preferred_element_type=jnp.float32) / TEACHER_TEMP
    )
    row_scale = live_rows
    partition = lax.psum(jnp.sum(stu_exp, axis=1), ("img", "proto"))
    first_sweep = 0
    for sweep_idx in range(first_sweep, ITERS):
        col_scale = 1.0 / jnp.dot(row_scale, kernel, precision=lax.Precision.HIGHEST)
        row_totals = summed_mass(jnp.dot(kernel, col_scale, precision=lax.Precision.HIGHEST))
        row_scale = live_rows / jnp.where(live_rows > 0, row_totals, 1.0)
    targets = row_scale[:, None] * kernel * col_scale[None, :]
    log_part = jnp.log(partition)
    loss_part = jnp.sum(row_weight * jnp.sum(targets * (log_part[:, None] - logits), axis=1))
    probability = stu_exp / partition[:, None]
    grad_logits = (
        row_weight[:, None] * rows_total * (probability - targets) / STUDENT_TEMP
    ).astype(jnp.bfloat16)
    grad_unit_w = lax.dot_general(
        stu_use, grad_logits, (((0,), (0,)), ((), ())), preferred_element_type=jnp.float32
    )
    w_float = w_unit.astype(jnp.float32)
    grad_weight = (
        P_SIZE
        / 128.0
        * (grad_unit_w - w_float * jnp.sum(w_float * grad_unit_w, axis=0)[None, :])
        / w_norm[None, :]
    )
    grad_unit_x = lax.dot_general(
        grad_logits, w_unit, (((1,), (1,)), ((), ())), preferred_element_type=jnp.float32
    )
    patch_loss = lax.psum(loss_part, ("img", "proto"))
    local_slots = stu_local.shape[0] * slot_count
    own_count = local_slots // lax.axis_size("proto")
    row_start = lax.axis_index("proto") * own_count
    grad_unit_x = (
        jnp.zeros((slot_total, feature_width), jnp.float32).at[packed_ids].set(grad_unit_x)
    )
    own_rows = lax.psum_scatter(grad_unit_x, ("img", "proto"), scatter_dimension=0, tiled=True)
    own_unit = lax.dynamic_slice_in_dim(
        stu_local.reshape(-1, feature_width), row_start, own_count, 0
    ).astype(jnp.float32)
    own_norm = lax.dynamic_slice_in_dim(stu_norm.reshape(-1), row_start, own_count, 0)
    grad_rows = (own_rows - own_unit * jnp.sum(own_unit * own_rows, axis=1)[:, None]) / own_norm[
        :, None
    ]
    return (patch_loss, grad_weight, grad_rows)


def solution(mesh):
    placed = (
        P("img", None, None),
        P("img", None, None),
        P(None, ("img", "proto")),
        P(None, ("img", "proto")),
        P("img", None),
    )
    return jax.shard_map(
        shards,
        mesh=mesh,
        in_specs=placed,
        out_specs=(P(), P(None, ("img", "proto")), P(("img", "proto"), None)),
        check_vma=False,
    )
```

profile of v0, /device:TPU:0, one launch (start us, length us, event | category | flops | bytes accessed | tf_op | source)
XLA Modules:
  0.0 361.4 jit_solution(17699387748589014894)
XLA Ops:
  7.2 1.4 reduce_sum.108
  9.4 1.2 dynamic-slice.7
  10.6 0.8 dynamic-update-slice
  12.0 23.1 %all-reduce.1 = bf16[8]{0:T(256)(128)(2,1)S(1)} all-reduce(bf16[8]{0:T(256)(128)(2,1)S(1)} %dynamic-update-slice), channel_id=1, replica_groups=mesh['img'=8,'proto'=4] {'img'}, use_global_device_ids=true, to_apply=%add.1 | all-reduce | flops 8 | bytes 32
  38.0 4.1 %scatter_custom_fusion = s32[160]{0:T(256)S(1)} fusion(s32[512]{0:T(512)S(1)} %bitcast.61, s32[512]{0:T(512)S(1)} %broadcast.169, s32[]{:T(128)} %constant.31.clone.1), kind=kCustom, calls=%fused_computation.82 | custom fusion | flops 512 | bytes 644 | tf_op jit(solution)/shard_map/scatter-add | solution.py:63
  43.6 1.6 gather_fusion
  45.2 2.6 fusion
  49.6 31.1 %all-gather = bf16[512,384]{1,0:T(8,128)(2,1)S(1)} all-gather(bf16[64,384]{1,0:T(8,128)(2,1)S(1)} %divide_convert_fusion.1), channel_id=2, replica_groups=mesh['img'=8,'proto'=4] {'img'}, dimensions={0}, use_global_device_ids=true | all-gather | bytes 442368 | tf_op jit(solution)/shard_map/all_gather | solution.py:47
  80.6 0.9 gather_fusion.1
  81.7 31.0 %all-gather.1 = bf16[512,384]{1,0:T(8,128)(2,1)S(1)} all-gather(bf16[64,384]{1,0:T(8,128)(2,1)S(1)} %divide_convert_fusion), channel_id=3, replica_groups=mesh['img'=8,'proto'=4] {'img'}, dimensions={0}, use_global_device_ids=true | all-gather | bytes 442368 | tf_op jit(solution)/shard_map/all_gather | solution.py:46
  112.7 0.9 gather_fusion.2
  113.6 2.9 fusion.8
  116.5 1.3 fusion.29
  117.8 2.1 fusion.37
  120.0 37.0 %psum.35 = f32[160]{0:T(256)S(1)} all-reduce(f32[160]{0:T(256)S(1)} %bitcast.57), channel_id=1, replica_groups=mesh['img'=8,'proto'=4] {'img','proto'}, use_global_device_ids=true, to_apply=%region_11.12 | all-reduce | flops 160 | bytes 1280 | tf_op jit(solution)/shard_map/psum | solution.py:37
  157.0 1.3 fusion.38
  158.3 2.1 fusion.39
  160.5 42.3 %psum.36 = f32[160]{0:T(256)S(1)} all-reduce(f32[160]{0:T(256)S(1)} %bitcast.59), channel_id=1, replica_groups=mesh['img'=8,'proto'=4] {'img','proto'}, use_global_device_ids=true, to_apply=%region_12.13 | all-reduce | flops 160 | bytes 1280 | tf_op jit(solution)/shard_map/psum | solution.py:37
  202.8 1.3 fusion.40
  204.1 2.1 fusion.41
  206.3 2.7 exponential_reduce_fusion
  208.9 38.3 %all-reduce.2 = (f32[160]{0:T(256)S(1)}, f32[160]{0:T(256)S(1)}) all-reduce(f32[160]{0:T(256)S(1)} %get-tuple-element.11, f32[160]{0:T(256)S(1)} %bitcast.56), channel_id=1, replica_groups=mesh['img'=8,'proto'=4] {'img','proto'}, use_global_device_ids=true, to_apply=%region_17.18 | all-reduce | flops 320 | bytes 2560 | tf_op jit(solution)/shard_map/psum | solution.py:74
  247.3 3.2 multiply_convert_fusion
  250.6 1.1 copy-done.5
  251.6 1.8 fusion.34
  253.4 2.5 scatter_custom_fusion.1
  255.9 5.1 %fusion.4 = (f32[4096]{0:T(1024)S(1)}, f32[384,4096]{1,0:T(8,128)}) fusion(f32[4096]{0:T(1024)S(1)} %add_sqrt_fusion, bf16[384,4096]{1,0:T(8,128)(2,1)S(1)} %copy-done.4, bf16[160,384]{1,0:T(8,128)(2,1)S(1)} %gather_fusion.2, bf16[160,4096]{1,0:T(8,128)(2,1)} %copy-done.5), kind=kOutput, calls=%fused_computation.15 | convolution fusion | flops 512749568 | bytes 10903552 | tf_op jit(solution)/shard_map/dot_general | solution.py:87
  261.7 41.8 %psum.39 = f32[]{:T(128)} all-reduce(f32[]{:T(128)} %multiply_reduce_fusion.3), channel_id=1, replica_groups=mesh['img'=8,'proto'=4] {'img','proto'}, use_global_device_ids=true, to_apply=%region_20.21 | all-reduce | flops 1 | bytes 8 | tf_op jit(solution)/shard_map/psum | solution.py:100
  303.5 5.6 %fusion.7 = f32[384,4096]{1,0:T(8,128)} fusion(f32[384,4096]{1,0:T(8,128)} %get-tuple-element.14, f32[4096]{0:T(1024)S(1)} %get-tuple-element.13, f32[4096]{0:T(1024)S(1)} %add_sqrt_fusion, bf16[384,4096]{1,0:T(8,128)(2,1)S(1)} %copy-done.4), kind=kLoop, calls=%fused_computation.18 | loop fusion | flops 12582912 | bytes 15761408 | tf_op jit(solution)/shard_map/div | solution.py:92
  309.1 43.3 %reduce-scatter.2.cloned.1.call-done = f32[16,384]{1,0:T(8,128)} async-done(((f32[512,384]{1,0:T(8,128)}), f32[16,384]{1,0:T(8,128)}) %reduce-scatter.2.cloned.1.call-update) | async-done | bytes 24592 | tf_op jit(solution)/shard_map/reduce_scatter | solution.py:107
  352.3 0.9 fusion.19
  353.2 1.4 fusion.21
  (68 shorter events, 7.6 us)
Async XLA Ops:
  7.2 41.8 %copy-start = (bf16[1,128,384]{2,1,0:T(8,128)(2,1)S(1)}, bf16[1,128,384]{2,1,0:T(8,128)(2,1)}, u32[]{:S(2)}) copy-start(bf16[1,128,384]{2,1,0:T(8,128)(2,1)} %param.5) | copy-start | bytes 294916
  7.2 40.6 %copy-start.1 = (bf16[384,4096]{1,0:T(8,128)(2,1)S(1)}, bf16[384,4096]{1,0:T(8,128)(2,1)}, u32[]{:S(2)}) copy-start(bf16[384,4096]{1,0:T(8,128)(2,1)} %param.7) | copy-start | bytes 9437188
  7.2 345.1 %reduce-scatter.2.cloned.1.call-start = ((), (), s32[]{:S(2)}) async-start(), calls=%async_computation.1 | async-start | bytes 811008 | tf_op jit(solution)/shard_map/reduce_scatter | solution.py:107
  45.2 3.3 copy-start.7
  47.8 1.4 copy-start.6
  202.8 3.5 copy-start.2
  247.3 4.3 %copy-start.3 = (bf16[384,4096]{1,0:T(8,128)(2,1)S(1)}, bf16[384,4096]{1,0:T(8,128)(2,1)}, u32[]{:S(2)}) copy-start(bf16[384,4096]{1,0:T(8,128)(2,1)} %param.7) | copy-start | bytes 9437188
  250.5 1.1 copy-start.5
  251.6 4.3 %copy-start.4 = (bf16[384,4096]{1,0:T(8,128)(2,1)S(1)}, bf16[384,4096]{1,0:T(8,128)(2,1)}, u32[]{:S(2)}) copy-start(bf16[384,4096]{1,0:T(8,128)(2,1)} %param.7) | copy-start | bytes 9437188
Sparse Core Ops, SparseCore 0:
  256.1 96.2 reduce-scatter.1
where the time goes:
time: 362 us; the launch traced here: 361 us
  blocking collectives  245 us (68%)
  waiting for transfers between devices  43.3 us (12%)
  other arithmetic  25.2 us (7%)
  matrix products  23.4 us (6%)
  between operations  14.9 us (4%)
  local copies, waits for them, and re-layouts  10 us (3%)
    psum x2, blocking collectives, summed_mass(): return lax.psum(row_part, ('img', 'proto'))  79.3 us
    reduce_scatter x1, waiting for transfers between devices, shards(): lax.psum_scatter(grad_unit_x, ('img', 'proto'), scatter_dimension=0, tile...  43.3 us
    psum x1, blocking collectives, shards(): patch_loss = lax.psum(loss_part, ('img', 'proto'))  41.8 us
    psum x1, blocking collectives, shards(): partition = lax.psum(jnp.sum(stu_exp, axis=1), ('img', 'proto'))  38.3 us
    all_gather x1, blocking collectives, shards(): lax.all_gather(tea_local, 'img', axis=0, tiled=True)  31.1 us
    all_gather x1, blocking collectives, shards(): lax.all_gather(stu_local, 'img', axis=0, tiled=True)  31 us
    unnamed x1, blocking collectives  23.1 us
  transfers between devices with their start and end apart: 1, of which 1 were waited for; matrix products, arithmetic and copies ran while one was open for 3% of the time, Pallas kernels for 0%

commit v1 on v0

v1 whole, which is shorter than its diff:
```python
import functools

import jax
import jax.numpy as jnp
from jax import lax
from jax.experimental import pallas as pl
from jax.experimental.pallas import tpu as pltpu
from jax.sharding import PartitionSpec as P

ITERS = 3
TEACHER_TEMP = 0.07
STUDENT_TEMP = 0.1
NORM_EPS = 1e-06
GRAD_SCALE = 1.0 / 128.0
EMPTY = 2.0
LANES = 128
F32 = jnp.float32
BF16 = jnp.bfloat16
AXES = ("img", "proto")

VMEM = pl.BlockSpec(memory_space=pltpu.VMEM)
SMEM = pl.BlockSpec(memory_space=pltpu.SMEM)


def call(body, outs, *args, flops=0, moved=0, exps=0):
    return pl.pallas_call(
        body,
        out_shape=outs,
        in_specs=[VMEM] * len(args),
        out_specs=jax.tree.map(lambda _: VMEM, outs),
        compiler_params=pltpu.CompilerParams(vmem_limit_bytes=56 * 1024 * 1024),
        cost_estimate=pl.CostEstimate(flops=flops, bytes_accessed=moved, transcendentals=exps),
    )(*args)


def dot(a, b, dims):
    return lax.dot_general(a, b, (dims, ((), ())), preferred_element_type=F32)


def iota(shape, dim):
    return lax.broadcasted_iota(jnp.int32, shape, dim)


def sds(shape, dtype):
    return jax.ShapeDtypeStruct(shape, dtype)


def to_column(row, rows):
    wide = jnp.broadcast_to(row, (LANES, row.shape[1]))
    return wide.T[:rows]


def to_row(part, width):
    rows = part.shape[0]
    if width > rows:
        part = jnp.concatenate([part, jnp.zeros((width - rows, LANES), F32)], axis=0)
    return jnp.sum(part.T, axis=0, keepdims=True)


def fold(x):
    parts = [x[:, i : i + LANES] for i in range(0, x.shape[1], LANES)]
    return functools.reduce(jnp.add, parts)


def spread(col, width):
    return jnp.concatenate([col] * (width // LANES), axis=1)


def chunks(columns):
    step = min(512, columns)
    return step, columns // step


def select_kernel(mask_ref, stu_ref, tea_ref, tea_out, stu_out, unit_out, norm_out):
    own = unit_out.shape[0]
    patches = mask_ref.shape[1]
    slot = iota((own, patches), 0) + lax.axis_index("proto") * own
    mask = jnp.broadcast_to(mask_ref[...].astype(F32), (own, patches))
    upto = (iota((patches, patches), 0) <= iota((patches, patches), 1)).astype(BF16)
    rank = dot(mask.astype(BF16), upto, ((1,), (0,)))
    pick = jnp.where((rank == slot.astype(F32) + 1.0) & (mask > 0.5), 1.0, 0.0).astype(BF16)
    valid = slot[:, :1].astype(F32) < rank[:, patches - 1 :]
    for source, target in ((tea_ref, tea_out), (stu_ref, stu_out)):
        rows = dot(pick, source[0], ((1,), (0,)))
        norm = jnp.sqrt(jnp.sum(rows * rows, axis=1, keepdims=True) + NORM_EPS)
        unit = (rows / norm).astype(BF16)
        sent = jnp.where(valid, unit.astype(F32), EMPTY).astype(BF16)
        target[...] = jnp.broadcast_to(sent[None], target.shape)
        if source is stu_ref:
            unit_out[...] = unit.astype(F32)
            norm_out[...] = jnp.broadcast_to(norm, norm_out.shape)


def norms_kernel(stu_w, tea_w, stu_out, tea_out):
    step, count = chunks(stu_w.shape[1])
    for ref, out in ((tea_w, tea_out), (stu_w, stu_out)):

        def body(i, _, ref=ref, out=out):
            at = pl.ds(pl.multiple_of(i * step, step), step)
            w = ref[:, at].astype(F32)
            out[:, at] = 1.0 / jnp.sqrt(jnp.sum(w * w, axis=0, keepdims=True) + NORM_EPS)
            return 0

        lax.fori_loop(0, count, body, 0)


def packing(slots_ref, rows, emit):
    total, width = slots_ref.shape
    step = min(512, total)
    before = jnp.zeros((1, 1), F32)
    upto = (iota((step, step), 0) <= iota((step, step), 1)).astype(BF16)
    for c in range(total // step):
        data = slots_ref[c * step : (c + 1) * step, :]
        flags = jnp.where(data[:, :LANES].astype(F32) < 1.5, 1.0, 0.0).astype(BF16)
        upto_here = dot(flags, upto, ((0,), (0,)))[:1]
        own = dot(flags, (iota((step, step), 0) == iota((step, step), 1)).astype(BF16), ((0,), (0,)))[:1]
        place = before + upto_here
        row = iota((rows, step), 0).astype(F32) + 1.0
        hot = jnp.where((row == place) & (own > 0.5), 1.0, 0.0).astype(BF16)
        emit(c, hot, data, flags)
        before = place[:, step - 1 :]


def pack_rows(slots_ref, rows):
    parts = []
    packing(slots_ref, rows, lambda c, hot, data, flags: parts.append(dot(hot, data, ((1,), (0,)))))
    return functools.reduce(jnp.add, parts).astype(BF16)


def first_kernel(tea_all, tea_w, inv, kernel_out, sent_out, *, rows):
    x = pack_rows(tea_all, rows)
    step, count = chunks(tea_w.shape[1])

    def body(i, acc):
        at = pl.ds(pl.multiple_of(i * step, step), step)
        z = dot(x, tea_w[:, at], ((1,), (0,)))
        k = jnp.exp(z * (inv[:, at] * (1.0 / TEACHER_TEMP)))
        kernel_out[:, at] = k
        c = 1.0 / jnp.sum(k, axis=0, keepdims=True)
        return acc + fold(k * c)

    acc = lax.fori_loop(0, count, body, jnp.zeros((rows, LANES), F32))
    row = to_row(acc, sent_out.shape[2])
    sent_out[...] = jnp.broadcast_to(row[None], sent_out.shape)


def student_kernel(stu_all, stu_w, inv, logits_out, part_out, x_out, hot_out, weight_out, *, per_image):
    rows = x_out.shape[0]
    state = {"x": [], "count": [], "images": []}

    def emit(c, hot, data, flags):
        step = data.shape[0]
        state["x"].append(dot(hot, data, ((1,), (0,))))
        hot_out[:, c * step : (c + 1) * step] = hot
        same = (iota((step, step), 0) // per_image == iota((step, step), 1) // per_image).astype(BF16)
        held = dot(same, flags, ((1,), (0,)))
        state["count"].append(dot(hot, held.astype(BF16), ((1,), (0,))))
        first = (iota(held.shape, 0) % per_image == 0) & (held > 0.5)
        state["images"].append(jnp.sum(first.astype(F32), axis=0, keepdims=True))

    packing(stu_all, rows, emit)
    add = functools.partial(functools.reduce, jnp.add)
    x = add(state["x"]).astype(BF16)
    x_out[...] = x
    weight_out[...] = 1.0 / (jnp.maximum(add(state["count"]), 1.0) * add(state["images"]))
    step, count = chunks(stu_w.shape[1])

    def body(i, acc):
        at = pl.ds(pl.multiple_of(i * step, step), step)
        l = dot(x, stu_w[:, at], ((1,), (0,))) * (inv[:, at] * (1.0 / STUDENT_TEMP))
        logits_out[:, at] = l
        return acc + fold(jnp.exp(l))

    acc = lax.fori_loop(0, count, body, jnp.zeros((rows, LANES), F32))
    part_out[...] = to_row(acc, part_out.shape[1])


def sweep_kernel(got, kernel, sent_out):
    rows, columns = kernel.shape
    scale = to_column(1.0 / jnp.sum(got[...], axis=0), rows)
    step, count = chunks(columns)
    wide = spread(scale, step)

    def body(i, acc):
        at = pl.ds(pl.multiple_of(i * step, step), step)
        k = kernel[:, at]
        c = 1.0 / jnp.sum(k * wide, axis=0, keepdims=True)
        return acc + fold(k * c)

    acc = lax.fori_loop(0, count, body, jnp.zeros((rows, LANES), F32))
    row = to_row(acc, sent_out.shape[2])
    sent_out[...] = jnp.broadcast_to(row[None], sent_out.shape)


def last_sweep_kernel(got, kernel, logits, part, scaled_out, sent_out):
    rows, columns = kernel.shape
    width = part.shape[1]
    scale = to_column(1.0 / jnp.sum(got[...], axis=0), rows)
    step, count = chunks(columns)
    wide = spread(scale, step)

    def body(i, accs):
        at = pl.ds(pl.multiple_of(i * step, step), step)
        k = kernel[:, at]
        kc = k / jnp.sum(k * wide, axis=0, keepdims=True)
        scaled_out[:, at] = kc
        return accs[0] + fold(kc), accs[1] + fold(kc * logits[:, at])

    zero = jnp.zeros((rows, LANES), F32)
    total, cross = lax.fori_loop(0, count, body, (zero, zero))
    row = jnp.concatenate([to_row(total, width), to_row(cross, width), part[...]], axis=1)
    sent_out[...] = jnp.broadcast_to(row[None], sent_out.shape)


def grads_kernel(got, scaled, logits, stu_w, inv, hot, weight, sent_out, grad_out, along_out, loss_out):
    rows, columns = scaled.shape
    width = got.shape[2] // 3
    sums = jnp.sum(got[...], axis=0)
    total = to_column(sums[:, :width], rows)
    cross = to_column(sums[:, width : 2 * width], rows)
    partition = to_column(sums[:, 2 * width :], rows)
    share = weight[...]
    loss = jnp.sum(share * (jnp.log(partition) - cross / total), axis=0, keepdims=True)
    loss_out[...] = loss[:, :1]
    factor = share * (rows / STUDENT_TEMP)
    step, count = chunks(columns)
    grow = spread(factor / partition, step)
    shrink = spread(factor / total, step)

    def body(i, acc):
        at = pl.ds(pl.multiple_of(i * step, step), step)
        l = logits[:, at]
        g = grow * jnp.exp(l) - shrink * scaled[:, at]
        n = inv[:, at]
        along_out[:, at] = jnp.sum(g * l, axis=0, keepdims=True) * STUDENT_TEMP
        gn = (g * n).astype(BF16)
        grad_out[:, at] = gn
        return acc + dot(gn, stu_w[:, at], ((1,), (1,)))

    acc = lax.fori_loop(0, count, body, jnp.zeros((rows, stu_w.shape[0]), F32))
    spots = dot(hot[...], acc.astype(BF16), ((0,), (0,)))
    sent_out[...] = spots.astype(BF16).reshape(sent_out.shape)


def weight_grad_kernel(x, grad, along, inv, stu_w, out, *, scale):
    n = inv[...]
    direct = dot(x[...], grad[...], ((0,), (0,)))
    out[...] = scale * (direct - stu_w[...].astype(F32) * (along[...] * n * n))


def rows_kernel(got, unit, norm, out):
    full = jnp.sum(got[...].astype(F32), axis=0)
    u = unit[...]
    out[...] = (full - u * jnp.sum(u * full, axis=1, keepdims=True)) / norm[:, :1]


def shards(student_feats, teacher_feats, student_weight, teacher_weight, patch_masks):
    devices = lax.axis_size(AXES)
    protos = lax.axis_size("proto")
    images, patches, feat = student_feats.shape
    assert images == 1
    columns = student_weight.shape[1]
    per_image = patches // 2
    own = per_image // protos
    slots = own * devices
    rows = slots * 5 // 16
    width = -(-rows // LANES) * LANES
    big = rows * columns
    exchange = functools.partial(lax.all_to_all, axis_name=AXES, split_axis=0, concat_axis=0)

    tea_sent, stu_sent, unit, norm = call(
        select_kernel,
        (
            sds((devices, own, feat), BF16),
            sds((devices, own, feat), BF16),
            sds((own, feat), F32),
            sds((own, LANES), F32),
        ),
        patch_masks,
        student_feats,
        teacher_feats,
    )
    tea_all = exchange(tea_sent).reshape(slots, feat)
    stu_all = exchange(stu_sent).reshape(slots, feat)
    stu_inv, tea_inv = call(
        norms_kernel,
        (sds((1, columns), F32), sds((1, columns), F32)),
        student_weight,
        teacher_weight,
        flops=4 * feat * columns,
        moved=4 * feat * columns,
    )
    vector = sds((devices, 1, width), F32)
    kernel, sent = call(
        functools.partial(first_kernel, rows=rows),
        (sds((rows, columns), F32), vector),
        tea_all,
        teacher_weight,
        tea_inv,
        flops=2 * big * feat,
        moved=4 * big,
        exps=big,
    )
    got = exchange(sent)
    logits, part, x, hot, weight = call(
        functools.partial(student_kernel, per_image=per_image),
        (
            sds((rows, columns), F32),
            sds((1, width), F32),
            sds((rows, feat), BF16),
            sds((rows, slots), BF16),
            sds((rows, LANES), F32),
        ),
        stu_all,
        student_weight,
        stu_inv,
        flops=2 * big * feat,
        moved=4 * big,
        exps=big,
    )
    for _ in range(ITERS - 2):
        sent = call(sweep_kernel, vector, got, kernel, flops=4 * big, moved=4 * big)
        got = exchange(sent)
    scaled, sent = call(
        last_sweep_kernel,
        (sds((rows, columns), F32), sds((devices, 1, 3 * width), F32)),
        got,
        kernel,
        logits,
        part,
        flops=6 * big,
        moved=12 * big,
    )
    got = exchange(sent)
    sent, grad, along, loss = call(
        grads_kernel,
        (
            sds((devices, own, feat), BF16),
            sds((rows, columns), BF16),
            sds((1, columns), F32),
            sds((1, 1), F32),
        ),
        got,
        scaled,
        logits,
        student_weight,
        stu_inv,
        hot,
        weight,
        flops=2 * big * feat,
        moved=8 * big,
        exps=big,
    )
    got = exchange(sent)
    step = min(512, columns)
    grad_weight = pl.pallas_call(
        functools.partial(weight_grad_kernel, scale=columns * devices * GRAD_SCALE),
        out_shape=sds((feat, columns), F32),
        grid=(columns // step,),
        in_specs=[
            pl.BlockSpec((rows, feat), lambda i: (0, 0)),
            pl.BlockSpec((rows, step), lambda i: (0, i)),
            pl.BlockSpec((1, step), lambda i: (0, i)),
            pl.BlockSpec((1, step), lambda i: (0, i)),
            pl.BlockSpec((feat, step), lambda i: (0, i)),
        ],
        out_specs=pl.BlockSpec((feat, step), lambda i: (0, i)),
        cost_estimate=pl.CostEstimate(flops=2 * big * feat, bytes_accessed=6 * feat * columns, transcendentals=0),
    )(x, grad, along, stu_inv, student_weight)
    grad_rows = call(rows_kernel, sds((own, feat), F32), got, unit, norm)
    return loss.reshape(()), grad_weight, grad_rows


def solution(mesh):
    placed = (
        P("img", None, None),
        P("img", None, None),
        P(None, AXES),
        P(None, AXES),
        P("img", None),
    )
    return jax.shard_map(
        shards,
        mesh=mesh,
        in_specs=placed,
        out_specs=(P(), P(None, AXES), P(AXES, None)),
        check_vma=False,
    )
```

time: 362 us -> 112 us (0.31)
  blocking collectives: 245 us -> 23.5 us
  Pallas kernels: 0 us -> 45.4 us
  other arithmetic: 25.2 us -> 0 us
  matrix products: 23.4 us -> 0 us
  waiting for transfers between devices: 43.3 us -> 24.2 us
  starting transfers between devices: 0.04 us -> 15 us
  between operations: 14.9 us -> 0.68 us
  local copies, waits for them, and re-layouts: 10 us -> 2.1 us
    psum x4 -> x0, blocking collectives: 159 us -> none  [the longest x2 79.3 us: summed_mass(): return lax.psum(row_part, ('img', 'proto'))]
    all_gather x2 -> x0, blocking collectives: 62 us -> none  [the longest x1 31.1 us: shards(): lax.all_gather(tea_local, 'img', axis=0, tiled=True)]
    pallas_call x0 -> x9, Pallas kernels: none -> 45.4 us  [the longest x8 36.9 us: call(): pl.pallas_call(body, out_shape=outs, in_specs=[VMEM] * len(args), out_spe...]
    reduce_scatter x1 -> x0, waiting for transfers between devices: 43.3 us -> none  [shards(): lax.psum_scatter(grad_unit_x, ('img', 'proto'), scatter_dimension=0, tile...]
    all_to_all x0 -> x4, waiting for transfers between devices: none -> 24.2 us  [the longest x1 10 us: shards(): stu_all = exchange(stu_sent).reshape(slots, feat)]
    all_to_all x0 -> x2, blocking collectives: none -> 23.5 us  [shards(): got = exchange(sent)]
    dot_general x12 -> x0, matrix products: 23.4 us -> none  [the longest x3 6.4 us: shards(): jnp.dot(kernel, col_scale, precision=lax.Precision.HIGHEST)]
    unnamed x1 -> x0, blocking collectives: 23.1 us -> none
  transfers between devices with their start and end apart: 1 -> 4, of which waited for: 1 -> 4; matrix products, arithmetic and copies ran while one was open for 3% -> 0% of each run, Pallas kernels for 0% -> 20%
where the time goes in v1:
time: 112 us; the launch traced here: 111 us
  Pallas kernels  45.4 us (41%)
  waiting for transfers between devices  24.2 us (22%)
  blocking collectives  23.5 us (21%)
  starting transfers between devices  15 us (13%)
  local copies, waits for them, and re-layouts  2.1 us (2%)
    pallas_call x8, Pallas kernels, call(): pl.pallas_call(body, out_shape=outs, in_specs=[VMEM] * len(args), out_spe...  36.9 us
    all_to_all x2, blocking collectives, shards(): got = exchange(sent)  23.5 us
    all_to_all x1, waiting for transfers between devices, shards(): stu_all = exchange(stu_sent).reshape(slots, feat)  10 us
    all_to_all x1, waiting for transfers between devices, shards(): tea_all = exchange(tea_sent).reshape(slots, feat)  8.81 us
    pallas_call x1, Pallas kernels, shards(): pl.pallas_call(functools.partial(weight_grad_kernel, scale=columns * devi...  8.52 us
    all_to_all x1, starting transfers between devices, shards(): tea_all = exchange(tea_sent).reshape(slots, feat)  7.3 us
    all_to_all x2, waiting for transfers between devices, shards(): got = exchange(sent)  5.39 us
    all_to_all x2, starting transfers between devices, shards(): got = exchange(sent)  5.15 us
  transfers between devices with their start and end apart: 4, of which 4 were waited for; matrix products, arithmetic and copies ran while one was open for 0% of the time, Pallas kernels for 20%

profile of v1, /device:TPU:0, one launch (start us, length us, event | category | flops | bytes accessed | tf_op | source)
XLA Modules:
  0.0 110.9 jit_solution(5382094407686943008)
XLA Ops:
  0.6 2.2 %shard_map.76 = (bf16[32,16,384]{2,1,0:T(8,128)(2,1)}, bf16[32,16,384]{2,1,0:T(8,128)(2,1)}, f32[16,384]{1,0:T(8,128)}, f32[16,128]{1,0:T(8,128)}) custom-call(s32[1,128]{1,0:T(1,128)} %mask_ref.1, bf16[1,128,384]{2,1,0:T(8,128)(2,1)} %stu_ref.1, bf16[1,128,384]{2,1,0:T(8,128)(2,1)} %tea_ref.1), custom_call_target="tpu_custom_call" | custom-call | tf_op jit(solution)/shard_map/pallas_call | solution.py:26
  2.9 7.3 %all-to-all-start = ((bf16[32,16,384]{2,1,0:T(8,128)(2,1)}), bf16[32,16,384]{2,1,0:T(8,128)(2,1)S(1)}, u32[]{:S(2)}, u32[]{:S(2)}) async-start(bf16[32,16,384]{2,1,0:T(8,128)(2,1)} %get-tuple-element.22), calls=%async_computation | async-start | bytes 786432 | tf_op jit(solution)/shard_map/all_to_all | solution.py:283
  10.2 4.4 %shard_map.77 = (f32[1,4096]{1,0:T(1,128)}, f32[1,4096]{1,0:T(1,128)}) custom-call(bf16[384,4096]{1,0:T(8,128)(2,1)} %stu_w.7, bf16[384,4096]{1,0:T(8,128)(2,1)} %tea_w.3), custom_call_target="tpu_custom_call" | custom-call | flops 6291456 | bytes 6291456 | tf_op jit(solution)/shard_map/pallas_call | solution.py:26
  14.5 8.8 %all-to-all-done = bf16[32,16,384]{2,1,0:T(8,128)(2,1)S(1)} async-done(((bf16[32,16,384]{2,1,0:T(8,128)(2,1)}), bf16[32,16,384]{2,1,0:T(8,128)(2,1)S(1)}, u32[]{:S(2)}, u32[]{:S(2)}) %all-to-all-start) | async-done | bytes 393248 | tf_op jit(solution)/shard_map/all_to_all | solution.py:283
  23.3 0.0 copy-start.2
  23.3 0.7 copy-done.2
  24.1 6.4 %shard_map.78 = (f32[160,4096]{1,0:T(8,128)}, f32[32,1,256]{2,1,0:T(1,128)}) custom-call(bf16[512,384]{1,0:T(8,128)(2,1)} %bitcast.4, bf16[384,4096]{1,0:T(8,128)(2,1)} %tea_w.3, f32[1,4096]{1,0:T(1,128)} %get-tuple-element.23.inv), custom_call_target="tpu_custom_call" | custom-call | flops 503316480 | bytes 2621440 | tf_op jit(solution)/shard_map/pallas_call | solution.py:26
  30.5 10.4 %all_to_all.30.got = f32[32,1,256]{2,1,0:T(1,128)} all-to-all(f32[32,1,256]{2,1,0:T(1,128)} %get-tuple-element.24), channel_id=1, replica_groups=mesh['img'=8,'proto'=4] {'img','proto'}, dimensions={0} | all-to-all | bytes 65536 | tf_op jit(solution)/shard_map/all_to_all | solution.py:304
  40.9 2.6 %all-to-all-start.3 = ((bf16[32,16,384]{2,1,0:T(8,128)(2,1)}), bf16[32,16,384]{2,1,0:T(8,128)(2,1)S(1)}, u32[]{:S(2)}, u32[]{:S(2)}) async-start(bf16[32,16,384]{2,1,0:T(8,128)(2,1)} %get-tuple-element.26), calls=%async_computation.3 | async-start | bytes 786432 | tf_op jit(solution)/shard_map/all_to_all | solution.py:284
  43.5 3.1 %shard_map.79 = f32[32,1,256]{2,1,0:T(1,128)} custom-call(f32[32,1,256]{2,1,0:T(1,128)} %all_to_all.30.got, f32[160,4096]{1,0:T(8,128)} %get-tuple-element.25.kernel), custom_call_target="tpu_custom_call" | custom-call | flops 2621440 | bytes 2621440 | tf_op jit(solution)/shard_map/pallas_call | solution.py:26
  46.6 10.0 %all-to-all-done.3 = bf16[32,16,384]{2,1,0:T(8,128)(2,1)S(1)} async-done(((bf16[32,16,384]{2,1,0:T(8,128)(2,1)}), bf16[32,16,384]{2,1,0:T(8,128)(2,1)S(1)}, u32[]{:S(2)}, u32[]{:S(2)}) %all-to-all-start.3) | async-done | bytes 393248 | tf_op jit(solution)/shard_map/all_to_all | solution.py:284
  56.7 0.0 copy-start
  56.7 2.6 %all-to-all-start.2 = ((f32[32,1,256]{2,1,0:T(1,128)}), f32[32,1,256]{2,1,0:T(1,128)S(1)}, u32[]{:S(2)}, u32[]{:S(2)}) async-start(f32[32,1,256]{2,1,0:T(1,128)} %shard_map.79), calls=%async_computation.2 | async-start | bytes 65536 | tf_op jit(solution)/shard_map/all_to_all | solution.py:323
  59.3 0.0 copy-done
  59.3 6.5 %shard_map.80 = (f32[160,4096]{1,0:T(8,128)}, f32[1,256]{1,0:T(1,128)}, bf16[160,384]{1,0:T(8,128)(2,1)}, bf16[160,512]{1,0:T(8,128)(2,1)}, f32[160,128]{1,0:T(8,128)}) custom-call(bf16[512,384]{1,0:T(8,128)(2,1)} %bitcast.3, bf16[384,4096]{1,0:T(8,128)(2,1)} %stu_w.7, f32[1,4096]{1,0:T(1,128)} %get-tuple-element.27.inv), custom_call_target="tpu_custom_call" | custom-call | flops 503316480 | bytes 2621440 | tf_op jit(solution)/shard_map/pallas_call | solution.py:26
  65.8 0.7 all-to-all-done.2.got
  66.5 0.0 copy-start.3
  66.5 0.6 copy-done.3
  67.1 5.0 %shard_map.81 = (f32[160,4096]{1,0:T(8,128)}, f32[32,1,768]{2,1,0:T(1,128)}) custom-call(f32[32,1,256]{2,1,0:T(1,128)} %copy-done.3, f32[160,4096]{1,0:T(8,128)} %get-tuple-element.25.kernel, f32[160,4096]{1,0:T(8,128)} %get-tuple-element.28.logits, f32[1,256]{1,0:T(1,128)} %get-tuple-element.29.part), custom_call_target="tpu_custom_call" | custom-call | flops 3932160 | bytes 7864320 | tf_op jit(solution)/shard_map/pallas_call | solution.py:26
  72.1 13.0 %all_to_all.31.got = f32[32,1,768]{2,1,0:T(1,128)} all-to-all(f32[32,1,768]{2,1,0:T(1,128)} %get-tuple-element.30), channel_id=1, replica_groups=mesh['img'=8,'proto'=4] {'img','proto'}, dimensions={0} | all-to-all | bytes 196608 | tf_op jit(solution)/shard_map/all_to_all | solution.py:334
  85.2 7.5 %shard_map.82 = (bf16[32,16,384]{2,1,0:T(8,128)(2,1)}, bf16[160,4096]{1,0:T(8,128)(2,1)}, f32[1,4096]{1,0:T(1,128)}, f32[1,1]{1,0:T(1,128)}) custom-call(f32[32,1,768]{2,1,0:T(1,128)} %all_to_all.31.got, f32[160,4096]{1,0:T(8,128)} %get-tuple-element.31.scaled, f32[160,4096]{1,0:T(8,128)} %get-tuple-element.28.logits, bf16[384,4096]{1,0:T(8,128)(2,1)} %stu_w.7, ...), custom_call_target="tpu_custom_call" | custom-call | flops 503316480 | bytes 5242880 | tf_op jit(solution)/shard_map/pallas_call | solution.py:26
  92.6 2.6 %all-to-all-start.5 = ((bf16[32,16,384]{2,1,0:T(8,128)(2,1)}), bf16[32,16,384]{2,1,0:T(8,128)(2,1)S(1)}, u32[]{:S(2)}, u32[]{:S(2)}) async-start(bf16[32,16,384]{2,1,0:T(8,128)(2,1)} %get-tuple-element.38), calls=%async_computation.5 | async-start | bytes 786432 | tf_op jit(solution)/shard_map/all_to_all | solution.py:354
  95.2 8.5 %shard_map.83 = f32[384,4096]{1,0:T(8,128)} custom-call(bf16[160,384]{1,0:T(8,128)(2,1)} %get-tuple-element.35.x, bf16[160,4096]{1,0:T(8,128)(2,1)} %get-tuple-element.36.grad, f32[1,4096]{1,0:T(1,128)} %get-tuple-element.37.along, f32[1,4096]{1,0:T(1,128)} %get-tuple-element.27.inv, bf16[384,4096]{1,0:T(8,128)(2,1)} %stu_w.7), custom_call_target="tpu_custom_call" | custom-call | flops 503316480 | bytes 9437184 | tf_op jit(solution)/shard_map/pallas_call | solution.py:356
  103.8 4.7 %all-to-all-done.5.got = bf16[32,16,384]{2,1,0:T(8,128)(2,1)S(1)} async-done(((bf16[32,16,384]{2,1,0:T(8,128)(2,1)}), bf16[32,16,384]{2,1,0:T(8,128)(2,1)S(1)}, u32[]{:S(2)}, u32[]{:S(2)}) %all-to-all-start.5) | async-done | bytes 393248 | tf_op jit(solution)/shard_map/all_to_all | solution.py:354
  108.4 0.0 copy-start.1
  108.4 0.8 copy-done.1
  109.2 1.8 %shard_map.84 = f32[16,384]{1,0:T(8,128)} custom-call(bf16[32,16,384]{2,1,0:T(8,128)(2,1)} %copy-done.1, f32[16,384]{1,0:T(8,128)} %get-tuple-element.39.unit, f32[16,128]{1,0:T(8,128)} %get-tuple-element.40.norm), custom_call_target="tpu_custom_call" | custom-call | tf_op jit(solution)/shard_map/pallas_call | solution.py:26
Async XLA Ops:
  2.9 20.5 %all-to-all-start = ((bf16[32,16,384]{2,1,0:T(8,128)(2,1)}), bf16[32,16,384]{2,1,0:T(8,128)(2,1)S(1)}, u32[]{:S(2)}, u32[]{:S(2)}) async-start(bf16[32,16,384]{2,1,0:T(8,128)(2,1)} %get-tuple-element.22), calls=%async_computation | async-start | bytes 786432 | tf_op jit(solution)/shard_map/all_to_all | solution.py:283
  23.3 0.7 copy-start.2
  40.9 15.8 %all-to-all-start.3 = ((bf16[32,16,384]{2,1,0:T(8,128)(2,1)}), bf16[32,16,384]{2,1,0:T(8,128)(2,1)S(1)}, u32[]{:S(2)}, u32[]{:S(2)}) async-start(bf16[32,16,384]{2,1,0:T(8,128)(2,1)} %get-tuple-element.26), calls=%async_computation.3 | async-start | bytes 786432 | tf_op jit(solution)/shard_map/all_to_all | solution.py:284
  56.7 2.6 %copy-start = (bf16[32,16,384]{2,1,0:T(8,128)(2,1)}, bf16[32,16,384]{2,1,0:T(8,128)(2,1)S(1)}, u32[]{:S(2)}) copy-start(bf16[32,16,384]{2,1,0:T(8,128)(2,1)S(1)} %all-to-all-done.3) | copy-start | bytes 1179652
  56.7 9.8 %all-to-all-start.2 = ((f32[32,1,256]{2,1,0:T(1,128)}), f32[32,1,256]{2,1,0:T(1,128)S(1)}, u32[]{:S(2)}, u32[]{:S(2)}) async-start(f32[32,1,256]{2,1,0:T(1,128)} %shard_map.79), calls=%async_computation.2 | async-start | bytes 65536 | tf_op jit(solution)/shard_map/all_to_all | solution.py:323
  66.5 0.6 copy-start.3
  92.6 15.8 %all-to-all-start.5 = ((bf16[32,16,384]{2,1,0:T(8,128)(2,1)}), bf16[32,16,384]{2,1,0:T(8,128)(2,1)S(1)}, u32[]{:S(2)}, u32[]{:S(2)}) async-start(bf16[32,16,384]{2,1,0:T(8,128)(2,1)} %get-tuple-element.38), calls=%async_computation.5 | async-start | bytes 786432 | tf_op jit(solution)/shard_map/all_to_all | solution.py:354
  108.4 0.8 copy-start.1

commit v2 on v1

v2 whole, which is shorter than its diff:
```python
import functools

import jax
import jax.numpy as jnp
from jax import lax
from jax.experimental import pallas as pl
from jax.experimental.pallas import tpu as pltpu
from jax.sharding import PartitionSpec as P

ITERS = 3
TEACHER_TEMP = 0.07
STUDENT_TEMP = 0.1
NORM_EPS = 1e-06
GRAD_SCALE = 1.0 / 128.0
EMPTY = 2.0
LANES = 128
F32 = jnp.float32
BF16 = jnp.bfloat16
AXES = ("img", "proto")

VMEM = pl.BlockSpec(memory_space=pltpu.VMEM)


def call(body, outs, *args, flops=0, moved=0, exps=0, limit=24):
    return pl.pallas_call(
        body,
        out_shape=outs,
        in_specs=[VMEM] * len(args),
        out_specs=tuple(VMEM for _ in outs),
        compiler_params=pltpu.CompilerParams(vmem_limit_bytes=limit * 1024 * 1024),
        cost_estimate=pl.CostEstimate(flops=flops, bytes_accessed=moved, transcendentals=exps),
    )(*args)


def near(x):
    return pltpu.with_memory_space_constraint(x, pltpu.VMEM)


def dot(a, b, dims, precision=None):
    return lax.dot_general(a, b, (dims, ((), ())), precision=precision, preferred_element_type=F32)


def iota(shape, dim):
    return lax.broadcasted_iota(jnp.int32, shape, dim)


def add_all(parts):
    return functools.reduce(jnp.add, parts)


def to_column(vector, rows):
    parts = [jnp.broadcast_to(vector[i : i + 1], (LANES, LANES)).T for i in range(vector.shape[0])]
    return jnp.concatenate(parts, axis=0)[:rows]


def to_tiles(part, width):
    rows = part.shape[0]
    if width > rows:
        part = jnp.concatenate([part, jnp.zeros((width - rows, LANES), F32)], axis=0)
    row = jnp.sum(part.T, axis=0, keepdims=True)
    return jnp.concatenate([row[:, i : i + LANES] for i in range(0, width, LANES)], axis=0)


def split(tiles):
    high = tiles.astype(BF16).astype(F32)
    return [high, tiles - high]


def fold(x):
    return add_all([x[:, i : i + LANES] for i in range(0, x.shape[1], LANES)])


def spread(col, width):
    return jnp.concatenate([col] * (width // LANES), axis=1)


def chunks(columns):
    step = min(512, columns)
    return step, columns // step


def odd_half():
    return lax.rem(lax.axis_index("proto"), 2)


def select_kernel(mask_ref, stu_ref, tea_ref, sent_out, unit_out, norm_out):
    own, feat = unit_out.shape
    patches = mask_ref.shape[1]
    slot = iota((own, patches), 0) + lax.axis_index("proto") * own
    mask = jnp.broadcast_to(mask_ref[...].astype(F32), (own, patches))
    upto = (iota((patches, patches), 0) <= iota((patches, patches), 1)).astype(BF16)
    rank = dot(mask.astype(BF16), upto, ((1,), (0,)))
    pick = jnp.where((rank == slot.astype(F32) + 1.0) & (mask > 0.5), 1.0, 0.0).astype(BF16)
    valid = slot[:, :1].astype(F32) < rank[:, patches - 1 :]
    for source, at in ((tea_ref, 0), (stu_ref, feat)):
        rows = dot(pick, source[0], ((1,), (0,)))
        norm = jnp.sqrt(jnp.sum(rows * rows, axis=1, keepdims=True) + NORM_EPS)
        unit = (rows / norm).astype(BF16)
        sent = jnp.where(valid, unit.astype(F32), EMPTY).astype(BF16)
        sent_out[:, :, at : at + feat] = jnp.broadcast_to(sent[None], (sent_out.shape[0], own, feat))
        if source is stu_ref:
            unit_out[...] = unit.astype(F32)
            norm_out[...] = jnp.broadcast_to(norm, norm_out.shape)


def norms_kernel(stu_w, tea_w, stu_out, tea_out):
    step, count = chunks(stu_w.shape[1])
    for ref, out in ((tea_w, tea_out), (stu_w, stu_out)):

        def body(i, _, ref=ref, out=out):
            at = pl.ds(pl.multiple_of(i * step, step), step)
            w = ref[:, at].astype(F32)
            out[:, at] = 1.0 / jnp.sqrt(jnp.sum(w * w, axis=0, keepdims=True) + NORM_EPS)
            return 0

        lax.fori_loop(0, count, body, 0)


def packing(mine, other, at, feat, rows, emit):
    half = mine.shape[0]
    step = min(256, half)
    before = jnp.zeros((1, 1), F32)
    upto = (iota((step, step), 0) <= iota((step, step), 1)).astype(BF16)
    same = (iota((step, step), 0) == iota((step, step), 1)).astype(BF16)
    row = iota((rows, step), 0).astype(F32) + 1.0
    for h in range(2):
        for c in range(0, half, step):
            block = slice(c, c + step), slice(at, at + feat)
            data = jnp.where(odd_half() == h, mine[block], other[block])
            flags = jnp.where(data[:, :LANES].astype(F32) < 1.5, 1.0, 0.0).astype(BF16)
            place = before + dot(flags, upto, ((0,), (0,)))[:1]
            held = dot(flags, same, ((0,), (0,)))[:1]
            hot = jnp.where((row == place) & (held > 0.5), 1.0, 0.0).astype(BF16)
            emit(h * half + c, hot, data, flags)
            before = place[:, step - 1 :]


def first_kernel(mine, other, tea_w, inv, kernel_out, sent_out):
    rows = kernel_out.shape[0]
    feat = tea_w.shape[0]
    parts = []
    packing(mine, other, 0, feat, rows, lambda at, hot, data, flags: parts.append(dot(hot, data, ((1,), (0,)))))
    x = add_all(parts).astype(BF16)
    step, count = chunks(tea_w.shape[1])

    def body(i, acc):
        at = pl.ds(pl.multiple_of(i * step, step), step)
        z = dot(x, tea_w[:, at], ((1,), (0,)))
        k = jnp.exp(z * (inv[:, at] * (1.0 / TEACHER_TEMP)))
        kernel_out[:, at] = k
        c = 1.0 / jnp.sum(k, axis=0, keepdims=True)
        return acc + fold(k * c)

    acc = lax.fori_loop(0, count, body, jnp.zeros((rows, LANES), F32))
    tiles = to_tiles(acc, sent_out.shape[1] * LANES)
    sent_out[...] = jnp.broadcast_to(tiles[None], sent_out.shape)


def spots(hot, x, at, half):
    return dot(hot[:, at : at + half], x, ((0,), (0,)))


def halves(hot, x, keep_out, give_out):
    half = keep_out.shape[0]
    low, high = spots(hot, x, 0, half), spots(hot, x, half, half)
    odd = odd_half() == 1
    keep_out[...] = jnp.where(odd, high, low)
    give_out[...] = jnp.where(odd, low, high)


def student_kernel(
    mine, other, stu_w, inv, logits_out, part_out, x_out, hot_out, own_out, weight_out, keep_out, give_out, *, protos
):
    rows, feat = x_out.shape
    devices = lax.axis_size(AXES)
    each = mine.shape[0] // devices
    per_image = each * protos
    packed, count, images = [], [], []

    def emit(at, hot, data, flags):
        step = data.shape[0]
        packed.append(dot(hot, data, ((1,), (0,))))
        hot_out[:, at : at + step] = hot

    packing(mine, other, feat, feat, rows, emit)
    x = add_all(packed).astype(BF16)
    x_out[...] = x

    half = mine.shape[0]
    step = min(256, half)
    block = lax.broadcasted_iota(jnp.int32, (step, step), 0) // per_image
    same = (block == iota((step, step), 1) // per_image).astype(BF16)
    for c in range(0, half, step):
        flags = [
            jnp.where(ref[c : c + step, feat : feat + LANES].astype(F32) < 1.5, 1.0, 0.0) for ref in (mine, other)
        ]
        held = dot(same, (flags[0] + flags[1]).astype(BF16), ((1,), (0,)))
        for h in range(2):
            hot = hot_out[:, h * half + c : h * half + c + step]
            count.append(dot(hot, held.astype(BF16), ((1,), (0,))))
        first = (iota(held.shape, 0) % per_image == 0) & (held > 0.5)
        images.append(jnp.sum(first.astype(F32), axis=0, keepdims=True))
    weight_out[...] = 1.0 / (jnp.maximum(add_all(count), 1.0) * add_all(images))

    own = own_out.shape[0]
    me = lax.axis_index("img") * protos + lax.axis_index("proto")
    q = iota((own, 2 * half), 0)
    spot = q // each * half + me * each + q % each
    mark = (iota((own, 2 * half), 1) == spot).astype(BF16)
    own_out[...] = dot(mark, hot_out[...], ((1,), (1,)))

    step, count = chunks(stu_w.shape[1])

    def body(i, accs):
        at = pl.ds(pl.multiple_of(i * step, step), step)
        w = stu_w[:, at]
        n = inv[:, at]
        l = dot(x, w, ((1,), (0,))) * (n * (1.0 / STUDENT_TEMP))
        logits_out[:, at] = l
        p = jnp.exp(l)
        return accs[0] + fold(p), accs[1] + dot((p * n).astype(BF16), w, ((1,), (1,)))

    zeros = jnp.zeros((rows, LANES), F32), jnp.zeros((rows, feat), F32)
    acc, pull = lax.fori_loop(0, count, body, zeros)
    part_out[...] = to_tiles(acc, part_out.shape[0] * LANES)
    halves(hot_out, pull.astype(BF16), keep_out, give_out)


def fill(sent_out, keep, got, vectors):
    devices, each, wide = sent_out.shape
    feat = keep.shape[1]
    sent_out[:, :, :feat] = (keep[...] + got[...]).reshape(devices, each, feat).astype(BF16)
    tiles = add_all_rows([part for vector in vectors for part in split(vector)], each, (wide - feat) // LANES)
    sent_out[:, :, feat:] = jnp.broadcast_to(tiles[None], (devices, each, wide - feat)).astype(BF16)


def add_all_rows(parts, each, groups):
    tiles = jnp.concatenate(parts, axis=0)
    spare = each * groups - tiles.shape[0]
    if spare:
        tiles = jnp.concatenate([tiles, jnp.zeros((spare, LANES), F32)], axis=0)
    return jnp.concatenate([tiles[g * each : (g + 1) * each] for g in range(groups)], axis=1)


def vectors_of(got, feat, width, count):
    _, each, wide = got.shape
    sums = jnp.sum(got[:, :, feat:].astype(F32), axis=0)
    tiles = jnp.concatenate([sums[:, g : g + LANES] for g in range(0, wide - feat, LANES)], axis=0)
    m = width // LANES
    return [tiles[2 * v * m : (2 * v + 1) * m] + tiles[(2 * v + 1) * m : (2 * v + 2) * m] for v in range(count)]


def slots_of(got, feat):
    devices, each, _ = got.shape
    parts = got[:, :, :feat].astype(F32).reshape(devices // 2, 2, each, feat)
    return jnp.sum(parts, axis=0).reshape(2 * each, feat)


def sweep_kernel(got, kernel, part, keep, give, sent_out):
    rows, columns = kernel.shape
    width = part.shape[0] * LANES
    scale = to_column(1.0 / jnp.sum(got[...], axis=0), rows)
    step, count = chunks(columns)
    wide = spread(scale, step)

    def body(i, acc):
        at = pl.ds(pl.multiple_of(i * step, step), step)
        k = kernel[:, at]
        c = 1.0 / jnp.sum(k * wide, axis=0, keepdims=True)
        return acc + fold(k * c)

    acc = lax.fori_loop(0, count, body, jnp.zeros((rows, LANES), F32))
    fill(sent_out, keep, give, [to_tiles(acc, width), part[...]])


def last_sweep_kernel(
    got, kernel, logits, stu_w, inv, hot, scaled_out, total_out, cross_out, keep_out, give_out
):
    rows, columns = kernel.shape
    feat = stu_w.shape[0]
    width = total_out.shape[0] * LANES
    (total,) = vectors_of(got, feat, width, 1)
    scale = to_column(1.0 / total, rows)
    step, count = chunks(columns)
    wide = spread(scale, step)

    def body(i, accs):
        at = pl.ds(pl.multiple_of(i * step, step), step)
        k = kernel[:, at]
        kc = k * (1.0 / jnp.sum(k * wide, axis=0, keepdims=True))
        scaled_out[:, at] = kc
        kn = (kc * inv[:, at]).astype(BF16)
        return (
            accs[0] + fold(kc),
            accs[1] + fold(kc * logits[:, at]),
            accs[2] + dot(kn, stu_w[:, at], ((1,), (1,))),
        )

    zero = jnp.zeros((rows, LANES), F32)
    total, cross, push = lax.fori_loop(0, count, body, (zero, zero, jnp.zeros((rows, feat), F32)))
    total_out[...] = to_tiles(total, width)
    cross_out[...] = to_tiles(cross, width)
    halves(hot, push.astype(BF16), keep_out, give_out)


def fill_kernel(keep, got, total, cross, sent_out):
    fill(sent_out, keep, got, [total[...], cross[...]])


def prepare_kernel(got, scaled, logits, inv, weight, own, pull_out, push_out, rise_out, loss_out, *, scale):
    rows, columns = scaled.shape
    feat = rise_out.shape[1]
    width = -(-rows // LANES) * LANES
    _, partition = vectors_of(got, feat, width, 2)
    partition = to_column(partition, rows)
    share = weight[...]
    loss_out[...] = jnp.log(partition)
    factor = share * (rows / STUDENT_TEMP)
    step, count = chunks(columns)
    grow, shrink = spread(factor / partition, step), spread(factor, step)

    def body(i, _):
        at = pl.ds(pl.multiple_of(i * step, step), step)
        n = inv[:, at] * scale
        pull_out[:, at] = grow * jnp.exp(logits[:, at]) * n
        push_out[:, at] = shrink * scaled[:, at] * n
        return 0

    lax.fori_loop(0, count, body, 0)
    held = dot(own[...], factor / partition, ((1,), (0,)), lax.Precision.HIGHEST)
    rise_out[...] = slots_of(got, feat) * held[:, :1]


def final_kernel(
    got, pull, push, logits, inv, stu_w, x, weight, own, rise, log_part, unit, norm, out, rows_out, loss_out, scale_ref
):
    rows = pull.shape[0]
    feat = x.shape[1]
    width = -(-rows // LANES) * LANES

    @pl.when(pl.program_id(0) == 0)
    def _():
        total, cross = (to_column(v, rows) for v in vectors_of(got, feat, width, 2))
        scale = 1.0 / total
        scale_ref[...] = scale
        share = weight[...]
        loss = jnp.sum(share * (log_part[...] - cross * scale), axis=0, keepdims=True)
        loss_out[...] = loss[:, :1]
        held = dot(own[...], share * (rows / STUDENT_TEMP) * scale, ((1,), (0,)), lax.Precision.HIGHEST)
        full = rise[...] - slots_of(got, feat) * held[:, :1]
        u = unit[...]
        rows_out[...] = (full - u * jnp.sum(u * full, axis=1, keepdims=True)) / norm[:, :1]

    g = pull[...] - spread(scale_ref[...], pull.shape[1]) * push[...]
    along = jnp.sum(g * logits[...], axis=0, keepdims=True) * (inv[...] * STUDENT_TEMP)
    out[...] = dot(x[...], g.astype(BF16), ((0,), (0,))) - stu_w[...].astype(F32) * along


def shards(student_feats, teacher_feats, student_weight, teacher_weight, patch_masks):
    devices = lax.axis_size(AXES)
    protos = lax.axis_size("proto")
    images, patches, feat = student_feats.shape
    assert images == 1 and protos % 2 == 0
    columns = student_weight.shape[1]
    own = patches // 2 // protos
    each = own // 2
    half = each * devices
    rows = 2 * half * 5 // 16
    tiles = -(-rows // LANES)
    wide = feat + LANES * -(-4 * tiles // each)
    big = rows * columns
    exchange = functools.partial(lax.all_to_all, axis_name=AXES, split_axis=0, concat_axis=0)
    swap = functools.partial(lax.ppermute, axis_name="proto", perm=[(p, p ^ 1) for p in range(protos)])
    vector = pltpu.VMEM((tiles, LANES), F32)
    matrix = pltpu.VMEM((rows, columns), F32)
    column = pltpu.VMEM((rows, LANES), F32)
    line = pltpu.VMEM((1, columns), F32)
    block = pltpu.VMEM((half, feat), F32)
    payload = pltpu.VMEM((devices, each, wide), BF16)

    stu_w, tea_w = near(student_weight), near(teacher_weight)
    sent, unit, norm = call(
        select_kernel,
        (
            pltpu.VMEM((devices // 2, own, 2 * feat), BF16),
            pltpu.VMEM((own, feat), F32),
            pltpu.VMEM((own, LANES), F32),
        ),
        patch_masks,
        student_feats,
        teacher_feats,
    )
    mine = exchange(sent.reshape(devices, each, 2 * feat)).reshape(half, 2 * feat)
    other = near(swap(mine))
    mine = near(mine)
    stu_inv, tea_inv = call(
        norms_kernel,
        (line, line),
        stu_w,
        tea_w,
        flops=4 * feat * columns,
        moved=4 * feat * columns,
    )
    kernel, sent = call(
        first_kernel,
        (matrix, pltpu.VMEM((devices, tiles, LANES), F32)),
        mine,
        other,
        tea_w,
        tea_inv,
        flops=2 * big * feat,
        moved=4 * big,
        exps=big,
    )
    got = near(exchange(sent))
    logits, part, x, hot, own_hot, weight, keep, give = call(
        functools.partial(student_kernel, protos=protos),
        (
            matrix,
            vector,
            pltpu.VMEM((rows, feat), BF16),
            pltpu.VMEM((rows, 2 * half), BF16),
            pltpu.VMEM((own, rows), F32),
            column,
            block,
            block,
        ),
        mine,
        other,
        stu_w,
        stu_inv,
        flops=4 * big * feat,
        moved=4 * big,
        exps=big,
    )
    give = near(swap(give))
    (sent,) = call(sweep_kernel, (payload,), got, kernel, part, keep, give, flops=4 * big, moved=4 * big)
    swept = near(exchange(sent))
    scaled, total, cross, keep, give = call(
        last_sweep_kernel,
        (matrix, vector, vector, block, block),
        swept,
        kernel,
        logits,
        stu_w,
        stu_inv,
        hot,
        flops=2 * big * feat,
        moved=12 * big,
    )
    (sent,) = call(fill_kernel, (payload,), keep, near(swap(give)), total, cross)
    got = near(exchange(sent))
    pull, push, rise, log_part = call(
        functools.partial(prepare_kernel, scale=columns * devices * GRAD_SCALE),
        (matrix, matrix, pltpu.VMEM((own, feat), F32), column),
        swept,
        scaled,
        logits,
        stu_inv,
        weight,
        own_hot,
        flops=4 * big,
        moved=16 * big,
        exps=big,
    )
    step = min(512, columns)
    whole = lambda shape: pl.BlockSpec(shape, lambda i: (0,) * len(shape))
    part = lambda height: pl.BlockSpec((height, step), lambda i: (0, i))
    grad_weight, grad_rows, loss = pl.pallas_call(
        final_kernel,
        out_shape=(
            jax.ShapeDtypeStruct((feat, columns), F32),
            jax.ShapeDtypeStruct((own, feat), F32),
            jax.ShapeDtypeStruct((1, 1), F32),
        ),
        grid=(columns // step,),
        in_specs=[
            whole((devices, each, wide)),
            part(rows),
            part(rows),
            part(rows),
            part(1),
            part(feat),
            whole((rows, feat)),
            whole((rows, LANES)),
            whole((own, rows)),
            whole((own, feat)),
            whole((rows, LANES)),
            whole((own, feat)),
            whole((own, LANES)),
        ],
        out_specs=(part(feat), whole((own, feat)), whole((1, 1))),
        scratch_shapes=[pltpu.VMEM((rows, LANES), F32)],
        compiler_params=pltpu.CompilerParams(vmem_limit_bytes=24 * 1024 * 1024),
        cost_estimate=pl.CostEstimate(flops=2 * big * feat, bytes_accessed=6 * feat * columns, transcendentals=0),
    )(got, pull, push, logits, stu_inv, stu_w, x, weight, own_hot, rise, log_part, unit, norm)
    return loss.reshape(()), grad_weight, grad_rows


def solution(mesh):
    placed = (
        P("img", None, None),
        P("img", None, None),
        P(None, AXES),
        P(None, AXES),
        P("img", None),
    )
    return jax.shard_map(
        shards,
        mesh=mesh,
        in_specs=placed,
        out_specs=(P(), P(None, AXES), P(AXES, None)),
        check_vma=False,
    )
```

time: 112 us -> 96.9 us (0.87)
  Pallas kernels: 45.4 us -> 21.3 us
  local copies, waits for them, and re-layouts: 2.1 us -> 24.5 us
  waiting for transfers between devices: 24.2 us -> 3.47 us
  blocking collectives: 23.5 us -> 42.3 us
  starting transfers between devices: 15 us -> 3.82 us
    all_to_all x4 -> x1, waiting for transfers between devices: 24.2 us -> 1.74 us  [shards(): got = near(exchange(sent))]
    pallas_call x8, Pallas kernels: 36.9 us -> 14.4 us  [call(): pl.pallas_call(body, out_shape=outs, in_specs=[VMEM] * len(args), out_spe...]
    unnamed x8 -> x46, local copies, waits for them, and re-layouts: 2.1 us -> 24.5 us
    all_to_all x2 -> x3, blocking collectives: 23.5 us -> 42.3 us  [the longest x1 20.3 us: shards(): exchange(sent.reshape(devices, each, 2 * feat)).reshape(half, 2 * feat)]
    all_to_all x4 -> x1, starting transfers between devices: 15 us -> 3.3 us  [shards(): got = near(exchange(sent))]
    ppermute x0 -> x3, waiting for transfers between devices: none -> 1.73 us  [the longest x1 1.72 us: shards(): sent, = call(fill_kernel, (payload,), keep, near(swap(give)), total, cross)]
    pallas_call x1, Pallas kernels: 8.52 us -> 6.89 us  [shards(): pl.pallas_call(final_kernel, out_shape=(jax.ShapeDtypeStruct((feat, colum...]
  transfers between devices with their start and end apart: 4 -> 4, of which waited for: 4 -> 2; matrix products, arithmetic and copies ran while one was open for 0% -> 0% of each run, Pallas kernels for 20% -> 5%
where the time goes in v2:
time: 96.9 us; the launch traced here: 96.2 us
  blocking collectives  42.3 us (44%)
  local copies, waits for them, and re-layouts  24.5 us (25%)
  Pallas kernels  21.3 us (22%)
  starting transfers between devices  3.82 us (4%)
  waiting for transfers between devices  3.47 us (4%)
    unnamed x46, local copies, waits for them, and re-layouts  24.5 us
    all_to_all x1, blocking collectives, shards(): exchange(sent.reshape(devices, each, 2 * feat)).reshape(half, 2 * feat)  20.3 us
    pallas_call x8, Pallas kernels, call(): pl.pallas_call(body, out_shape=outs, in_specs=[VMEM] * len(args), out_spe...  14.4 us
    all_to_all x1, blocking collectives, shards(): swept = near(exchange(sent))  12.3 us
    all_to_all x1, blocking collectives, shards(): got = near(exchange(sent))  9.69 us
    pallas_call x1, Pallas kernels, shards(): pl.pallas_call(final_kernel, out_shape=(jax.ShapeDtypeStruct((feat, colum...  6.89 us
    all_to_all x1, starting transfers between devices, shards(): got = near(exchange(sent))  3.3 us
  transfers between devices with their start and end apart: 4, of which 2 were waited for; matrix products, arithmetic and copies ran while one was open for 0% of the time, Pallas kernels for 5%

profile of v2, /device:TPU:0, one launch (start us, length us, event | category | flops | bytes accessed | tf_op | source)
XLA Modules:
  0.0 96.2 jit_solution(792850056418801467)
XLA Ops:
  0.6 0.9 copy-done.16
  1.5 0.9 copy-done.17
  2.4 0.7 copy-done.22
  3.5 20.3 %all_to_all.20 = bf16[32,8,768]{2,1,0:T(8,128)(2,1)S(1)} all-to-all(bf16[32,8,768]{2,1,0:T(8,128)(2,1)S(1)} %bitcast.6), channel_id=1, replica_groups=mesh['img'=8,'proto'=4] {'img','proto'}, dimensions={0} | all-to-all | bytes 786432 | tf_op jit(solution)/shard_map/all_to_all | solution.py:393
  23.7 1.9 %copy-done = bf16[384,4096]{1,0:T(8,128)(2,1)S(1)} copy-done((bf16[384,4096]{1,0:T(8,128)(2,1)S(1)}, bf16[384,4096]{1,0:T(8,128)(2,1)}, u32[]{:S(2)}) %copy-start) | copy-done | bytes 3145752
  25.6 1.9 %copy-done.5 = bf16[384,4096]{1,0:T(8,128)(2,1)S(1)} copy-done((bf16[384,4096]{1,0:T(8,128)(2,1)S(1)}, bf16[384,4096]{1,0:T(8,128)(2,1)}, u32[]{:S(2)}) %copy-start.5) | copy-done | bytes 3145752
  27.5 0.9 shard_map.77
  28.5 4.8 %shard_map.79 = (f32[160,4096]{1,0:T(8,128)S(1)}, f32[2,128]{1,0:T(2,128)S(1)}, bf16[160,384]{1,0:T(8,128)(2,1)S(1)}, bf16[160,512]{1,0:T(8,128)(2,1)S(1)}, f32[...) custom-call(bf16[256,768]{1,0:T(8,128)(2,1)S(1)} %bitcast.4, ...), custom_call_target="tpu_custom_call" | custom-call | flops 1006632960 | bytes 2621440 | tf_op jit(solution)/shard_map/pallas_call | solution.py:25
  33.3 0.6 copy-done.14
  34.4 3.1 %shard_map.78 = (f32[160,4096]{1,0:T(8,128)S(1)}, f32[32,2,128]{2,1,0:T(2,128)S(1)}) custom-call(bf16[256,768]{1,0:T(8,128)(2,1)S(1)} %bitcast.5, bf16[256,768]{1,0:T(8,128)(2,1)S(1)} %collective-permute-done.other, bf16[384,4096]{1,0:T(8,128)(2,1)S(1)} %copy-done.6, f32[1,4096]{1,0:T(1,128)S(1)} %get-tuple-element.31.inv), custom_call_target="tpu_custom_call" | custom-call | flops 503316480 | bytes 2621440 | tf_op jit(solution)/shard_map/pallas_call | solution.py:25
  37.5 9.7 %all_to_all.21.got = f32[32,2,128]{2,1,0:T(2,128)S(1)} all-to-all(f32[32,2,128]{2,1,0:T(2,128)S(1)} %get-tuple-element.32), channel_id=1, replica_groups=mesh['img'=8,'proto'=4] {'img','proto'}, dimensions={0} | all-to-all | bytes 65536 | tf_op jit(solution)/shard_map/all_to_all | solution.py:415
  47.2 0.8 shard_map.80
  48.0 12.3 %all_to_all.22.got = bf16[32,8,512]{2,1,0:T(8,128)(2,1)S(1)} all-to-all(bf16[32,8,512]{2,1,0:T(8,128)(2,1)S(1)} %shard_map.80), channel_id=1, replica_groups=mesh['img'=8,'proto'=4] {'img','proto'}, dimensions={0} | all-to-all | bytes 524288 | tf_op jit(solution)/shard_map/all_to_all | solution.py:438
  60.3 3.4 %shard_map.81 = (f32[160,4096]{1,0:T(8,128)S(1)}, f32[2,128]{1,0:T(2,128)S(1)}, f32[2,128]{1,0:T(2,128)S(1)}, f32[256,384]{1,0:T(8,128)S(1)}, f32[256,384]{1,0:T(8,128)S(1)}) custom-call(bf16[32,8,512]{2,1,0:T(8,128)(2,1)S(1)} %all_to_all.22.got, f32[160,4096]{1,0:T(8,128)S(1)} %get-tuple-element.33.kernel, f32[160,4096]{1,0:T(8,128)S(1)} %get-tuple-element.38.logits, ...), custom_call_target="tpu_custom_call" | custom-call | flops 503316480 | bytes 7864320 | tf_op jit(solution)/shard_map/pallas_call | solution.py:25
  63.7 1.5 %copy-done.7 = f32[160,4096]{1,0:T(8,128)} copy-done((f32[160,4096]{1,0:T(8,128)}, f32[160,4096]{1,0:T(8,128)S(1)}, u32[]{:S(2)}) %copy-start.7) | copy-done | bytes 2621464
  65.2 1.7 %collective-permute-done.2.got = f32[256,384]{1,0:T(8,128)S(1)} collective-permute-done((f32[256,384]{1,0:T(8,128)S(1)}, f32[256,384]{1,0:T(8,128)S(1)}, u32[]{:S(2)}, u32[]{:S(2)}) %collective-permute-start.2) | collective-permute-done | bytes 393248 | tf_op jit(solution)/shard_map/ppermute | solution.py:451
  67.0 0.7 copy-done.13
  67.7 3.3 %all-to-all-start.3 = ((bf16[32,8,512]{2,1,0:T(8,128)(2,1)}), bf16[32,8,512]{2,1,0:T(8,128)(2,1)}, u32[]{:S(2)}, u32[]{:S(2)}) async-start(bf16[32,8,512]{2,1,0:T(8,128)(2,1)} %copy-done.13), calls=%async_computation.3 | async-start | bytes 524288 | tf_op jit(solution)/shard_map/all_to_all | solution.py:452
  71.0 1.7 %copy-done.3 = f32[160,4096]{1,0:T(8,128)S(1)} copy-done((f32[160,4096]{1,0:T(8,128)S(1)}, f32[160,4096]{1,0:T(8,128)}, u32[]{:S(2)}) %copy-start.3) | copy-done | bytes 2621464
  72.7 1.7 %copy-done.8 = f32[160,4096]{1,0:T(8,128)S(1)} copy-done((f32[160,4096]{1,0:T(8,128)S(1)}, f32[160,4096]{1,0:T(8,128)}, u32[]{:S(2)}) %copy-start.8) | copy-done | bytes 2621464
  74.5 1.1 %shard_map.83 = (f32[160,4096]{1,0:T(8,128)S(1)}, f32[160,4096]{1,0:T(8,128)S(1)}, f32[16,384]{1,0:T(8,128)S(1)}, f32[160,128]{1,0:T(8,128)S(1)}) custom-call(bf16[32,8,512]{2,1,0:T(8,128)(2,1)S(1)} %all_to_all.22.got, f32[160,4096]{1,0:T(8,128)S(1)} %copy-done.8, f32[160,4096]{1,0:T(8,128)S(1)} %copy-done.3, f32[1,4096]{1,0:T(1,128)S(1)} %get-tuple-element.34.inv, ...), custom_call_target="tpu_custom_call" | custom-call | flops 2621440 | bytes 10485760 | tf_op jit(solution)/shard_map/pallas_call | solution.py:25
  75.5 1.5 %copy-done.9 = f32[160,4096]{1,0:T(8,128)} copy-done((f32[160,4096]{1,0:T(8,128)}, f32[160,4096]{1,0:T(8,128)S(1)}, u32[]{:S(2)}) %copy-start.9) | copy-done | bytes 2621464
  77.0 1.5 %copy-done.11 = f32[160,4096]{1,0:T(8,128)} copy-done((f32[160,4096]{1,0:T(8,128)}, f32[160,4096]{1,0:T(8,128)S(1)}, u32[]{:S(2)}) %copy-start.11) | copy-done | bytes 2621464
  78.6 0.6 copy-done.18
  79.8 1.7 %all-to-all-done.3.got = bf16[32,8,512]{2,1,0:T(8,128)(2,1)} async-done(((bf16[32,8,512]{2,1,0:T(8,128)(2,1)}), bf16[32,8,512]{2,1,0:T(8,128)(2,1)}, u32[]{:S(2)}, u32[]{:S(2)}) %all-to-all-start.3) | async-done | bytes 262176 | tf_op jit(solution)/shard_map/all_to_all | solution.py:452
  81.6 1.7 %copy-done.4 = f32[160,4096]{1,0:T(8,128)S(1)} copy-done((f32[160,4096]{1,0:T(8,128)S(1)}, f32[160,4096]{1,0:T(8,128)}, u32[]{:S(2)}) %copy-start.4) | copy-done | bytes 2621464
  83.3 1.7 %copy-done.10 = f32[160,4096]{1,0:T(8,128)S(1)} copy-done((f32[160,4096]{1,0:T(8,128)S(1)}, f32[160,4096]{1,0:T(8,128)}, u32[]{:S(2)}) %copy-start.10) | copy-done | bytes 2621464
  85.0 1.7 %copy-done.12 = f32[160,4096]{1,0:T(8,128)S(1)} copy-done((f32[160,4096]{1,0:T(8,128)S(1)}, f32[160,4096]{1,0:T(8,128)}, u32[]{:S(2)}) %copy-start.12) | copy-done | bytes 2621464
  86.8 0.9 copy-done.15
  87.7 0.9 copy-done.19
  88.6 0.7 copy-done.21
  89.3 6.9 %shard_map.84 = (f32[384,4096]{1,0:T(8,128)}, f32[16,384]{1,0:T(8,128)}, f32[1,1]{1,0:T(1,128)}) custom-call(bf16[32,8,512]{2,1,0:T(8,128)(2,1)} %all-to-all-done.3.got, f32[160,4096]{1,0:T(8,128)S(1)} %copy-done.10, f32[160,4096]{1,0:T(8,128)S(1)} %copy-done.12, f32[160,4096]{1,0:T(8,128)S(1)} %copy-done.4, f32[1,4096]{1,0:T(1,128)S(1)} %get-tuple-element.34.inv, ...), custom_call_target="tpu_custom_call" | custom-call | flops 503316480 | bytes 9437184 | tf_op jit(solution)/shard_map/pallas_call | solution.py:469
  (34 shorter events, 1.6 us)
Async XLA Ops:
  0.6 0.9 copy-start.16
  1.5 0.9 copy-start.17
  2.4 0.7 copy-start.22
  23.7 4.7 %collective-permute-start = (bf16[256,768]{1,0:T(8,128)(2,1)S(1)}, bf16[256,768]{1,0:T(8,128)(2,1)S(1)}, u32[]{:S(2)}, u32[]{:S(2)}) collective-permute-start(bf16[256,768]{1,0:T(8,128)(2,1)S(1)} %bitcast.3), channel_id=1, source_target_pairs={{0,1},{1,0},{2,3},{3,2},{4,5},{5,4},{6,7},{7,6},{8,9},{9,8},{10,11... | collective-permute-start | bytes 1179656 | tf_op jit(solution)/shard_map/ppermute | solution.py:394
  23.7 1.9 %copy-start = (bf16[384,4096]{1,0:T(8,128)(2,1)S(1)}, bf16[384,4096]{1,0:T(8,128)(2,1)}, u32[]{:S(2)}) copy-start(bf16[384,4096]{1,0:T(8,128)(2,1)} %stu_w.7) | copy-start | bytes 9437188
  25.6 1.9 %copy-start.5 = (bf16[384,4096]{1,0:T(8,128)(2,1)S(1)}, bf16[384,4096]{1,0:T(8,128)(2,1)}, u32[]{:S(2)}) copy-start(bf16[384,4096]{1,0:T(8,128)(2,1)} %tea_w.3) | copy-start | bytes 9437188
  28.4 6.0 %copy-start.6 = (bf16[384,4096]{1,0:T(8,128)(2,1)S(1)}, bf16[384,4096]{1,0:T(8,128)(2,1)}, u32[]{:S(2)}) copy-start(bf16[384,4096]{1,0:T(8,128)(2,1)} %tea_w.3) | copy-start | bytes 9437188
  33.3 0.6 copy-start.14
  33.9 26.4 %copy-start.2 = (f32[160,4096]{1,0:T(8,128)}, f32[160,4096]{1,0:T(8,128)S(1)}, u32[]{:S(2)}) copy-start(f32[160,4096]{1,0:T(8,128)S(1)} %get-tuple-element.38.logits) | copy-start | bytes 7864324
  33.9 13.3 %collective-permute-start.1 = (f32[256,384]{1,0:T(8,128)S(1)}, f32[256,384]{1,0:T(8,128)S(1)}, u32[]{:S(2)}, u32[]{:S(2)}) collective-permute-start(f32[256,384]{1,0:T(8,128)S(1)} %get-tuple-element.37), channel_id=1, source_target_pairs={{0,1},{1,0},{2,3},{3,2},{4,5},{5,4},{6,7},{7,6},{8,9},{9,8},{10,11... | collective-permute-start | bytes 1179656 | tf_op jit(solution)/shard_map/ppermute | solution.py:436
  37.5 22.8 %copy-start.1 = (bf16[384,4096]{1,0:T(8,128)(2,1)S(1)}, bf16[384,4096]{1,0:T(8,128)(2,1)}, u32[]{:S(2)}) copy-start(bf16[384,4096]{1,0:T(8,128)(2,1)} %stu_w.7) | copy-start | bytes 9437188
  63.7 1.5 %copy-start.7 = (f32[160,4096]{1,0:T(8,128)}, f32[160,4096]{1,0:T(8,128)S(1)}, u32[]{:S(2)}) copy-start(f32[160,4096]{1,0:T(8,128)S(1)} %get-tuple-element.44.scaled) | copy-start | bytes 7864324
  65.2 1.7 %collective-permute-start.2 = (f32[256,384]{1,0:T(8,128)S(1)}, f32[256,384]{1,0:T(8,128)S(1)}, u32[]{:S(2)}, u32[]{:S(2)}) collective-permute-start(f32[256,384]{1,0:T(8,128)S(1)} %get-tuple-element.41), channel_id=1, source_target_pairs={{0,1},{1,0},{2,3},{3,2},{4,5},{5,4},{6,7},{7,6},{8,9},{9,8},{10,11... | collective-permute-start | bytes 1179656 | tf_op jit(solution)/shard_map/ppermute | solution.py:451
  67.0 0.7 copy-start.13
  67.7 13.9 %all-to-all-start.3 = ((bf16[32,8,512]{2,1,0:T(8,128)(2,1)}), bf16[32,8,512]{2,1,0:T(8,128)(2,1)}, u32[]{:S(2)}, u32[]{:S(2)}) async-start(bf16[32,8,512]{2,1,0:T(8,128)(2,1)} %copy-done.13), calls=%async_computation.3 | async-start | bytes 524288 | tf_op jit(solution)/shard_map/all_to_all | solution.py:452
  71.0 1.7 %copy-start.3 = (f32[160,4096]{1,0:T(8,128)S(1)}, f32[160,4096]{1,0:T(8,128)}, u32[]{:S(2)}) copy-start(f32[160,4096]{1,0:T(8,128)} %copy-done.2) | copy-start | bytes 7864324
  72.7 1.7 %copy-start.8 = (f32[160,4096]{1,0:T(8,128)S(1)}, f32[160,4096]{1,0:T(8,128)}, u32[]{:S(2)}) copy-start(f32[160,4096]{1,0:T(8,128)} %copy-done.7) | copy-start | bytes 7864324
  75.5 1.5 %copy-start.9 = (f32[160,4096]{1,0:T(8,128)}, f32[160,4096]{1,0:T(8,128)S(1)}, u32[]{:S(2)}) copy-start(f32[160,4096]{1,0:T(8,128)S(1)} %get-tuple-element.47.pull) | copy-start | bytes 7864324
  77.0 1.5 %copy-start.11 = (f32[160,4096]{1,0:T(8,128)}, f32[160,4096]{1,0:T(8,128)S(1)}, u32[]{:S(2)}) copy-start(f32[160,4096]{1,0:T(8,128)S(1)} %get-tuple-element.48.push) | copy-start | bytes 7864324
  78.6 0.6 copy-start.18
  79.2 0.6 copy-start.20
  81.6 1.7 %copy-start.4 = (f32[160,4096]{1,0:T(8,128)S(1)}, f32[160,4096]{1,0:T(8,128)}, u32[]{:S(2)}) copy-start(f32[160,4096]{1,0:T(8,128)} %copy-done.2) | copy-start | bytes 7864324
  83.3 1.7 %copy-start.10 = (f32[160,4096]{1,0:T(8,128)S(1)}, f32[160,4096]{1,0:T(8,128)}, u32[]{:S(2)}) copy-start(f32[160,4096]{1,0:T(8,128)} %copy-done.9) | copy-start | bytes 7864324
  85.0 1.7 %copy-start.12 = (f32[160,4096]{1,0:T(8,128)S(1)}, f32[160,4096]{1,0:T(8,128)}, u32[]{:S(2)}) copy-start(f32[160,4096]{1,0:T(8,128)} %copy-done.11) | copy-start | bytes 7864324
  86.8 0.9 copy-start.15
  87.7 0.9 copy-start.19
  88.6 0.7 copy-start.21

commit v3 on v2

--- a/solution.py
+++ b/solution.py
@@ -19,14 +19,16 @@
 AXES = ("img", "proto")
 
 VMEM = pl.BlockSpec(memory_space=pltpu.VMEM)
-
-
-def call(body, outs, *args, flops=0, moved=0, exps=0, limit=24):
+HBM = pl.BlockSpec(memory_space=pltpu.HBM)
+
+
+def call(body, outs, *args, flops=0, moved=0, exps=0, limit=24, specs=None, out_specs=None, scratch=()):
     return pl.pallas_call(
         body,
         out_shape=outs,
-        in_specs=[VMEM] * len(args),
-        out_specs=tuple(VMEM for _ in outs),
+        in_specs=specs or [VMEM] * len(args),
+        out_specs=out_specs or tuple(VMEM for _ in outs),
+        scratch_shapes=scratch,
         compiler_params=pltpu.CompilerParams(vmem_limit_bytes=limit * 1024 * 1024),
         cost_estimate=pl.CostEstimate(flops=flops, bytes_accessed=moved, transcendentals=exps),
     )(*args)
@@ -34,6 +36,10 @@
 
 def near(x):
     return pltpu.with_memory_space_constraint(x, pltpu.VMEM)
+
+
+def far(x):
+    return pltpu.with_memory_space_constraint(x, pltpu.HBM)
 
 
 def dot(a, b, dims, precision=None):
@@ -83,7 +89,13 @@
     return lax.rem(lax.axis_index("proto"), 2)
 
 
-def select_kernel(mask_ref, stu_ref, tea_ref, sent_out, unit_out, norm_out):
+def select_kernel(mask_hbm, stu_hbm, tea_hbm, sent_out, unit_out, norm_out, mask_ref, stu_ref, tea_ref, sems):
+    pairs = ((mask_hbm, mask_ref), (tea_hbm, tea_ref), (stu_hbm, stu_ref))
+    copies = [pltpu.make_async_copy(*pair, sems.at[i]) for i, pair in enumerate(pairs)]
+    for copy in copies:
+        copy.start()
+    for copy in copies:
+        copy.wait()
     own, feat = unit_out.shape
     patches = mask_ref.shape[1]
     slot = iota((own, patches), 0) + lax.axis_index("proto") * own
@@ -103,17 +115,22 @@
             norm_out[...] = jnp.broadcast_to(norm, norm_out.shape)
 
 
-def norms_kernel(stu_w, tea_w, stu_out, tea_out):
+def norms_kernel(stu_hbm, tea_hbm, stu_w, tea_w, stu_out, tea_out, sems):
     step, count = chunks(stu_w.shape[1])
-    for ref, out in ((tea_w, tea_out), (stu_w, stu_out)):
-
-        def body(i, _, ref=ref, out=out):
-            at = pl.ds(pl.multiple_of(i * step, step), step)
+    parts = [slice(i * step, (i + 1) * step) for i in range(count)]
+    sets = ((tea_hbm, tea_w, tea_out), (stu_hbm, stu_w, stu_out))
+    copies = [
+        [pltpu.make_async_copy(source.at[:, at], ref.at[:, at], sems.at[k, i]) for i, at in enumerate(parts)]
+        for k, (source, ref, _) in enumerate(sets)
+    ]
+    for row in copies:
+        for copy in row:
+            copy.start()
+    for row, (_, ref, out) in zip(copies, sets):
+        for copy, at in zip(row, parts):
+            copy.wait()
             w = ref[:, at].astype(F32)
             out[:, at] = 1.0 / jnp.sqrt(jnp.sum(w * w, axis=0, keepdims=True) + NORM_EPS)
-            return 0
-
-        lax.fori_loop(0, count, body, 0)
 
 
 def packing(mine, other, at, feat, rows, emit):
@@ -256,9 +273,8 @@
     return jnp.sum(parts, axis=0).reshape(2 * each, feat)
 
 
-def sweep_kernel(got, kernel, part, keep, give, sent_out):
+def sweep_kernel(got, kernel, total_out):
     rows, columns = kernel.shape
-    width = part.shape[0] * LANES
     scale = to_column(1.0 / jnp.sum(got[...], axis=0), rows)
     step, count = chunks(columns)
     wide = spread(scale, step)
@@ -270,11 +286,11 @@
         return acc + fold(k * c)
 
     acc = lax.fori_loop(0, count, body, jnp.zeros((rows, LANES), F32))
-    fill(sent_out, keep, give, [to_tiles(acc, width), part[...]])
+    total_out[...] = to_tiles(acc, total_out.shape[0] * LANES)
 
 
 def last_sweep_kernel(
-    got, kernel, logits, stu_w, inv, hot, scaled_out, total_out, cross_out, keep_out, give_out
+    got, kernel, x, stu_w, inv, hot, scaled_out, total_out, cross_out, keep_out, give_out
 ):
     rows, columns = kernel.shape
     feat = stu_w.shape[0]
@@ -290,16 +306,12 @@
         kc = k * (1.0 / jnp.sum(k * wide, axis=0, keepdims=True))
         scaled_out[:, at] = kc
         kn = (kc * inv[:, at]).astype(BF16)
-        return (
-            accs[0] + fold(kc),
-            accs[1] + fold(kc * logits[:, at]),
-            accs[2] + dot(kn, stu_w[:, at], ((1,), (1,))),
-        )
-
-    zero = jnp.zeros((rows, LANES), F32)
-    total, cross, push = lax.fori_loop(0, count, body, (zero, zero, jnp.zeros((rows, feat), F32)))
+        return accs[0] + fold(kc), accs[1] + dot(kn, stu_w[:, at], ((1,), (1,)))
+
+    zeros = jnp.zeros((rows, LANES), F32), jnp.zeros((rows, feat), F32)
+    total, push = lax.fori_loop(0, count, body, zeros)
     total_out[...] = to_tiles(total, width)
-    cross_out[...] = to_tiles(cross, width)
+    cross_out[...] = to_tiles(fold(push * x[...].astype(F32)) * (1.0 / STUDENT_TEMP), width)
     halves(hot, push.astype(BF16), keep_out, give_out)
 
 
@@ -332,28 +344,32 @@
 
 
 def final_kernel(
-    got, pull, push, logits, inv, stu_w, x, weight, own, rise, log_part, unit, norm, out, rows_out, loss_out, scale_ref
+    got, pull, push, logits, inv, stu_w, x, weight, own, rise, log_part, unit, norm, out_hbm, rows_out, loss_out, out, sems
 ):
-    rows = pull.shape[0]
+    rows, columns = pull.shape
     feat = x.shape[1]
     width = -(-rows // LANES) * LANES
-
-    @pl.when(pl.program_id(0) == 0)
-    def _():
-        total, cross = (to_column(v, rows) for v in vectors_of(got, feat, width, 2))
-        scale = 1.0 / total
-        scale_ref[...] = scale
-        share = weight[...]
-        loss = jnp.sum(share * (log_part[...] - cross * scale), axis=0, keepdims=True)
-        loss_out[...] = loss[:, :1]
-        held = dot(own[...], share * (rows / STUDENT_TEMP) * scale, ((1,), (0,)), lax.Precision.HIGHEST)
-        full = rise[...] - slots_of(got, feat) * held[:, :1]
-        u = unit[...]
-        rows_out[...] = (full - u * jnp.sum(u * full, axis=1, keepdims=True)) / norm[:, :1]
-
-    g = pull[...] - spread(scale_ref[...], pull.shape[1]) * push[...]
-    along = jnp.sum(g * logits[...], axis=0, keepdims=True) * (inv[...] * STUDENT_TEMP)
-    out[...] = dot(x[...], g.astype(BF16), ((0,), (0,))) - stu_w[...].astype(F32) * along
+    total, cross = (to_column(v, rows) for v in vectors_of(got, feat, width, 2))
+    scale = 1.0 / total
+    step, count = chunks(columns)
+    wide = spread(scale, step)
+    copies = []
+    for i in range(count):
+        at = slice(i * step, (i + 1) * step)
+        g = pull[:, at] - wide * push[:, at]
+        along = jnp.sum(g * logits[:, at], axis=0, keepdims=True) * (inv[:, at] * STUDENT_TEMP)
+        out[:, at] = dot(x[...], g.astype(BF16), ((0,), (0,))) - stu_w[:, at].astype(F32) * along
+        copies.append(pltpu.make_async_copy(out.at[:, at], out_hbm.at[:, at], sems.at[i]))
+        copies[-1].start()
+    share = weight[...]
+    loss = jnp.sum(share * (log_part[...] - cross * scale), axis=0, keepdims=True)
+    loss_out[...] = loss[:, :1]
+    held = dot(own[...], share * (rows / STUDENT_TEMP) * scale, ((1,), (0,)), lax.Precision.HIGHEST)
+    full = rise[...] - slots_of(got, feat) * held[:, :1]
+    u = unit[...]
+    rows_out[...] = (full - u * jnp.sum(u * full, axis=1, keepdims=True)) / norm[:, :1]
+    for copy in copies:
+        copy.wait()
 
 
 def shards(student_feats, teacher_feats, student_weight, teacher_weight, patch_masks):
@@ -378,7 +394,6 @@
     block = pltpu.VMEM((half, feat), F32)
     payload = pltpu.VMEM((devices, each, wide), BF16)
 
-    stu_w, tea_w = near(student_weight), near(teacher_weight)
     sent, unit, norm = call(
         select_kernel,
         (
@@ -386,20 +401,31 @@
             pltpu.VMEM((own, feat), F32),
             pltpu.VMEM((own, LANES), F32),
         ),
-        patch_masks,
-        student_feats,
-        teacher_feats,
+        far(patch_masks),
+        far(student_feats),
+        far(teacher_feats),
+        specs=[HBM] * 3,
+        scratch=[
+            pltpu.VMEM(patch_masks.shape, patch_masks.dtype),
+            pltpu.VMEM(student_feats.shape, BF16),
+            pltpu.VMEM(teacher_feats.shape, BF16),
+            pltpu.SemaphoreType.DMA((3,)),
+        ],
     )
     mine = exchange(sent.reshape(devices, each, 2 * feat)).reshape(half, 2 * feat)
+    mine, student_weight, teacher_weight = lax.optimization_barrier((mine, student_weight, teacher_weight))
     other = near(swap(mine))
     mine = near(mine)
-    stu_inv, tea_inv = call(
+    held = pltpu.VMEM(student_weight.shape, BF16)
+    stu_w, tea_w, stu_inv, tea_inv = call(
         norms_kernel,
-        (line, line),
-        stu_w,
-        tea_w,
+        (held, held, line, line),
+        far(student_weight),
+        far(teacher_weight),
         flops=4 * feat * columns,
-        moved=4 * feat * columns,
+        moved=8 * feat * columns,
+        specs=[HBM] * 2,
+        scratch=[pltpu.SemaphoreType.DMA((2, chunks(columns)[1]))],
     )
     kernel, sent = call(
         first_kernel,
@@ -413,6 +439,7 @@
         exps=big,
     )
     got = near(exchange(sent))
+    mine, other, got = lax.optimization_barrier((mine, other, got))
     logits, part, x, hot, own_hot, weight, keep, give = call(
         functools.partial(student_kernel, protos=protos),
         (
@@ -434,22 +461,22 @@
         exps=big,
     )
     give = near(swap(give))
-    (sent,) = call(sweep_kernel, (payload,), got, kernel, part, keep, give, flops=4 * big, moved=4 * big)
+    (total,) = call(sweep_kernel, (vector,), got, kernel, flops=4 * big, moved=4 * big)
+    (sent,) = call(fill_kernel, (payload,), keep, give, total, part)
     swept = near(exchange(sent))
     scaled, total, cross, keep, give = call(
         last_sweep_kernel,
         (matrix, vector, vector, block, block),
         swept,
         kernel,
-        logits,
+        x,
         stu_w,
         stu_inv,
         hot,
         flops=2 * big * feat,
         moved=12 * big,
     )
-    (sent,) = call(fill_kernel, (payload,), keep, near(swap(give)), total, cross)
-    got = near(exchange(sent))
+    give = near(swap(give))
     pull, push, rise, log_part = call(
         functools.partial(prepare_kernel, scale=columns * devices * GRAD_SCALE),
         (matrix, matrix, pltpu.VMEM((own, feat), F32), column),
@@ -463,37 +490,34 @@
         moved=16 * big,
         exps=big,
     )
-    step = min(512, columns)
-    whole = lambda shape: pl.BlockSpec(shape, lambda i: (0,) * len(shape))
-    part = lambda height: pl.BlockSpec((height, step), lambda i: (0, i))
-    grad_weight, grad_rows, loss = pl.pallas_call(
+    keep, pull, push, rise, log_part = lax.optimization_barrier((keep, pull, push, rise, log_part))
+    (sent,) = call(fill_kernel, (payload,), keep, give, total, cross)
+    got = near(exchange(sent))
+    grad_weight, grad_rows, loss = call(
         final_kernel,
-        out_shape=(
+        (
             jax.ShapeDtypeStruct((feat, columns), F32),
             jax.ShapeDtypeStruct((own, feat), F32),
             jax.ShapeDtypeStruct((1, 1), F32),
         ),
-        grid=(columns // step,),
-        in_specs=[
-            whole((devices, each, wide)),
-            part(rows),
-            part(rows),
-            part(rows),
-            part(1),
-            part(feat),
-            whole((rows, feat)),
-            whole((rows, LANES)),
-            whole((own, rows)),
-            whole((own, feat)),
-            whole((rows, LANES)),
-            whole((own, feat)),
-            whole((own, LANES)),
-        ],
-        out_specs=(part(feat), whole((own, feat)), whole((1, 1))),
-        scratch_shapes=[pltpu.VMEM((rows, LANES), F32)],
-        compiler_params=pltpu.CompilerParams(vmem_limit_bytes=24 * 1024 * 1024),
-        cost_estimate=pl.CostEstimate(flops=2 * big * feat, bytes_accessed=6 * feat * columns, transcendentals=0),
-    )(got, pull, push, logits, stu_inv, stu_w, x, weight, own_hot, rise, log_part, unit, norm)
+        got,
+        pull,
+        push,
+        logits,
+        stu_inv,
+        stu_w,
+        x,
+        weight,
+        own_hot,
+        rise,
+        log_part,
+        unit,
+        norm,
+        flops=2 * big * feat,
+        moved=8 * feat * columns,
+        out_specs=(HBM, VMEM, VMEM),
+        scratch=[pltpu.VMEM((feat, columns), F32), pltpu.SemaphoreType.DMA((chunks(columns)[1],))],
+    )
     return loss.reshape(()), grad_weight, grad_rows
 
 

time: 96.9 us -> 79.1 us (0.82)
  local copies, waits for them, and re-layouts: 24.5 us -> 0 us
  blocking collectives: 42.3 us -> 55.1 us
  starting transfers between devices: 3.82 us -> 0.25 us
  waiting for transfers between devices: 3.47 us -> 1.49 us
    unnamed x46 -> x0, local copies, waits for them, and re-layouts: 24.5 us -> none
    all_to_all x1 -> x2, blocking collectives: 9.69 us -> 22.5 us  [shards(): got = near(exchange(sent))]
    all_to_all x1 -> x0, starting transfers between devices: 3.3 us -> none  [shards(): got = near(exchange(sent))]
    all_to_all x1 -> x0, waiting for transfers between devices: 1.74 us -> none  [shards(): got = near(exchange(sent))]
    ppermute x1 -> x0, waiting for transfers between devices: 1.72 us -> none  [shards(): sent, = call(fill_kernel, (payload,), keep, near(swap(give)), total, cross)]
    ppermute x1 -> x2, waiting for transfers between devices: 0.01 us -> 1.49 us  [shards(): give = near(swap(give))]
    pallas_call x9 -> x10, Pallas kernels: 21.3 us -> 21.4 us  [call(): pl.pallas_call(body, out_shape=outs, in_specs=specs or [VMEM] * len(args)...]
  transfers between devices with their start and end apart: 4 -> 3, of which waited for: 2 -> 2; matrix products, arithmetic and copies ran while one was open for 0% -> 0% of each run, Pallas kernels for 5% -> 6%
where the time goes in v3:
time: 79.1 us; the launch traced here: 78.9 us
  blocking collectives  55.1 us (70%)
  Pallas kernels  21.4 us (27%)
  waiting for transfers between devices  1.49 us (2%)
    all_to_all x2, blocking collectives, shards(): got = near(exchange(sent))  22.5 us
    pallas_call x10, Pallas kernels, call(): pl.pallas_call(body, out_shape=outs, in_specs=specs or [VMEM] * len(args)...  21.4 us
    all_to_all x1, blocking collectives, shards(): exchange(sent.reshape(devices, each, 2 * feat)).reshape(half, 2 * feat)  20.3 us
    all_to_all x1, blocking collectives, shards(): swept = near(exchange(sent))  12.3 us
  transfers between devices with their start and end apart: 3, of which 2 were waited for; matrix products, arithmetic and copies ran while one was open for 0% of the time, Pallas kernels for 6%

profile of v3, /device:TPU:0, one launch (start us, length us, event | category | flops | bytes accessed | tf_op | source)
XLA Modules:
  0.0 78.9 jit_solution(17500878842745129710)
XLA Ops:
  0.6 1.4 %shard_map.76 = (bf16[16,16,768]{2,1,0:T(8,128)(2,1)S(1)}, f32[16,384]{1,0:T(8,128)S(1)}, f32[16,128]{1,0:T(8,128)S(1)}) custom-call(s32[1,128]{1,0:T(1,128)} %mask_hbm.1, bf16[1,128,384]{2,1,0:T(8,128)(2,1)} %stu_hbm.1, bf16[1,128,384]{2,1,0:T(8,128)(2,1)} %tea_hbm.1), custom_call_target="tpu_custom_call" | custom-call | tf_op jit(solution)/shard_map/pallas_call | solution.py:26
  2.0 20.3 %all_to_all.20 = bf16[32,8,768]{2,1,0:T(8,128)(2,1)S(1)} all-to-all(bf16[32,8,768]{2,1,0:T(8,128)(2,1)S(1)} %bitcast.6), channel_id=1, replica_groups=mesh['img'=8,'proto'=4] {'img','proto'}, dimensions={0} | all-to-all | bytes 786432 | tf_op jit(solution)/shard_map/all_to_all | solution.py:415
  22.3 0.0 collective-permute-start
  22.3 3.0 %shard_map.77 = (bf16[384,4096]{1,0:T(8,128)(2,1)S(1)}, bf16[384,4096]{1,0:T(8,128)(2,1)S(1)}, f32[1,4096]{1,0:T(1,128)S(1)}, f32[1,4096]{1,0:T(1,128)S(1)}) custom-call(bf16[384,4096]{1,0:T(8,128)(2,1)} %stu_hbm.2, bf16[384,4096]{1,0:T(8,128)(2,1)} %tea_hbm.2), custom_call_target="tpu_custom_call" | custom-call | flops 6291456 | bytes 12582912 | tf_op jit(solution)/shard_map/pallas_call | solution.py:26
  25.3 0.0 collective-permute-done.other
  25.3 3.1 %shard_map.78 = (f32[160,4096]{1,0:T(8,128)S(1)}, f32[32,2,128]{2,1,0:T(2,128)S(1)}) custom-call(bf16[256,768]{1,0:T(8,128)(2,1)S(1)} %bitcast.4, bf16[256,768]{1,0:T(8,128)(2,1)S(1)} %collective-permute-done.other, bf16[384,4096]{1,0:T(8,128)(2,1)S(1)} %get-tuple-element.47.tea_w, f32[1,4096]{1,0:T(1,128)S(1)} %get-tuple-element.48.inv), custom_call_target="tpu_custom_call" | custom-call | flops 503316480 | bytes 2621440 | tf_op jit(solution)/shard_map/pallas_call | solution.py:26
  28.4 9.8 %all_to_all.21.got = f32[32,2,128]{2,1,0:T(2,128)S(1)} all-to-all(f32[32,2,128]{2,1,0:T(2,128)S(1)} %get-tuple-element.49), channel_id=1, replica_groups=mesh['img'=8,'proto'=4] {'img','proto'}, dimensions={0} | all-to-all | bytes 65536 | tf_op jit(solution)/shard_map/all_to_all | solution.py:441
  38.2 4.8 %shard_map.79 = (f32[160,4096]{1,0:T(8,128)S(1)}, f32[2,128]{1,0:T(2,128)S(1)}, bf16[160,384]{1,0:T(8,128)(2,1)S(1)}, bf16[160,512]{1,0:T(8,128)(2,1)S(1)}, f32[...) custom-call(bf16[256,768]{1,0:T(8,128)(2,1)S(1)} %bitcast.5, ...), custom_call_target="tpu_custom_call" | custom-call | flops 1006632960 | bytes 2621440 | tf_op jit(solution)/shard_map/pallas_call | solution.py:26
  43.0 0.2 collective-permute-start.1
  43.2 0.7 shard_map.80.total
  43.9 0.9 %collective-permute-done.1.got = f32[256,384]{1,0:T(8,128)S(1)} collective-permute-done((f32[256,384]{1,0:T(8,128)S(1)}, f32[256,384]{1,0:T(8,128)S(1)}, u32[]{:S(2)}, u32[]{:S(2)}) %collective-permute-start.1) | collective-permute-done | bytes 393248 | tf_op jit(solution)/shard_map/ppermute | solution.py:463
  44.8 0.1 shard_map.81
  44.9 12.3 %all_to_all.22.got = bf16[32,8,512]{2,1,0:T(8,128)(2,1)S(1)} all-to-all(bf16[32,8,512]{2,1,0:T(8,128)(2,1)S(1)} %shard_map.81), channel_id=1, replica_groups=mesh['img'=8,'proto'=4] {'img','proto'}, dimensions={0} | all-to-all | bytes 524288 | tf_op jit(solution)/shard_map/all_to_all | solution.py:466
  57.2 3.2 %shard_map.82 = (f32[160,4096]{1,0:T(8,128)S(1)}, f32[2,128]{1,0:T(2,128)S(1)}, f32[2,128]{1,0:T(2,128)S(1)}, f32[256,384]{1,0:T(8,128)S(1)}, f32[256,384]{1,0:T(8,128)S(1)}) custom-call(bf16[32,8,512]{2,1,0:T(8,128)(2,1)S(1)} %all_to_all.22.got, f32[160,4096]{1,0:T(8,128)S(1)} %get-tuple-element.57.kernel, bf16[160,384]{1,0:T(8,128)(2,1)S(1)} %get-tuple-element.59.x, ...), custom_call_target="tpu_custom_call" | custom-call | flops 503316480 | bytes 7864320 | tf_op jit(solution)/shard_map/pallas_call | solution.py:26
  60.4 0.1 collective-permute-start.2
  60.5 1.1 %shard_map.83 = (f32[160,4096]{1,0:T(8,128)S(1)}, f32[160,4096]{1,0:T(8,128)S(1)}, f32[16,384]{1,0:T(8,128)S(1)}, f32[160,128]{1,0:T(8,128)S(1)}) custom-call(bf16[32,8,512]{2,1,0:T(8,128)(2,1)S(1)} %all_to_all.22.got, f32[160,4096]{1,0:T(8,128)S(1)} %get-tuple-element.62.scaled, f32[160,4096]{1,0:T(8,128)S(1)} %get-tuple-element.63.logits, ...), custom_call_target="tpu_custom_call" | custom-call | flops 2621440 | bytes 10485760 | tf_op jit(solution)/shard_map/pallas_call | solution.py:26
  61.5 0.6 collective-permute-done.2.got
  62.2 0.1 shard_map.84
  62.3 12.7 %all_to_all.23.got = bf16[32,8,512]{2,1,0:T(8,128)(2,1)S(1)} all-to-all(bf16[32,8,512]{2,1,0:T(8,128)(2,1)S(1)} %shard_map.84), channel_id=1, replica_groups=mesh['img'=8,'proto'=4] {'img','proto'}, dimensions={0} | all-to-all | bytes 524288 | tf_op jit(solution)/shard_map/all_to_all | solution.py:495
  75.0 3.9 %shard_map.85 = (f32[384,4096]{1,0:T(8,128)}, f32[16,384]{1,0:T(8,128)}, f32[1,1]{1,0:T(1,128)}) custom-call(bf16[32,8,512]{2,1,0:T(8,128)(2,1)S(1)} %all_to_all.23.got, f32[160,4096]{1,0:T(8,128)S(1)} %get-tuple-element.74.pull, f32[160,4096]{1,0:T(8,128)S(1)} %get-tuple-element.75.push, f32[160,4096]{1,0:T(8,128)S(1)} %get-tuple-element.63.logits, ...), custom_call_target="tpu_custom_call" | custom-call | flops 503316480 | bytes 12582912 | tf_op jit(solution)/shard_map/pallas_call | solution.py:26
Async XLA Ops:
  22.3 3.0 %collective-permute-start = (bf16[256,768]{1,0:T(8,128)(2,1)S(1)}, bf16[256,768]{1,0:T(8,128)(2,1)S(1)}, u32[]{:S(2)}, u32[]{:S(2)}) collective-permute-start(bf16[256,768]{1,0:T(8,128)(2,1)S(1)} %bitcast.3), channel_id=1, source_target_pairs={{0,1},{1,0},{2,3},{3,2},{4,5},{5,4},{6,7},{7,6},{8,9},{9,8},{10,11... | collective-permute-start | bytes 1179656 | tf_op jit(solution)/shard_map/ppermute | solution.py:417
  43.0 1.8 %collective-permute-start.1 = (f32[256,384]{1,0:T(8,128)S(1)}, f32[256,384]{1,0:T(8,128)S(1)}, u32[]{:S(2)}, u32[]{:S(2)}) collective-permute-start(f32[256,384]{1,0:T(8,128)S(1)} %get-tuple-element.55), channel_id=1, source_target_pairs={{0,1},{1,0},{2,3},{3,2},{4,5},{5,4},{6,7},{7,6},{8,9},{9,8},{10,11... | collective-permute-start | bytes 1179656 | tf_op jit(solution)/shard_map/ppermute | solution.py:463
  60.4 1.8 %collective-permute-start.2 = (f32[256,384]{1,0:T(8,128)S(1)}, f32[256,384]{1,0:T(8,128)S(1)}, u32[]{:S(2)}, u32[]{:S(2)}) collective-permute-start(f32[256,384]{1,0:T(8,128)S(1)} %get-tuple-element.71), channel_id=1, source_target_pairs={{0,1},{1,0},{2,3},{3,2},{4,5},{5,4},{6,7},{7,6},{8,9},{9,8},{10,11... | collective-permute-start | bytes 1179656 | tf_op jit(solution)/shard_map/ppermute | solution.py:479

commit v4 on v3

v4 whole, which is shorter than its diff:
```python
import functools

import jax
import jax.numpy as jnp
from jax import lax
from jax.experimental import pallas as pl
from jax.experimental.pallas import tpu as pltpu
from jax.sharding import PartitionSpec as P

ITERS = 3
TEACHER_TEMP = 0.07
STUDENT_TEMP = 0.1
NORM_EPS = 1e-06
GRAD_SCALE = 1.0 / 128.0
EMPTY = 2.0
LANES = 128
F32 = jnp.float32
BF16 = jnp.bfloat16
AXES = ("img", "proto")

VMEM = pl.BlockSpec(memory_space=pltpu.VMEM)
HBM = pl.BlockSpec(memory_space=pltpu.HBM)


def call(body, outs, *args, flops=0, moved=0, exps=0, limit=24, specs=None, out_specs=None, scratch=()):
    return pl.pallas_call(
        body,
        out_shape=outs,
        in_specs=specs or [VMEM] * len(args),
        out_specs=out_specs or tuple(VMEM for _ in outs),
        scratch_shapes=scratch,
        compiler_params=pltpu.CompilerParams(vmem_limit_bytes=limit * 1024 * 1024),
        cost_estimate=pl.CostEstimate(flops=flops, bytes_accessed=moved, transcendentals=exps),
    )(*args)


def near(x):
    return pltpu.with_memory_space_constraint(x, pltpu.VMEM)


def far(x):
    return pltpu.with_memory_space_constraint(x, pltpu.HBM)


def dot(a, b, dims, precision=None):
    return lax.dot_general(a, b, (dims, ((), ())), precision=precision, preferred_element_type=F32)


def iota(shape, dim):
    return lax.broadcasted_iota(jnp.int32, shape, dim)


def add_all(parts):
    return functools.reduce(jnp.add, parts)


def to_column(vector, rows):
    parts = [jnp.broadcast_to(vector[i : i + 1], (LANES, LANES)).T for i in range(vector.shape[0])]
    return jnp.concatenate(parts, axis=0)[:rows]


def to_tiles(part, width):
    rows = part.shape[0]
    if width > rows:
        part = jnp.concatenate([part, jnp.zeros((width - rows, LANES), F32)], axis=0)
    row = jnp.sum(part.T, axis=0, keepdims=True)
    return jnp.concatenate([row[:, i : i + LANES] for i in range(0, width, LANES)], axis=0)


def split(tiles):
    high = tiles.astype(BF16).astype(F32)
    return [high, tiles - high]


def fold(x):
    return add_all([x[:, i : i + LANES] for i in range(0, x.shape[1], LANES)])


def spread(col, width):
    return jnp.concatenate([col] * (width // LANES), axis=1)


def chunks(columns):
    step = min(512, columns)
    return [slice(at, at + step) for at in range(0, columns, step)]


def over_chunks(columns, body, start):
    for at in chunks(columns):
        start = body(at, start)
    return start


def start_load(source, target, sems):
    parts = chunks(target.shape[1])
    copies = [pltpu.make_async_copy(source.at[:, at], target.at[:, at], sems.at[i]) for i, at in enumerate(parts)]
    for copy in copies:
        copy.start()
    return copies


def inverse_norms(w):
    w = w.astype(F32)
    return 1.0 / jnp.sqrt(jnp.sum(w * w, axis=0, keepdims=True) + NORM_EPS)


def odd_half():
    return lax.rem(lax.axis_index("proto"), 2)


def select_kernel(mask_hbm, stu_hbm, tea_hbm, sent_out, unit_out, norm_out, mask_ref, stu_ref, tea_ref, sems):
    pairs = ((mask_hbm, mask_ref), (tea_hbm, tea_ref), (stu_hbm, stu_ref))
    copies = [pltpu.make_async_copy(*pair, sems.at[i]) for i, pair in enumerate(pairs)]
    for copy in copies:
        copy.start()
    copies[0].wait()
    own, feat = unit_out.shape
    patches = mask_ref.shape[1]
    slot = iota((own, patches), 0) + lax.axis_index("proto") * own
    mask = jnp.broadcast_to(mask_ref[...].astype(F32), (own, patches))
    upto = (iota((patches, patches), 0) <= iota((patches, patches), 1)).astype(BF16)
    rank = dot(mask.astype(BF16), upto, ((1,), (0,)))
    pick = jnp.where((rank == slot.astype(F32) + 1.0) & (mask > 0.5), 1.0, 0.0).astype(BF16)
    valid = slot[:, :1].astype(F32) < rank[:, patches - 1 :]
    for copy, source, at in ((copies[1], tea_ref, 0), (copies[2], stu_ref, feat)):
        copy.wait()
        rows = dot(pick, source[0], ((1,), (0,)))
        norm = jnp.sqrt(jnp.sum(rows * rows, axis=1, keepdims=True) + NORM_EPS)
        unit = (rows / norm).astype(BF16)
        sent = jnp.where(valid, unit.astype(F32), EMPTY).astype(BF16)
        sent_out[:, :, at : at + feat] = jnp.broadcast_to(sent[None], (sent_out.shape[0], own, feat))
        if source is stu_ref:
            unit_out[...] = unit.astype(F32)
            norm_out[...] = jnp.broadcast_to(norm, norm_out.shape)


def norms_kernel(tea_hbm, tea_w, inv_out, sems):
    copies = start_load(tea_hbm, tea_w, sems)
    for copy, at in zip(copies, chunks(tea_w.shape[1])):
        copy.wait()
        inv_out[:, at] = inverse_norms(tea_w[:, at])


def in_order(mine, other, h, at, feat):
    return jnp.where(odd_half() == h, mine[:, at : at + feat], other[:, at : at + feat])


def slot_flags(data):
    return jnp.where(data[:, :LANES].astype(F32) < 1.5, 1.0, 0.0).astype(BF16)


def packing(flags, hot_out):
    rows = hot_out.shape[0]
    half = flags[0].shape[0]
    step = min(256, half)
    before = jnp.zeros((1, 1), F32)
    upto = (iota((step, step), 0) <= iota((step, step), 1)).astype(BF16)
    same = (iota((step, step), 0) == iota((step, step), 1)).astype(BF16)
    row = iota((rows, step), 0).astype(F32) + 1.0
    for h in range(2):
        for c in range(0, half, step):
            part = flags[h][c : c + step]
            place = before + dot(part, upto, ((0,), (0,)))[:1]
            held = dot(part, same, ((0,), (0,)))[:1]
            hot = jnp.where((row == place) & (held > 0.5), 1.0, 0.0).astype(BF16)
            hot_out[:, h * half + c : h * half + c + step] = hot
            before = place[:, step - 1 :]


def pack_rows(hot, mine, other, at, feat):
    half = mine.shape[0]
    parts = [
        dot(hot[:, h * half : (h + 1) * half], in_order(mine, other, h, at, feat), ((1,), (0,))) for h in range(2)
    ]
    return add_all(parts).astype(BF16)


def first_kernel(mine, other, tea_w, inv, kernel_out, sent_out, hot_out):
    rows = kernel_out.shape[0]
    feat = tea_w.shape[0]
    packing([slot_flags(in_order(mine, other, h, 0, LANES)) for h in range(2)], hot_out)
    x = pack_rows(hot_out, mine, other, 0, feat)

    def body(at, acc):
        z = dot(x, tea_w[:, at], ((1,), (0,)))
        k = jnp.exp(z * (inv[:, at] * (1.0 / TEACHER_TEMP)))
        kernel_out[:, at] = k
        c = 1.0 / jnp.sum(k, axis=0, keepdims=True)
        return acc + fold(k * c)

    acc = over_chunks(tea_w.shape[1], body, jnp.zeros((rows, LANES), F32))
    tiles = to_tiles(acc, sent_out.shape[1] * LANES)
    sent_out[...] = jnp.broadcast_to(tiles[None], sent_out.shape)


def spots(hot, sums, at, half):
    return dot(hot[:, at : at + half], sums, ((0,), (1,)))


def halves(hot, sums, keep_out, give_out):
    half = keep_out.shape[0]
    low, high = spots(hot, sums, 0, half), spots(hot, sums, half, half)
    odd = odd_half() == 1
    keep_out[...] = jnp.where(odd, high, low)
    give_out[...] = jnp.where(odd, low, high).astype(BF16)


def student_kernel(mine, other, stu_w, hot, inv_out, logits_out, part_out, xt_out, keep_out, give_out, pulls):
    rows, columns = logits_out.shape
    feat = stu_w.shape[0]
    x = pack_rows(hot, mine, other, feat, feat)
    xt_out[...] = x.astype(F32).T.astype(BF16)

    def body(at, acc):
        w = stu_w[:, at]
        n = inverse_norms(w)
        inv_out[:, at] = n
        l = dot(x, w, ((1,), (0,))) * (n * (1.0 / STUDENT_TEMP))
        logits_out[:, at] = l
        p = jnp.exp(l)
        pulls[:, at] = (p * n).astype(BF16)
        return acc + fold(p)

    acc = over_chunks(columns, body, jnp.zeros((rows, LANES), F32))
    part_out[...] = to_tiles(acc, part_out.shape[0] * LANES)
    pull = dot(stu_w[...], pulls[...], ((1,), (1,)))
    halves(hot, pull.astype(BF16), keep_out, give_out)


def row_weights(mine, other, hot, own_out, weight_out, protos):
    devices = lax.axis_size(AXES)
    half = mine.shape[0]
    each = half // devices
    per_image = each * protos
    step = min(256, half)
    count, images = [], []
    block = iota((step, step), 0) // per_image
    same = (block == iota((step, step), 1) // per_image).astype(BF16)
    for c in range(0, half, step):
        flags = [slot_flags(ref[c : c + step, :LANES]).astype(F32) for ref in (mine, other)]
        held = dot(same, (flags[0] + flags[1]).astype(BF16), ((1,), (0,)))
        for h in range(2):
            count.append(dot(hot[:, h * half + c : h * half + c + step], held.astype(BF16), ((1,), (0,))))
        first = (iota(held.shape, 0) % per_image == 0) & (held > 0.5)
        images.append(jnp.sum(first.astype(F32), axis=0, keepdims=True))
    weight_out[...] = 1.0 / (jnp.maximum(add_all(count), 1.0) * add_all(images))

    own = own_out.shape[0]
    me = lax.axis_index("img") * protos + lax.axis_index("proto")
    q = iota((own, 2 * half), 0)
    spot = q // each * half + me * each + q % each
    mark = (iota((own, 2 * half), 1) == spot).astype(BF16)
    own_out[...] = dot(mark, hot[...], ((1,), (1,)))


def fill(sent_out, keep, got, vectors):
    devices, each, wide = sent_out.shape
    feat = keep.shape[1]
    sent_out[:, :, :feat] = (keep[...] + got[...].astype(F32)).reshape(devices, each, feat).astype(BF16)
    tiles = add_all_rows([part for vector in vectors for part in split(vector)], each, (wide - feat) // LANES)
    sent_out[:, :, feat:] = jnp.broadcast_to(tiles[None], (devices, each, wide - feat)).astype(BF16)


def add_all_rows(parts, each, groups):
    tiles = jnp.concatenate(parts, axis=0)
    spare = each * groups - tiles.shape[0]
    if spare:
        tiles = jnp.concatenate([tiles, jnp.zeros((spare, LANES), F32)], axis=0)
    return jnp.concatenate([tiles[g * each : (g + 1) * each] for g in range(groups)], axis=1)


def vectors_of(got, feat, width, count):
    _, each, wide = got.shape
    sums = jnp.sum(got[:, :, feat:].astype(F32), axis=0)
    tiles = jnp.concatenate([sums[:, g : g + LANES] for g in range(0, wide - feat, LANES)], axis=0)
    m = width // LANES
    return [tiles[2 * v * m : (2 * v + 1) * m] + tiles[(2 * v + 1) * m : (2 * v + 2) * m] for v in range(count)]


def slots_of(got, feat):
    devices, each, _ = got.shape
    parts = got[:, :, :feat].astype(F32).reshape(devices // 2, 2, each, feat)
    return jnp.sum(parts, axis=0).reshape(2 * each, feat)


def sweep_kernel(got, kernel, part, keep, give, sent_out):
    rows, columns = kernel.shape
    scale = to_column(1.0 / jnp.sum(got[...], axis=0), rows)
    wide = spread(scale, chunks(columns)[0].stop)

    def body(at, acc):
        k = kernel[:, at]
        c = 1.0 / jnp.sum(k * wide, axis=0, keepdims=True)
        return acc + fold(k * c)

    acc = over_chunks(columns, body, jnp.zeros((rows, LANES), F32))
    fill(sent_out, keep, give, [to_tiles(acc, part.shape[0] * LANES), part[...]])


def last_sweep_kernel(got, kernel, xt, stu_w, inv, hot, scaled_out, total_out, cross_out, keep_out, give_out, pushes):
    rows, columns = kernel.shape
    feat = stu_w.shape[0]
    width = total_out.shape[0] * LANES
    (total,) = vectors_of(got, feat, width, 1)
    scale = to_column(1.0 / total, rows)
    wide = spread(scale, chunks(columns)[0].stop)

    def body(at, acc):
        k = kernel[:, at]
        kc = k * (1.0 / jnp.sum(k * wide, axis=0, keepdims=True))
        scaled_out[:, at] = kc
        pushes[:, at] = (kc * inv[:, at]).astype(BF16)
        return acc + fold(kc)

    acc = over_chunks(columns, body, jnp.zeros((rows, LANES), F32))
    total_out[...] = to_tiles(acc, width)
    push = dot(stu_w[...], pushes[...], ((1,), (1,)))
    halves(hot, push.astype(BF16), keep_out, give_out)
    cross = jnp.sum(push * xt[...].astype(F32), axis=0, keepdims=True) * (1.0 / STUDENT_TEMP)
    if width > rows:
        cross = jnp.concatenate([cross, jnp.zeros((1, width - rows), F32)], axis=1)
    cross_out[...] = jnp.concatenate([cross[:, i : i + LANES] for i in range(0, width, LANES)], axis=0)


def fill_kernel(keep, got, total, cross, sent_out):
    fill(sent_out, keep, got, [total[...], cross[...]])


def prepare_kernel(
    got, scaled, logits, inv, mine, other, hot, pull_out, push_out, rise_out, log_out, own_out, weight_out, *, scale, protos
):
    rows, columns = scaled.shape
    feat = rise_out.shape[1]
    width = -(-rows // LANES) * LANES
    _, partition = vectors_of(got, feat, width, 2)
    partition = to_column(partition, rows)
    row_weights(mine, other, hot, own_out, weight_out, protos)
    share = weight_out[...]
    log_out[...] = jnp.log(partition)
    factor = share * (rows / STUDENT_TEMP)
    step = chunks(columns)[0].stop
    grow, shrink = spread(factor / partition, step), spread(factor, step)

    def body(at, _):
        n = inv[:, at] * scale
        pull_out[:, at] = grow * jnp.exp(logits[:, at]) * n
        push_out[:, at] = shrink * scaled[:, at] * n
        return 0

    over_chunks(columns, body, 0)
    held = dot(own_out[...], factor / partition, ((1,), (0,)), lax.Precision.HIGHEST)
    rise_out[...] = slots_of(got, feat) * held[:, :1]


def final_kernel(
    got,
    pull,
    push,
    logits,
    inv,
    stu_w,
    xt,
    weight,
    own,
    rise,
    log_part,
    unit,
    norm,
    out_hbm,
    rows_hbm,
    loss_hbm,
    out,
    rows_out,
    loss_out,
    sems,
):
    rows, columns = pull.shape
    feat = xt.shape[0]
    width = -(-rows // LANES) * LANES
    total, cross = vectors_of(got, feat, width, 2)
    scale = to_column(1.0 / total, rows)
    parts = chunks(columns)
    wide = spread(scale, parts[0].stop)
    copies = []

    def send(source, target):
        copies.append(pltpu.make_async_copy(source, target, sems.at[len(copies)]))
        copies[-1].start()

    for at in parts:
        g = pull[:, at] - wide * push[:, at]
        along = jnp.sum(g * logits[:, at], axis=0, keepdims=True) * (inv[:, at] * STUDENT_TEMP)
        out[:, at] = dot(xt[...], g.astype(BF16), ((1,), (0,))) - stu_w[:, at].astype(F32) * along
        send(out.at[:, at], out_hbm.at[:, at])
    share = weight[...]
    loss = jnp.sum(share * (log_part[...] - to_column(cross, rows) * scale), axis=0, keepdims=True)
    loss_out[...] = loss[:, :1]
    send(loss_out, loss_hbm)
    held = dot(own[...], share * (rows / STUDENT_TEMP) * scale, ((1,), (0,)), lax.Precision.HIGHEST)
    full = rise[...] - slots_of(got, feat) * held[:, :1]
    u = unit[...]
    rows_out[...] = (full - u * jnp.sum(u * full, axis=1, keepdims=True)) / norm[:, :1]
    send(rows_out, rows_hbm)
    for copy in copies:
        copy.wait()


def shards(student_feats, teacher_feats, student_weight, teacher_weight, patch_masks):
    devices = lax.axis_size(AXES)
    protos = lax.axis_size("proto")
    images, patches, feat = student_feats.shape
    assert images == 1 and protos % 2 == 0
    columns = student_weight.shape[1]
    own = patches // 2 // protos
    each = own // 2
    half = each * devices
    rows = 2 * half * 5 // 16
    tiles = -(-rows // LANES)
    wide = feat + LANES * -(-4 * tiles // each)
    big = rows * columns
    exchange = functools.partial(lax.all_to_all, axis_name=AXES, split_axis=0, concat_axis=0)
    swap = functools.partial(lax.ppermute, axis_name="proto", perm=[(p, p ^ 1) for p in range(protos)])
    vector = pltpu.VMEM((tiles, LANES), F32)
    matrix = pltpu.VMEM((rows, columns), F32)
    column = pltpu.VMEM((rows, LANES), F32)
    line = pltpu.VMEM((1, columns), F32)
    block, small = pltpu.VMEM((half, feat), F32), pltpu.VMEM((half, feat), BF16)
    payload = pltpu.VMEM((devices, each, wide), BF16)

    sent, unit, norm = call(
        select_kernel,
        (
            pltpu.VMEM((devices // 2, own, 2 * feat), BF16),
            pltpu.VMEM((own, feat), F32),
            pltpu.VMEM((own, LANES), F32),
        ),
        far(patch_masks),
        far(student_feats),
        far(teacher_feats),
        specs=[HBM] * 3,
        scratch=[
            pltpu.VMEM(patch_masks.shape, patch_masks.dtype),
            pltpu.VMEM(student_feats.shape, BF16),
            pltpu.VMEM(teacher_feats.shape, BF16),
            pltpu.SemaphoreType.DMA((3,)),
        ],
    )
    mine = exchange(sent.reshape(devices, each, 2 * feat)).reshape(half, 2 * feat)
    mine, teacher_weight = lax.optimization_barrier((mine, teacher_weight))
    other = near(swap(mine))
    mine = near(mine)
    tea_w, tea_inv = call(
        norms_kernel,
        (pltpu.VMEM(teacher_weight.shape, BF16), line),
        far(teacher_weight),
        flops=2 * feat * columns,
        moved=4 * feat * columns,
        specs=[HBM],
        scratch=[pltpu.SemaphoreType.DMA((len(chunks(columns)),))],
    )
    kernel, sent, hot = call(
        first_kernel,
        (matrix, pltpu.VMEM((devices, tiles, LANES), F32), pltpu.VMEM((rows, 2 * half), BF16)),
        mine,
        other,
        tea_w,
        tea_inv,
        flops=2 * big * feat,
        moved=4 * big,
        exps=big,
    )
    got = near(exchange(sent))
    mine, other, sent = lax.optimization_barrier((mine, other, sent))
    stu_inv, logits, part, xt, keep, give = call(
        student_kernel,
        (line, matrix, vector, pltpu.VMEM((feat, rows), BF16), block, small),
        mine,
        other,
        student_weight,
        hot,
        flops=4 * big * feat,
        moved=4 * big,
        exps=big,
        scratch=[pltpu.VMEM((rows, columns), BF16)],
    )
    give = near(swap(give))
    (sent,) = call(sweep_kernel, (payload,), got, kernel, part, keep, give, flops=4 * big, moved=4 * big)
    swept = near(exchange(sent))
    scaled, total, cross, keep, give = call(
        last_sweep_kernel,
        (matrix, vector, vector, block, small),
        swept,
        kernel,
        xt,
        student_weight,
        stu_inv,
        hot,
        flops=2 * big * feat,
        moved=12 * big,
        scratch=[pltpu.VMEM((rows, columns), BF16)],
    )
    give = near(swap(give))
    pull, push, rise, log_part, own_hot, weight = call(
        functools.partial(prepare_kernel, scale=columns * devices * GRAD_SCALE, protos=protos),
        (matrix, matrix, pltpu.VMEM((own, feat), F32), column, pltpu.VMEM((own, rows), F32), column),
        swept,
        scaled,
        logits,
        stu_inv,
        mine,
        other,
        hot,
        flops=4 * big,
        moved=16 * big,
        exps=big,
    )
    keep, pull, push, rise, log_part = lax.optimization_barrier((keep, pull, push, rise, log_part))
    (sent,) = call(fill_kernel, (payload,), keep, give, total, cross)
    got = near(exchange(sent))
    grad_weight, grad_rows, loss = call(
        final_kernel,
        (
            jax.ShapeDtypeStruct((feat, columns), F32),
            jax.ShapeDtypeStruct((own, feat), F32),
            jax.ShapeDtypeStruct((1, 1), F32),
        ),
        got,
        pull,
        push,
        logits,
        stu_inv,
        student_weight,
        xt,
        weight,
        own_hot,
        rise,
        log_part,
        unit,
        norm,
        flops=2 * big * feat,
        moved=8 * feat * columns,
        out_specs=(HBM, HBM, HBM),
        scratch=[
            pltpu.VMEM((feat, columns), F32),
            pltpu.VMEM((own, feat), F32),
            pltpu.VMEM((1, 1), F32),
            pltpu.SemaphoreType.DMA((len(chunks(columns)) + 2,)),
        ],
    )
    return loss.reshape(()), grad_weight, grad_rows


def solution(mesh):
    placed = (
        P("img", None, None),
        P("img", None, None),
        P(None, AXES),
        P(None, AXES),
        P("img", None),
    )
    return jax.shard_map(
        shards,
        mesh=mesh,
        in_specs=placed,
        out_specs=(P(), P(None, AXES), P(AXES, None)),
        check_vma=False,
    )
```

time: 79.1 us -> 72.4 us (0.915)
  Pallas kernels: 21.4 us -> 15.3 us
  waiting for transfers between devices: 1.49 us -> 0.01 us
    pallas_call x10 -> x9, Pallas kernels: 21.4 us -> 15.3 us  [call(): pl.pallas_call(body, out_shape=outs, in_specs=specs or [VMEM] * len(args)...]
    ppermute x2, waiting for transfers between devices: 1.49 us -> 0.01 us  [shards(): give = near(swap(give))]
  transfers between devices with their start and end apart: 3 -> 3, of which waited for: 2 -> 0; matrix products, arithmetic and copies ran while one was open for 0% -> 0% of each run, Pallas kernels for 6% -> 5%
where the time goes in v4:
time: 72.4 us; the launch traced here: 72.1 us
  blocking collectives  55.1 us (76%)
  Pallas kernels  15.3 us (21%)
    all_to_all x2, blocking collectives, shards(): got = near(exchange(sent))  22.5 us
    all_to_all x1, blocking collectives, shards(): exchange(sent.reshape(devices, each, 2 * feat)).reshape(half, 2 * feat)  20.3 us
    pallas_call x9, Pallas kernels, call(): pl.pallas_call(body, out_shape=outs, in_specs=specs or [VMEM] * len(args)...  15.3 us
    all_to_all x1, blocking collectives, shards(): swept = near(exchange(sent))  12.3 us
  transfers between devices with their start and end apart: 3, of which 0 were waited for; matrix products, arithmetic and copies ran while one was open for 0% of the time, Pallas kernels for 5%

profile of v4, /device:TPU:0, one launch (start us, length us, event | category | flops | bytes accessed | tf_op | source)
XLA Modules:
  0.0 72.1 jit_solution(8572709938408461349)
XLA Ops:
  0.6 1.4 %shard_map.76 = (bf16[16,16,768]{2,1,0:T(8,128)(2,1)S(1)}, f32[16,384]{1,0:T(8,128)S(1)}, f32[16,128]{1,0:T(8,128)S(1)}) custom-call(s32[1,128]{1,0:T(1,128)} %mask_hbm.1, bf16[1,128,384]{2,1,0:T(8,128)(2,1)} %stu_hbm.1, bf16[1,128,384]{2,1,0:T(8,128)(2,1)} %tea_hbm.1), custom_call_target="tpu_custom_call" | custom-call | tf_op jit(solution)/shard_map/pallas_call | solution.py:26
  2.1 20.3 %all_to_all.20 = bf16[32,8,768]{2,1,0:T(8,128)(2,1)S(1)} all-to-all(bf16[32,8,768]{2,1,0:T(8,128)(2,1)S(1)} %bitcast.7), channel_id=1, replica_groups=mesh['img'=8,'proto'=4] {'img','proto'}, dimensions={0} | all-to-all | bytes 786432 | tf_op jit(solution)/shard_map/all_to_all | solution.py:448
  22.3 0.0 collective-permute-start
  22.4 2.0 %shard_map.77 = (bf16[384,4096]{1,0:T(8,128)(2,1)S(1)}, f32[1,4096]{1,0:T(1,128)S(1)}) custom-call(bf16[384,4096]{1,0:T(8,128)(2,1)} %tea_hbm.2), custom_call_target="tpu_custom_call" | custom-call | flops 3145728 | bytes 6291456 | tf_op jit(solution)/shard_map/pallas_call | solution.py:26
  24.3 0.0 copy-start
  24.3 0.0 collective-permute-done.other
  24.4 1.6 %shard_map.78 = (f32[160,4096]{1,0:T(8,128)S(1)}, f32[32,2,128]{2,1,0:T(2,128)S(1)}, bf16[160,512]{1,0:T(8,128)(2,1)S(1)}) custom-call(bf16[256,768]{1,0:T(8,128)(2,1)S(1)} %bitcast.4, bf16[256,768]{1,0:T(8,128)(2,1)S(1)} %collective-permute-done.other, bf16[384,4096]{1,0:T(8,128)(2,1)S(1)} %get-tuple-element.43.tea_w, f32[1,4096]{1,0:T(1,128)S(1)} %get-tuple-element.44.inv), custom_call_target="tpu_custom_call" | custom-call | flops 503316480 | bytes 2621440 | tf_op jit(solution)/shard_map/pallas_call | solution.py:26
  25.9 0.3 copy-done
  26.2 2.7 %shard_map.79 = (f32[1,4096]{1,0:T(1,128)S(1)}, f32[160,4096]{1,0:T(8,128)S(1)}, f32[2,128]{1,0:T(2,128)S(1)}, bf16[384,160]{1,0:T(8,128)(2,1)S(1)}, f32[256,384...) custom-call(bf16[256,768]{1,0:T(8,128)(2,1)S(1)} %bitcast.5, bf16[256,768]{1,0:T(8,128)(2,1)S(1)} %collective-permute-done.other, ...), custom_call_target="tpu_custom_call" | custom-call | flops 1006632960 | bytes 2621440 | tf_op jit(solution)/shard_map/pallas_call | solution.py:26
  28.9 0.6 collective-permute-start.1
  29.5 9.7 %all_to_all.21.got = f32[32,2,128]{2,1,0:T(2,128)S(1)} all-to-all(f32[32,2,128]{2,1,0:T(2,128)S(1)} %get-tuple-element.45), channel_id=1, replica_groups=mesh['img'=8,'proto'=4] {'img','proto'}, dimensions={0} | all-to-all | bytes 65536 | tf_op jit(solution)/shard_map/all_to_all | solution.py:472
  39.2 0.0 collective-permute-done.1.give
  39.2 0.7 shard_map.80
  39.8 12.3 %all_to_all.22.got = bf16[32,8,512]{2,1,0:T(8,128)(2,1)S(1)} all-to-all(bf16[32,8,512]{2,1,0:T(8,128)(2,1)S(1)} %shard_map.80), channel_id=1, replica_groups=mesh['img'=8,'proto'=4] {'img','proto'}, dimensions={0} | all-to-all | bytes 524288 | tf_op jit(solution)/shard_map/all_to_all | solution.py:488
  52.2 2.1 %shard_map.81 = (f32[160,4096]{1,0:T(8,128)S(1)}, f32[2,128]{1,0:T(2,128)S(1)}, f32[2,128]{1,0:T(2,128)S(1)}, f32[256,384]{1,0:T(8,128)S(1)}, bf16[256,384]{1,0:T(8,128)(2,1)S(1)}) custom-call(bf16[32,8,512]{2,1,0:T(8,128)(2,1)S(1)} %all_to_all.22.got, f32[160,4096]{1,0:T(8,128)S(1)} %get-tuple-element.46.kernel, bf16[384,160]{1,0:T(8,128)(2,1)S(1)} %get-tuple-element.53.xt, ...), custom_call_target="tpu_custom_call" | custom-call | flops 503316480 | bytes 7864320 | tf_op jit(solution)/shard_map/pallas_call | solution.py:26
  54.3 0.1 collective-permute-start.2
  54.4 1.5 %shard_map.82 = (f32[160,4096]{1,0:T(8,128)S(1)}, f32[160,4096]{1,0:T(8,128)S(1)}, f32[16,384]{1,0:T(8,128)S(1)}, f32[160,128]{1,0:T(8,128)S(1)}, f32[16,160]{1,0:T(8,128)S(1)}, /*index=5*/f32[160,128]{1,0:T(8,128)S(1)}) custom-call(bf16[32,8,512]{2,1,0:T(8,128)(2,1)S(1)} %all_to_all.22.got, f32[160,4096]{1,0:T(8,128)S(1)} %get-tuple-element.56.scaled, ...), custom_call_target="tpu_custom_call" | custom-call | flops 2621440 | bytes 10485760 | tf_op jit(solution)/shard_map/pallas_call | solution.py:26
  55.9 0.0 collective-permute-done.2.got
  55.9 0.1 shard_map.83
  55.9 12.8 %all_to_all.23.got = bf16[32,8,512]{2,1,0:T(8,128)(2,1)S(1)} all-to-all(bf16[32,8,512]{2,1,0:T(8,128)(2,1)S(1)} %shard_map.83), channel_id=1, replica_groups=mesh['img'=8,'proto'=4] {'img','proto'}, dimensions={0} | all-to-all | bytes 524288 | tf_op jit(solution)/shard_map/all_to_all | solution.py:519
  68.8 3.3 %shard_map.84 = (f32[384,4096]{1,0:T(8,128)}, f32[16,384]{1,0:T(8,128)}, f32[1,1]{1,0:T(1,128)}) custom-call(bf16[32,8,512]{2,1,0:T(8,128)(2,1)S(1)} %all_to_all.23.got, f32[160,4096]{1,0:T(8,128)S(1)} %get-tuple-element.66.pull, f32[160,4096]{1,0:T(8,128)S(1)} %get-tuple-element.67.push, f32[160,4096]{1,0:T(8,128)S(1)} %get-tuple-element.57.logits, ...), custom_call_target="tpu_custom_call" | custom-call | flops 503316480 | bytes 12582912 | tf_op jit(solution)/shard_map/pallas_call | solution.py:26
Async XLA Ops:
  22.3 2.0 %collective-permute-start = (bf16[256,768]{1,0:T(8,128)(2,1)S(1)}, bf16[256,768]{1,0:T(8,128)(2,1)S(1)}, u32[]{:S(2)}, u32[]{:S(2)}) collective-permute-start(bf16[256,768]{1,0:T(8,128)(2,1)S(1)} %bitcast.3), channel_id=1, source_target_pairs={{0,1},{1,0},{2,3},{3,2},{4,5},{5,4},{6,7},{7,6},{8,9},{9,8},{10,11... | collective-permute-start | bytes 1179656 | tf_op jit(solution)/shard_map/ppermute | solution.py:450
  24.3 1.9 %copy-start = (bf16[384,4096]{1,0:T(8,128)(2,1)S(1)}, bf16[384,4096]{1,0:T(8,128)(2,1)}, u32[]{:S(2)}) copy-start(bf16[384,4096]{1,0:T(8,128)(2,1)} %stu_w.5) | copy-start | bytes 9437188
  28.9 10.3 %collective-permute-start.1 = (bf16[256,384]{1,0:T(8,128)(2,1)S(1)}, bf16[256,384]{1,0:T(8,128)(2,1)S(1)}, u32[]{:S(2)}, u32[]{:S(2)}) collective-permute-start(bf16[256,384]{1,0:T(8,128)(2,1)S(1)} %get-tuple-element.52), channel_id=1, source_target_pairs={{0,1},{1,0},{2,3},{3,2},{4,5},{5,4},{6,7},{7,6},{8,9},{9,8},{10,11... | collective-permute-start | bytes 589832 | tf_op jit(solution)/shard_map/ppermute | solution.py:486
  54.3 1.6 %collective-permute-start.2 = (bf16[256,384]{1,0:T(8,128)(2,1)S(1)}, bf16[256,384]{1,0:T(8,128)(2,1)S(1)}, u32[]{:S(2)}, u32[]{:S(2)}) collective-permute-start(bf16[256,384]{1,0:T(8,128)(2,1)S(1)} %get-tuple-element.63), channel_id=1, source_target_pairs={{0,1},{1,0},{2,3},{3,2},{4,5},{5,4},{6,7},{7,6},{8,9},{9,8},{10,11... | collective-permute-start | bytes 589832 | tf_op jit(solution)/shard_map/ppermute | solution.py:502

commit v5 on v4

v5 whole, which is shorter than its diff:
```python
import functools

import jax
import jax.numpy as jnp
from jax import lax
from jax.experimental import pallas as pl
from jax.experimental.pallas import tpu as pltpu
from jax.sharding import PartitionSpec as P

ITERS = 3
TEACHER_TEMP = 0.07
STUDENT_TEMP = 0.1
NORM_EPS = 1e-06
GRAD_SCALE = 1.0 / 128.0
EMPTY = 2.0
LANES = 128
F32 = jnp.float32
BF16 = jnp.bfloat16
AXES = ("img", "proto")

VMEM = pl.BlockSpec(memory_space=pltpu.VMEM)
HBM = pl.BlockSpec(memory_space=pltpu.HBM)


def call(body, outs, *args, flops=0, moved=0, exps=0, limit=24, specs=None, out_specs=None, scratch=()):
    return pl.pallas_call(
        body,
        out_shape=outs,
        in_specs=specs or [VMEM] * len(args),
        out_specs=out_specs or tuple(VMEM for _ in outs),
        scratch_shapes=scratch,
        compiler_params=pltpu.CompilerParams(vmem_limit_bytes=limit * 1024 * 1024),
        cost_estimate=pl.CostEstimate(flops=flops, bytes_accessed=moved, transcendentals=exps),
    )(*args)


def near(x):
    return pltpu.with_memory_space_constraint(x, pltpu.VMEM)


def far(x):
    return pltpu.with_memory_space_constraint(x, pltpu.HBM)


def dot(a, b, dims, precision=None):
    return lax.dot_general(a, b, (dims, ((), ())), precision=precision, preferred_element_type=F32)


def iota(shape, dim):
    return lax.broadcasted_iota(jnp.int32, shape, dim)


def add_all(parts):
    return functools.reduce(jnp.add, parts)


def widen(row):
    spare = -row.shape[1] % LANES
    return jnp.concatenate([row, jnp.zeros((1, spare), F32)], axis=1) if spare else row


def tiles_of(row):
    row = widen(row)
    return [row[:, i : i + LANES] for i in range(0, row.shape[1], LANES)]


def to_column(row):
    parts = [jnp.broadcast_to(tile, (LANES, LANES)).T for tile in tiles_of(row)]
    return jnp.concatenate(parts, axis=0)[: row.shape[1]]


def to_row(part):
    rows = part.shape[0]
    spare = -rows % LANES
    if spare:
        part = jnp.concatenate([part, jnp.zeros((spare, LANES), F32)], axis=0)
    return jnp.sum(part.T, axis=0, keepdims=True)[:, :rows]


def lay_out(vectors, each, wide):
    parts = []
    for vector in vectors:
        high = vector.astype(BF16).astype(F32)
        parts += [high, vector - high]
    tiles = tiles_of(jnp.concatenate(parts, axis=1))
    tiles += [jnp.zeros((1, LANES), F32)] * (each * wide // LANES - len(tiles))
    groups = [jnp.concatenate(tiles[g : g + each], axis=0) for g in range(0, len(tiles), each)]
    return jnp.concatenate(groups, axis=1)


def read_out(got, start, rows, count):
    _, each, wide = got.shape
    sums = jnp.sum(got[:, :, start:].astype(F32), axis=0)
    line = jnp.concatenate([sums[i : i + 1, g : g + LANES] for g in range(0, wide - start, LANES) for i in range(each)], axis=1)
    parts = [line[:, p * rows : (p + 1) * rows] for p in range(2 * count)]
    return [parts[2 * v] + parts[2 * v + 1] for v in range(count)]


def fold(x):
    return add_all([x[:, i : i + LANES] for i in range(0, x.shape[1], LANES)])


def spread(col, width):
    return jnp.concatenate([col] * (width // LANES), axis=1)


def chunks(columns):
    step = min(512, columns)
    return [slice(at, at + step) for at in range(0, columns, step)]


def over_chunks(columns, body, start):
    for at in chunks(columns):
        start = body(at, start)
    return start


def start_load(source, target, sems):
    parts = chunks(target.shape[1])
    copies = [pltpu.make_async_copy(source.at[:, at], target.at[:, at], sems.at[i]) for i, at in enumerate(parts)]
    for copy in copies:
        copy.start()
    return copies


def inverse_norms(w):
    w = w.astype(F32)
    return 1.0 / jnp.sqrt(jnp.sum(w * w, axis=0, keepdims=True) + NORM_EPS)


def odd_half():
    return lax.rem(lax.axis_index("proto"), 2)


def select_kernel(mask_hbm, stu_hbm, tea_hbm, sent_out, unit_out, norm_out, mask_ref, stu_ref, tea_ref, sems):
    pairs = ((mask_hbm, mask_ref), (tea_hbm, tea_ref), (stu_hbm, stu_ref))
    copies = [pltpu.make_async_copy(*pair, sems.at[i]) for i, pair in enumerate(pairs)]
    for copy in copies:
        copy.start()
    copies[0].wait()
    own, feat = unit_out.shape
    patches = mask_ref.shape[1]
    slot = iota((own, patches), 0) + lax.axis_index("proto") * own
    mask = jnp.broadcast_to(mask_ref[...].astype(F32), (own, patches))
    upto = (iota((patches, patches), 0) <= iota((patches, patches), 1)).astype(BF16)
    rank = dot(mask.astype(BF16), upto, ((1,), (0,)))
    pick = jnp.where((rank == slot.astype(F32) + 1.0) & (mask > 0.5), 1.0, 0.0).astype(BF16)
    valid = slot[:, :1].astype(F32) < rank[:, patches - 1 :]
    for copy, source in ((copies[1], tea_ref), (copies[2], stu_ref)):
        copy.wait()
        rows = dot(pick, source[0], ((1,), (0,)))
        norm = jnp.sqrt(jnp.sum(rows * rows, axis=1, keepdims=True) + NORM_EPS)
        unit = (rows / norm).astype(BF16)
        if source is tea_ref:
            sent = jnp.where(valid, unit.astype(F32), EMPTY).astype(BF16)
            sent_out[...] = jnp.broadcast_to(sent[None], sent_out.shape)
        else:
            unit_out[...] = unit.astype(F32)
            norm_out[...] = jnp.broadcast_to(norm, norm_out.shape)


def norms_kernel(tea_hbm, tea_w, inv_out, sems):
    copies = start_load(tea_hbm, tea_w, sems)
    for copy, at in zip(copies, chunks(tea_w.shape[1])):
        copy.wait()
        inv_out[:, at] = inverse_norms(tea_w[:, at])


def in_order(mine, other, h):
    return jnp.where(odd_half() == h, mine, other)


def slot_flags(data):
    return jnp.where(data[:, :LANES].astype(F32) < 1.5, 1.0, 0.0).astype(BF16)


def packing(flags, hot_out):
    rows = hot_out.shape[0]
    half = flags[0].shape[0]
    step = min(256, half)
    before = jnp.zeros((1, 1), F32)
    upto = (iota((step, step), 0) <= iota((step, step), 1)).astype(BF16)
    same = (iota((step, step), 0) == iota((step, step), 1)).astype(BF16)
    row = iota((rows, step), 0).astype(F32) + 1.0
    for h in range(2):
        for c in range(0, half, step):
            part = flags[h][c : c + step]
            place = before + dot(part, upto, ((0,), (0,)))[:1]
            held = dot(part, same, ((0,), (0,)))[:1]
            hot = jnp.where((row == place) & (held > 0.5), 1.0, 0.0).astype(BF16)
            hot_out[:, h * half + c : h * half + c + step] = hot
            before = place[:, step - 1 :]


def blocks(half):
    step = min(256, half)
    return [(at, at + step) for at in range(0, half, step)]


def pack_rows(hot, read_mine, read_other, half):
    parts = []
    for start, stop in blocks(half):
        mine, other = read_mine(start, stop), read_other(start, stop)
        for h in range(2):
            parts.append(dot(hot[:, h * half + start : h * half + stop], in_order(mine, other, h), ((1,), (0,))))
    return add_all(parts).astype(BF16)


def first_kernel(mine, other, tea_w, inv, unit, kernel_out, sent_out, hot_out):
    rows = kernel_out.shape[0]
    devices, each, wide = sent_out.shape
    feat = tea_w.shape[0]
    packing([slot_flags(in_order(mine[:, :LANES], other[:, :LANES], h)) for h in range(2)], hot_out)
    x = pack_rows(hot_out, lambda a, b: mine[a:b], lambda a, b: other[a:b], mine.shape[0])
    held = unit[...].reshape(1, 2, each, feat)
    sent_out[:, :, :feat] = jnp.broadcast_to(held, (devices // 2, 2, each, feat)).reshape(devices, each, feat).astype(BF16)

    def body(at, acc):
        z = dot(x, tea_w[:, at], ((1,), (0,)))
        k = jnp.exp(z * (inv[:, at] * (1.0 / TEACHER_TEMP)))
        kernel_out[:, at] = k
        c = 1.0 / jnp.sum(k, axis=0, keepdims=True)
        return acc + fold(k * c)

    acc = over_chunks(tea_w.shape[1], body, jnp.zeros((rows, LANES), F32))
    tiles = lay_out([to_row(acc)], each, wide - feat)
    sent_out[:, :, feat:] = jnp.broadcast_to(tiles[None], (devices, each, wide - feat)).astype(BF16)


def spots(hot, sums, start, stop):
    return dot(hot[:, start:stop], sums, ((0,), (1,)))


def halves(hot, sums, at, keep_out, give_out):
    half = keep_out.shape[0]
    odd = odd_half() == 1
    lanes = slice(at, at + sums.shape[0])
    for start, stop in blocks(half):
        low, high = spots(hot, sums, start, stop), spots(hot, sums, half + start, half + stop)
        keep_out[start:stop, lanes] = jnp.where(odd, high, low)
        give_out[start:stop, lanes] = jnp.where(odd, low, high).astype(BF16)


def row_weights(mine, other, hot, own_out, weight_out, protos):
    devices = lax.axis_size(AXES)
    half = mine.shape[0]
    each = half // devices
    per_image = each * protos
    step = min(256, half)
    count, images = [], []
    block = iota((step, step), 0) // per_image
    same = (block == iota((step, step), 1) // per_image).astype(BF16)
    for c in range(0, half, step):
        flags = [slot_flags(ref[c : c + step, :LANES]).astype(F32) for ref in (mine, other)]
        held = dot(same, (flags[0] + flags[1]).astype(BF16), ((1,), (0,)))
        for h in range(2):
            count.append(dot(hot[:, h * half + c : h * half + c + step], held.astype(BF16), ((1,), (0,))))
        first = (iota(held.shape, 0) % per_image == 0) & (held > 0.5)
        images.append(jnp.sum(first.astype(F32), axis=0, keepdims=True))
    weight_out[...] = 1.0 / (jnp.maximum(add_all(count), 1.0) * add_all(images))

    own = own_out.shape[0]
    me = lax.axis_index("img") * protos + lax.axis_index("proto")
    q = iota((own, 2 * half), 0)
    spot = q // each * half + me * each + q % each
    mark = (iota((own, 2 * half), 1) == spot).astype(BF16)
    own_out[...] = dot(mark, hot[...], ((1,), (1,)))


def slots_of(got, feat):
    devices, each, _ = got.shape
    parts = got[:, :, :feat].astype(F32).reshape(devices // 2, 2, each, feat)
    return jnp.sum(parts, axis=0).reshape(2 * each, feat)


def sweep_kernel(got, kernel, sent_out, *, feat):
    rows, columns = kernel.shape
    (total,) = read_out(got, feat, rows, 1)
    wide = spread(to_column(1.0 / total), chunks(columns)[0].stop)

    def body(at, acc):
        k = kernel[:, at]
        c = 1.0 / jnp.sum(k * wide, axis=0, keepdims=True)
        return acc + fold(k * c)

    acc = over_chunks(columns, body, jnp.zeros((rows, LANES), F32))
    tiles = jnp.concatenate(tiles_of(to_row(acc)), axis=0)
    sent_out[...] = jnp.broadcast_to(tiles[None], sent_out.shape)


def student_kernel(
    got,
    kernel,
    mine,
    other,
    hot,
    stu_w,
    inv_out,
    logits_out,
    scaled_out,
    xt_out,
    sums_out,
    keep_out,
    give_out,
    pulls,
    pushes,
):
    rows, columns = logits_out.shape
    feat = stu_w.shape[0]
    half = keep_out.shape[0]
    each = mine.shape[1]

    def reader(ref):
        def read(start, stop):
            part = ref[start // each : stop // each, :, :feat].astype(F32)
            return part.reshape(stop - start, feat).astype(BF16)

        return read

    x = pack_rows(hot, reader(mine), reader(other), half)
    xt = x.astype(F32).T
    xt_out[...] = xt.astype(BF16)
    sums = jnp.sum(got[...], axis=0)
    total = jnp.concatenate([sums[i : i + 1] for i in range(sums.shape[0])], axis=1)[:, :rows]
    wide = spread(to_column(1.0 / total), chunks(columns)[0].stop)

    def student(at, acc):
        w = stu_w[:, at]
        n = inverse_norms(w)
        inv_out[:, at] = n
        l = dot(x, w, ((1,), (0,))) * (n * (1.0 / STUDENT_TEMP))
        logits_out[:, at] = l
        p = jnp.exp(l)
        pulls[:, at] = (p * n).astype(BF16)
        return acc + fold(p)

    def sweep(at, acc):
        k = kernel[:, at]
        kc = k * (1.0 / jnp.sum(k * wide, axis=0, keepdims=True))
        scaled_out[:, at] = kc
        pushes[:, at] = (kc * inv_out[:, at]).astype(BF16)
        return acc + fold(kc)

    zero = jnp.zeros((rows, LANES), F32)
    part = over_chunks(columns, student, zero)
    pull = dot(stu_w[...], pulls[...], ((1,), (1,)))
    total = over_chunks(columns, sweep, zero)
    push = dot(stu_w[...], pushes[...], ((1,), (1,)))
    halves(hot, pull.astype(BF16), 0, keep_out, give_out)
    halves(hot, push.astype(BF16), feat, keep_out, give_out)
    cross = jnp.sum(push * xt, axis=0, keepdims=True) * (1.0 / STUDENT_TEMP)
    sums_out[...] = lay_out([to_row(part), to_row(total), cross], *sums_out.shape)


def prepare_kernel(
    scaled, logits, inv, mine, other, hot, pull_out, push_out, own_out, weight_out, *, scale, protos
):
    rows, columns = scaled.shape
    row_weights(mine, other, hot, own_out, weight_out, protos)
    factor = spread(weight_out[...] * (rows / STUDENT_TEMP), chunks(columns)[0].stop)

    def body(at, _):
        n = inv[:, at] * scale
        pull_out[:, at] = factor * jnp.exp(logits[:, at]) * n
        push_out[:, at] = factor * scaled[:, at] * n
        return 0

    over_chunks(columns, body, 0)


def fill_kernel(keep, give, sums, sent_out):
    devices, each, wide = sent_out.shape
    both = keep.shape[1]
    sent_out[:, :, :both] = (keep[...] + give[...].astype(F32)).reshape(devices, each, both).astype(BF16)
    sent_out[:, :, both:] = jnp.broadcast_to(sums[...][None], (devices, each, wide - both)).astype(BF16)


def final_kernel(
    got,
    pull,
    push,
    logits,
    inv,
    stu_w,
    xt,
    weight,
    own,
    unit,
    norm,
    out_hbm,
    rows_hbm,
    loss_hbm,
    out,
    rows_out,
    loss_out,
    sems,
):
    rows, columns = pull.shape
    feat = xt.shape[0]
    partition, total, cross = read_out(got, 2 * feat, rows, 3)
    parts = chunks(columns)
    raise_by, lower_by = to_column(1.0 / partition), to_column(1.0 / total)
    grow, shrink = spread(raise_by, parts[0].stop), spread(lower_by, parts[0].stop)
    copies = []

    def send(source, target):
        copies.append(pltpu.make_async_copy(source, target, sems.at[len(copies)]))
        copies[-1].start()

    for at in parts:
        g = grow * pull[:, at] - shrink * push[:, at]
        along = jnp.sum(g * logits[:, at], axis=0, keepdims=True) * (inv[:, at] * STUDENT_TEMP)
        out[:, at] = dot(xt[...], g.astype(BF16), ((1,), (0,))) - stu_w[:, at].astype(F32) * along
        send(out.at[:, at], out_hbm.at[:, at])
    share = weight[...]
    loss = jnp.sum(share * to_column(jnp.log(partition) - cross / total), axis=0, keepdims=True)
    loss_out[...] = loss[:, :1]
    send(loss_out, loss_hbm)
    factors = jnp.concatenate([raise_by, lower_by], axis=1) * spread(share * (rows / STUDENT_TEMP), 2 * LANES)
    held = dot(own[...], factors, ((1,), (0,)), lax.Precision.HIGHEST)
    sums = slots_of(got, 2 * feat)
    full = sums[:, :feat] * held[:, :1] - sums[:, feat:] * held[:, LANES : LANES + 1]
    u = unit[...]
    rows_out[...] = (full - u * jnp.sum(u * full, axis=1, keepdims=True)) / norm[:, :1]
    send(rows_out, rows_hbm)
    for copy in copies:
        copy.wait()


def shards(student_feats, teacher_feats, student_weight, teacher_weight, patch_masks):
    devices = lax.axis_size(AXES)
    protos = lax.axis_size("proto")
    images, patches, feat = student_feats.shape
    assert images == 1 and protos % 2 == 0
    columns = student_weight.shape[1]
    own = patches // 2 // protos
    each = own // 2
    half = each * devices
    rows = 2 * half * 5 // 16
    tiles = -(-rows // LANES)
    extra = lambda parts: LANES * -(-parts * rows // (each * LANES))
    big = rows * columns
    exchange = functools.partial(lax.all_to_all, axis_name=AXES, split_axis=0, concat_axis=0)
    swap = functools.partial(lax.ppermute, axis_name="proto", perm=[(p, p ^ 1) for p in range(protos)])
    matrix = pltpu.VMEM((rows, columns), F32)
    column = pltpu.VMEM((rows, LANES), F32)
    line = pltpu.VMEM((1, columns), F32)

    sent, unit, norm = call(
        select_kernel,
        (
            pltpu.VMEM((devices // 2, own, feat), BF16),
            pltpu.VMEM((own, feat), F32),
            pltpu.VMEM((own, LANES), F32),
        ),
        far(patch_masks),
        far(student_feats),
        far(teacher_feats),
        specs=[HBM] * 3,
        scratch=[
            pltpu.VMEM(patch_masks.shape, patch_masks.dtype),
            pltpu.VMEM(student_feats.shape, BF16),
            pltpu.VMEM(teacher_feats.shape, BF16),
            pltpu.SemaphoreType.DMA((3,)),
        ],
    )
    mine = exchange(sent.reshape(devices, each, feat)).reshape(half, feat)
    mine, teacher_weight = lax.optimization_barrier((mine, teacher_weight))
    other = near(swap(mine))
    mine = near(mine)
    tea_w, tea_inv = call(
        norms_kernel,
        (pltpu.VMEM(teacher_weight.shape, BF16), line),
        far(teacher_weight),
        flops=2 * feat * columns,
        moved=4 * feat * columns,
        specs=[HBM],
        scratch=[pltpu.SemaphoreType.DMA((len(chunks(columns)),))],
    )
    kernel, sent, hot = call(
        first_kernel,
        (matrix, pltpu.VMEM((devices, each, feat + extra(2)), BF16), pltpu.VMEM((rows, 2 * half), BF16)),
        mine,
        other,
        tea_w,
        tea_inv,
        unit,
        flops=2 * big * feat,
        moved=4 * big,
        exps=big,
    )
    stu_mine = exchange(sent)
    stu_other = near(swap(stu_mine))
    stu_mine = near(stu_mine)
    (sent,) = call(
        functools.partial(sweep_kernel, feat=feat),
        (pltpu.VMEM((devices, tiles, LANES), F32),),
        stu_mine,
        kernel,
        flops=4 * big,
        moved=4 * big,
    )
    got = near(exchange(sent))
    stu_inv, logits, scaled, xt, sums, keep, give = call(
        student_kernel,
        (
            line,
            matrix,
            matrix,
            pltpu.VMEM((feat, rows), BF16),
            pltpu.VMEM((each, extra(6)), F32),
            pltpu.VMEM((half, 2 * feat), F32),
            pltpu.VMEM((half, 2 * feat), BF16),
        ),
        got,
        kernel,
        stu_mine,
        stu_other,
        hot,
        student_weight,
        flops=6 * big * feat,
        moved=12 * big,
        exps=big,
        scratch=[pltpu.VMEM((rows, columns), BF16), pltpu.VMEM((rows, columns), BF16)],
        limit=22 + half // 112,
    )
    give = near(swap(give))
    pull, push, own_hot, weight = call(
        functools.partial(prepare_kernel, scale=columns * devices * GRAD_SCALE, protos=protos),
        (matrix, matrix, pltpu.VMEM((own, rows), F32), column),
        scaled,
        logits,
        stu_inv,
        mine,
        other,
        hot,
        flops=4 * big,
        moved=16 * big,
        exps=big,
    )
    keep, pull, push, own_hot, weight = lax.optimization_barrier((keep, pull, push, own_hot, weight))
    (sent,) = call(fill_kernel, (pltpu.VMEM((devices, each, 2 * feat + extra(6)), BF16),), keep, give, sums)
    got = near(exchange(sent))
    grad_weight, grad_rows, loss = call(
        final_kernel,
        (
            jax.ShapeDtypeStruct((feat, columns), F32),
            jax.ShapeDtypeStruct((own, feat), F32),
            jax.ShapeDtypeStruct((1, 1), F32),
        ),
        got,
        pull,
        push,
        logits,
        stu_inv,
        student_weight,
        xt,
        weight,
        own_hot,
        unit,
        norm,
        flops=2 * big * feat,
        moved=8 * feat * columns,
        out_specs=(HBM, HBM, HBM),
        scratch=[
            pltpu.VMEM((feat, columns), F32),
            pltpu.VMEM((own, feat), F32),
            pltpu.VMEM((1, 1), F32),
            pltpu.SemaphoreType.DMA((len(chunks(columns)) + 2,)),
        ],
    )
    return loss.reshape(()), grad_weight, grad_rows


def solution(mesh):
    placed = (
        P("img", None, None),
        P("img", None, None),
        P(None, AXES),
        P(None, AXES),
        P("img", None),
    )
    return jax.shard_map(
        shards,
        mesh=mesh,
        in_specs=placed,
        out_specs=(P(), P(None, AXES), P(AXES, None)),
        check_vma=False,
    )
```

time: 72.4 us -> 71 us (0.981)
  blocking collectives: 55.1 us -> 54.3 us
  Pallas kernels: 15.3 us -> 14.5 us
    all_to_all x2, blocking collectives: 32.6 us -> 28.6 us  [the longest x1 16 us: shards(): mine = exchange(sent.reshape(devices, each, feat)).reshape(half, feat)]
    all_to_all x2, blocking collectives: 22.5 us -> 25.7 us  [shards(): got = near(exchange(sent))]
    pallas_call x9 -> x8, Pallas kernels: 15.3 us -> 14.5 us  [call(): pl.pallas_call(body, out_shape=outs, in_specs=specs or [VMEM] * len(args)...]
  transfers between devices with their start and end apart: 3 -> 3, of which waited for: 0 -> 1; matrix products, arithmetic and copies ran while one was open for 0% -> 0% of each run, Pallas kernels for 5% -> 5%
where the time goes in v5:
time: 71 us; the launch traced here: 70.7 us
  blocking collectives  54.3 us (76%)
  Pallas kernels  14.5 us (20%)
  starting transfers between devices  0.78 us (1%)
    all_to_all x2, blocking collectives, shards(): got = near(exchange(sent))  25.7 us
    all_to_all x1, blocking collectives, shards(): mine = exchange(sent.reshape(devices, each, feat)).reshape(half, feat)  16 us
    pallas_call x8, Pallas kernels, call(): pl.pallas_call(body, out_shape=outs, in_specs=specs or [VMEM] * len(args)...  14.5 us
    all_to_all x1, blocking collectives, shards(): stu_mine = exchange(sent)  12.6 us
  transfers between devices with their start and end apart: 3, of which 1 were waited for; matrix products, arithmetic and copies ran while one was open for 0% of the time, Pallas kernels for 5%

profile of v5, /device:TPU:0, one launch (start us, length us, event | category | flops | bytes accessed | tf_op | source)
XLA Modules:
  0.0 70.7 jit_solution(3909906669342314073)
XLA Ops:
  0.6 1.4 %shard_map.76 = (bf16[16,16,384]{2,1,0:T(8,128)(2,1)S(1)}, f32[16,384]{1,0:T(8,128)S(1)}, f32[16,128]{1,0:T(8,128)S(1)}) custom-call(s32[1,128]{1,0:T(1,128)} %mask_hbm.1, bf16[1,128,384]{2,1,0:T(8,128)(2,1)} %stu_hbm.1, bf16[1,128,384]{2,1,0:T(8,128)(2,1)} %tea_hbm.1), custom_call_target="tpu_custom_call" | custom-call | tf_op jit(solution)/shard_map/pallas_call | solution.py:26
  2.0 16.0 %all_to_all.20 = bf16[32,8,384]{2,1,0:T(8,128)(2,1)S(1)} all-to-all(bf16[32,8,384]{2,1,0:T(8,128)(2,1)S(1)} %bitcast.6), channel_id=1, replica_groups=mesh['img'=8,'proto'=4] {'img','proto'}, dimensions={0} | all-to-all | bytes 393216 | tf_op jit(solution)/shard_map/all_to_all | solution.py:467
  18.0 0.6 collective-permute-start
  18.6 2.0 %shard_map.77 = (bf16[384,4096]{1,0:T(8,128)(2,1)S(1)}, f32[1,4096]{1,0:T(1,128)S(1)}) custom-call(bf16[384,4096]{1,0:T(8,128)(2,1)} %tea_hbm.2), custom_call_target="tpu_custom_call" | custom-call | flops 3145728 | bytes 6291456 | tf_op jit(solution)/shard_map/pallas_call | solution.py:26
  20.6 0.0 collective-permute-done.other
  20.6 1.6 %shard_map.78 = (f32[160,4096]{1,0:T(8,128)S(1)}, bf16[32,8,512]{2,1,0:T(8,128)(2,1)S(1)}, bf16[160,512]{1,0:T(8,128)(2,1)S(1)}) custom-call(bf16[256,384]{1,0:T(8,128)(2,1)S(1)} %bitcast.4, bf16[256,384]{1,0:T(8,128)(2,1)S(1)} %collective-permute-done.other, bf16[384,4096]{1,0:T(8,128)(2,1)S(1)} %get-tuple-element.35.tea_w, ...), custom_call_target="tpu_custom_call" | custom-call | flops 503316480 | bytes 2621440 | tf_op jit(solution)/shard_map/pallas_call | solution.py:26
  22.3 0.0 copy-start
  22.3 12.6 %all_to_all.21.got.mine = bf16[32,8,512]{2,1,0:T(8,128)(2,1)S(1)} all-to-all(bf16[32,8,512]{2,1,0:T(8,128)(2,1)S(1)} %get-tuple-element.38), channel_id=1, replica_groups=mesh['img'=8,'proto'=4] {'img','proto'}, dimensions={0} | all-to-all | bytes 524288 | tf_op jit(solution)/shard_map/all_to_all | solution.py:492
  34.9 0.0 collective-permute-start.1
  34.9 0.7 %shard_map.79 = f32[32,2,128]{2,1,0:T(2,128)S(1)} custom-call(bf16[32,8,512]{2,1,0:T(8,128)(2,1)S(1)} %all_to_all.21.got.mine, f32[160,4096]{1,0:T(8,128)S(1)} %get-tuple-element.39.kernel), custom_call_target="tpu_custom_call" | custom-call | flops 2621440 | bytes 2621440 | tf_op jit(solution)/shard_map/pallas_call | solution.py:26
  35.7 9.6 %all_to_all.22.got = f32[32,2,128]{2,1,0:T(2,128)S(1)} all-to-all(f32[32,2,128]{2,1,0:T(2,128)S(1)} %shard_map.79), channel_id=1, replica_groups=mesh['img'=8,'proto'=4] {'img','proto'}, dimensions={0} | all-to-all | bytes 65536 | tf_op jit(solution)/shard_map/all_to_all | solution.py:503
  45.2 0.0 collective-permute-done.1.other
  45.2 0.0 copy-done
  45.2 4.0 %shard_map.80 = (f32[1,4096]{1,0:T(1,128)S(1)}, f32[160,4096]{1,0:T(8,128)S(1)}, f32[160,4096]{1,0:T(8,128)S(1)}, bf16[384,160]{1,0:T(8,128)(2,1)S(1)}, f32[8,12...) custom-call(f32[32,2,128]{2,1,0:T(2,128)S(1)} %all_to_all.22.got, ...), custom_call_target="tpu_custom_call" | custom-call | flops 1509949440 | bytes 7864320 | tf_op jit(solution)/shard_map/pallas_call | solution.py:26
  49.2 0.2 collective-permute-start.2
  49.4 1.1 %shard_map.81 = (f32[160,4096]{1,0:T(8,128)S(1)}, f32[160,4096]{1,0:T(8,128)S(1)}, f32[16,160]{1,0:T(8,128)S(1)}, f32[160,128]{1,0:T(8,128)S(1)}) custom-call(f32[160,4096]{1,0:T(8,128)S(1)} %get-tuple-element.42.scaled, f32[160,4096]{1,0:T(8,128)S(1)} %get-tuple-element.43.logits, f32[1,4096]{1,0:T(1,128)S(1)} %get-tuple-element.44.inv, ...), custom_call_target="tpu_custom_call" | custom-call | flops 2621440 | bytes 10485760 | tf_op jit(solution)/shard_map/pallas_call | solution.py:26
  50.5 0.5 collective-permute-done.2.give
  51.0 0.1 shard_map.82
  51.1 16.1 %all_to_all.23.got = bf16[32,8,896]{2,1,0:T(8,128)(2,1)S(1)} all-to-all(bf16[32,8,896]{2,1,0:T(8,128)(2,1)S(1)} %shard_map.82), channel_id=1, replica_groups=mesh['img'=8,'proto'=4] {'img','proto'}, dimensions={0} | all-to-all | bytes 917504 | tf_op jit(solution)/shard_map/all_to_all | solution.py:543
  67.2 3.5 %shard_map.83 = (f32[384,4096]{1,0:T(8,128)}, f32[16,384]{1,0:T(8,128)}, f32[1,1]{1,0:T(1,128)}) custom-call(bf16[32,8,896]{2,1,0:T(8,128)(2,1)S(1)} %all_to_all.23.got, f32[160,4096]{1,0:T(8,128)S(1)} %get-tuple-element.52.pull, f32[160,4096]{1,0:T(8,128)S(1)} %get-tuple-element.53.push, f32[160,4096]{1,0:T(8,128)S(1)} %get-tuple-element.43.logits, ...), custom_call_target="tpu_custom_call" | custom-call | flops 503316480 | bytes 12582912 | tf_op jit(solution)/shard_map/pallas_call | solution.py:26
Async XLA Ops:
  18.0 2.6 %collective-permute-start = (bf16[256,384]{1,0:T(8,128)(2,1)S(1)}, bf16[256,384]{1,0:T(8,128)(2,1)S(1)}, u32[]{:S(2)}, u32[]{:S(2)}) collective-permute-start(bf16[256,384]{1,0:T(8,128)(2,1)S(1)} %bitcast.3), channel_id=1, source_target_pairs={{0,1},{1,0},{2,3},{3,2},{4,5},{5,4},{6,7},{7,6},{8,9},{9,8},{10,11... | collective-permute-start | bytes 589832 | tf_op jit(solution)/shard_map/ppermute | solution.py:469
  22.3 23.0 %copy-start = (bf16[384,4096]{1,0:T(8,128)(2,1)S(1)}, bf16[384,4096]{1,0:T(8,128)(2,1)}, u32[]{:S(2)}) copy-start(bf16[384,4096]{1,0:T(8,128)(2,1)} %stu_w.3) | copy-start | bytes 9437188
  34.9 10.3 %collective-permute-start.1 = (bf16[32,8,512]{2,1,0:T(8,128)(2,1)S(1)}, bf16[32,8,512]{2,1,0:T(8,128)(2,1)S(1)}, u32[]{:S(2)}, u32[]{:S(2)}) collective-permute-start(bf16[32,8,512]{2,1,0:T(8,128)(2,1)S(1)} %all_to_all.21.got.mine), channel_id=1, source_target_pairs={{0,1},{1,0},{2,3},{3,2},{4,5},{5,4},{6,7},{7,6},{8,9},{9,8},{10,11... | collective-permute-start | bytes 786440 | tf_op jit(solution)/shard_map/ppermute | solution.py:493
  49.2 1.8 %collective-permute-start.2 = (bf16[256,768]{1,0:T(8,128)(2,1)S(1)}, bf16[256,768]{1,0:T(8,128)(2,1)S(1)}, u32[]{:S(2)}, u32[]{:S(2)}) collective-permute-start(bf16[256,768]{1,0:T(8,128)(2,1)S(1)} %get-tuple-element.50), channel_id=1, source_target_pairs={{0,1},{1,0},{2,3},{3,2},{4,5},{5,4},{6,7},{7,6},{8,9},{9,8},{10,11... | collective-permute-start | bytes 1179656 | tf_op jit(solution)/shard_map/ppermute | solution.py:527

commit v6 on v5

--- a/solution.py
+++ b/solution.py
@@ -14,6 +14,7 @@
 GRAD_SCALE = 1.0 / 128.0
 EMPTY = 2.0
 LANES = 128
+QUAD = 4
 F32 = jnp.float32
 BF16 = jnp.bfloat16
 AXES = ("img", "proto")
@@ -64,11 +65,6 @@
     return [row[:, i : i + LANES] for i in range(0, row.shape[1], LANES)]
 
 
-def to_column(row):
-    parts = [jnp.broadcast_to(tile, (LANES, LANES)).T for tile in tiles_of(row)]
-    return jnp.concatenate(parts, axis=0)[: row.shape[1]]
-
-
 def to_row(part):
     rows = part.shape[0]
     spare = -rows % LANES
@@ -88,11 +84,24 @@
     return jnp.concatenate(groups, axis=1)
 
 
-def read_out(got, start, rows, count):
-    _, each, wide = got.shape
-    sums = jnp.sum(got[:, :, start:].astype(F32), axis=0)
-    line = jnp.concatenate([sums[i : i + 1, g : g + LANES] for g in range(0, wide - start, LANES) for i in range(each)], axis=1)
-    parts = [line[:, p * rows : (p + 1) * rows] for p in range(2 * count)]
+def read_out(sums, rows, count):
+    lines = sums.shape[0]
+    turned = [sums[:, g : g + LANES].T for g in range(0, sums.shape[1], LANES)]
+
+    def column(at, stop):
+        parts = []
+        while at < stop:
+            line, lane = divmod(at, LANES)
+            until = min(LANES, lane + stop - at)
+            parts.append(turned[line // lines][lane:until, line % lines : line % lines + 1])
+            at += until - lane
+        return jnp.concatenate(parts, axis=0)
+
+    return [jnp.broadcast_to(column(v * rows, (v + 1) * rows), (rows, LANES)) for v in range(count)]
+
+
+def read_pairs(got, start, rows, count):
+    parts = read_out(jnp.sum(got[:, :, start:].astype(F32), axis=0), rows, 2 * count)
     return [parts[2 * v] + parts[2 * v + 1] for v in range(count)]
 
 
@@ -104,8 +113,8 @@
     return jnp.concatenate([col] * (width // LANES), axis=1)
 
 
-def chunks(columns):
-    step = min(512, columns)
+def chunks(columns, step=512):
+    step = min(step, columns)
     return [slice(at, at + step) for at in range(0, columns, step)]
 
 
@@ -132,13 +141,7 @@
     return lax.rem(lax.axis_index("proto"), 2)
 
 
-def select_kernel(mask_hbm, stu_hbm, tea_hbm, sent_out, unit_out, norm_out, mask_ref, stu_ref, tea_ref, sems):
-    pairs = ((mask_hbm, mask_ref), (tea_hbm, tea_ref), (stu_hbm, stu_ref))
-    copies = [pltpu.make_async_copy(*pair, sems.at[i]) for i, pair in enumerate(pairs)]
-    for copy in copies:
-        copy.start()
-    copies[0].wait()
-    own, feat = unit_out.shape
+def own_slots(mask_ref, feats_ref, own):
     patches = mask_ref.shape[1]
     slot = iota((own, patches), 0) + lax.axis_index("proto") * own
     mask = jnp.broadcast_to(mask_ref[...].astype(F32), (own, patches))
@@ -146,21 +149,28 @@
     rank = dot(mask.astype(BF16), upto, ((1,), (0,)))
     pick = jnp.where((rank == slot.astype(F32) + 1.0) & (mask > 0.5), 1.0, 0.0).astype(BF16)
     valid = slot[:, :1].astype(F32) < rank[:, patches - 1 :]
-    for copy, source in ((copies[1], tea_ref), (copies[2], stu_ref)):
+    rows = dot(pick, feats_ref[0], ((1,), (0,)))
+    norm = jnp.sqrt(jnp.sum(rows * rows, axis=1, keepdims=True) + NORM_EPS)
+    return (rows / norm).astype(BF16).astype(F32), norm, valid
+
+
+def teacher_kernel(mask_hbm, stu_hbm, tea_hbm, sent_out, mask_out, stu_out, tea_ref, sems):
+    pairs = ((mask_hbm, mask_out), (tea_hbm, tea_ref), (stu_hbm, stu_out))
+    copies = [pltpu.make_async_copy(*pair, sems.at[i]) for i, pair in enumerate(pairs)]
+    for copy in copies:
+        copy.start()
+    for copy in copies[:2]:
         copy.wait()
-        rows = dot(pick, source[0], ((1,), (0,)))
-        norm = jnp.sqrt(jnp.sum(rows * rows, axis=1, keepdims=True) + NORM_EPS)
-        unit = (rows / norm).astype(BF16)
-        if source is tea_ref:
-            sent = jnp.where(valid, unit.astype(F32), EMPTY).astype(BF16)
-            sent_out[...] = jnp.broadcast_to(sent[None], sent_out.shape)
-        else:
-            unit_out[...] = unit.astype(F32)
-            norm_out[...] = jnp.broadcast_to(norm, norm_out.shape)
-
-
-def norms_kernel(tea_hbm, tea_w, inv_out, sems):
+    unit, _, valid = own_slots(mask_out, tea_ref, sent_out.shape[1])
+    sent_out[...] = jnp.broadcast_to(jnp.where(valid, unit, EMPTY).astype(BF16)[None], sent_out.shape)
+    copies[2].wait()
+
+
+def norms_kernel(mask_ref, stu_ref, tea_hbm, tea_w, inv_out, unit_out, norm_out, sems):
     copies = start_load(tea_hbm, tea_w, sems)
+    unit, norm, _ = own_slots(mask_ref, stu_ref, unit_out.shape[0])
+    unit_out[...] = unit
+    norm_out[...] = jnp.broadcast_to(norm, norm_out.shape)
     for copy, at in zip(copies, chunks(tea_w.shape[1])):
         copy.wait()
         inv_out[:, at] = inverse_norms(tea_w[:, at])
@@ -206,14 +216,21 @@
     return add_all(parts).astype(BF16)
 
 
+def quads(each, feat):
+    return [(row, lane) for lane in range(0, feat, LANES) for row in range(0, each, QUAD)]
+
+
 def first_kernel(mine, other, tea_w, inv, unit, kernel_out, sent_out, hot_out):
     rows = kernel_out.shape[0]
-    devices, each, wide = sent_out.shape
+    peers, _, groups, _, _ = sent_out.shape
     feat = tea_w.shape[0]
     packing([slot_flags(in_order(mine[:, :LANES], other[:, :LANES], h)) for h in range(2)], hot_out)
     x = pack_rows(hot_out, lambda a, b: mine[a:b], lambda a, b: other[a:b], mine.shape[0])
-    held = unit[...].reshape(1, 2, each, feat)
-    sent_out[:, :, :feat] = jnp.broadcast_to(held, (devices // 2, 2, each, feat)).reshape(devices, each, feat).astype(BF16)
+    each = unit.shape[0] // 2
+    for h in range(2):
+        for g, (row, lane) in enumerate(quads(each, feat)):
+            part = unit[h * each + row : h * each + row + QUAD, lane : lane + LANES]
+            sent_out[:, h, g] = jnp.broadcast_to(part[None], (peers, QUAD, LANES)).astype(BF16)
 
     def body(at, acc):
         z = dot(x, tea_w[:, at], ((1,), (0,)))
@@ -223,8 +240,12 @@
         return acc + fold(k * c)
 
     acc = over_chunks(tea_w.shape[1], body, jnp.zeros((rows, LANES), F32))
-    tiles = lay_out([to_row(acc)], each, wide - feat)
-    sent_out[:, :, feat:] = jnp.broadcast_to(tiles[None], (devices, each, wide - feat)).astype(BF16)
+    held = len(quads(each, feat))
+    tiles = lay_out([to_row(acc)], QUAD, (groups - held) * LANES)
+    for g in range(groups - held):
+        tile = tiles[:, g * LANES : (g + 1) * LANES]
+        for h in range(2):
+            sent_out[:, h, held + g] = jnp.broadcast_to(tile[None], (peers, QUAD, LANES)).astype(BF16)
 
 
 def spots(hot, sums, start, stop):
@@ -273,10 +294,12 @@
     return jnp.sum(parts, axis=0).reshape(2 * each, feat)
 
 
-def sweep_kernel(got, kernel, sent_out, *, feat):
+def sweep_kernel(got, kernel, sent_out, *, held):
     rows, columns = kernel.shape
-    (total,) = read_out(got, feat, rows, 1)
-    wide = spread(to_column(1.0 / total), chunks(columns)[0].stop)
+    sums = [jnp.sum(got[:, g].astype(F32), axis=0) for g in range(held, got.shape[1])]
+    high, low = read_out(jnp.concatenate(sums, axis=1), rows, 2)
+    total = high + low
+    wide = spread(1.0 / total, chunks(columns)[0].stop)
 
     def body(at, acc):
         k = kernel[:, at]
@@ -308,21 +331,23 @@
     rows, columns = logits_out.shape
     feat = stu_w.shape[0]
     half = keep_out.shape[0]
-    each = mine.shape[1]
+    each = half // lax.axis_size(AXES)
 
     def reader(ref):
         def read(start, stop):
-            part = ref[start // each : stop // each, :, :feat].astype(F32)
-            return part.reshape(stop - start, feat).astype(BF16)
+            peers = slice(start // each, stop // each)
+            parts = [ref[peers, g].astype(F32) for g in range(len(quads(each, feat)))]
+            deep = each // QUAD
+            lanes = [jnp.concatenate(parts[g : g + deep], axis=1) for g in range(0, len(parts), deep)]
+            return jnp.concatenate([part.reshape(stop - start, LANES) for part in lanes], axis=1).astype(BF16)
 
         return read
 
     x = pack_rows(hot, reader(mine), reader(other), half)
     xt = x.astype(F32).T
     xt_out[...] = xt.astype(BF16)
-    sums = jnp.sum(got[...], axis=0)
-    total = jnp.concatenate([sums[i : i + 1] for i in range(sums.shape[0])], axis=1)[:, :rows]
-    wide = spread(to_column(1.0 / total), chunks(columns)[0].stop)
+    (total,) = read_out(jnp.sum(got[...], axis=0), rows, 1)
+    wide = spread(1.0 / total, chunks(columns)[0].stop)
 
     def student(at, acc):
         w = stu_w[:, at]
@@ -345,7 +370,7 @@
     part = over_chunks(columns, student, zero)
     pull = dot(stu_w[...], pulls[...], ((1,), (1,)))
     total = over_chunks(columns, sweep, zero)
-    push = dot(stu_w[...], pushes[...], ((1,), (1,)))
+    push = dot(pushes[...], stu_w[...], ((1,), (1,))).T
     halves(hot, pull.astype(BF16), 0, keep_out, give_out)
     halves(hot, push.astype(BF16), feat, keep_out, give_out)
     cross = jnp.sum(push * xt, axis=0, keepdims=True) * (1.0 / STUDENT_TEMP)
@@ -397,9 +422,9 @@
 ):
     rows, columns = pull.shape
     feat = xt.shape[0]
-    partition, total, cross = read_out(got, 2 * feat, rows, 3)
-    parts = chunks(columns)
-    raise_by, lower_by = to_column(1.0 / partition), to_column(1.0 / total)
+    partition, total, cross = read_pairs(got, 2 * feat, rows, 3)
+    parts = chunks(columns, 256)
+    raise_by, lower_by = 1.0 / partition, 1.0 / total
     grow, shrink = spread(raise_by, parts[0].stop), spread(lower_by, parts[0].stop)
     copies = []
 
@@ -407,13 +432,21 @@
         copies.append(pltpu.make_async_copy(source, target, sems.at[len(copies)]))
         copies[-1].start()
 
-    for at in parts:
+    def gradient(at):
         g = grow * pull[:, at] - shrink * push[:, at]
         along = jnp.sum(g * logits[:, at], axis=0, keepdims=True) * (inv[:, at] * STUDENT_TEMP)
-        out[:, at] = dot(xt[...], g.astype(BF16), ((1,), (0,))) - stu_w[:, at].astype(F32) * along
+        return g.astype(BF16), along
+
+    ready = gradient(parts[0])
+    for at, following in zip(parts, parts[1:] + [None]):
+        g, along = ready
+        direct = dot(xt[...], g, ((1,), (0,)))
+        if following is not None:
+            ready = gradient(following)
+        out[:, at] = direct - stu_w[:, at].astype(F32) * along
         send(out.at[:, at], out_hbm.at[:, at])
     share = weight[...]
-    loss = jnp.sum(share * to_column(jnp.log(partition) - cross / total), axis=0, keepdims=True)
+    loss = jnp.sum(share * (jnp.log(partition) - cross * lower_by), axis=0, keepdims=True)
     loss_out[...] = loss[:, :1]
     send(loss_out, loss_hbm)
     factors = jnp.concatenate([raise_by, lower_by], axis=1) * spread(share * (rows / STUDENT_TEMP), 2 * LANES)
@@ -439,6 +472,7 @@
     rows = 2 * half * 5 // 16
     tiles = -(-rows // LANES)
     extra = lambda parts: LANES * -(-parts * rows // (each * LANES))
+    held = len(quads(each, feat))
     big = rows * columns
     exchange = functools.partial(lax.all_to_all, axis_name=AXES, split_axis=0, concat_axis=0)
     swap = functools.partial(lax.ppermute, axis_name="proto", perm=[(p, p ^ 1) for p in range(protos)])
@@ -446,40 +480,44 @@
     column = pltpu.VMEM((rows, LANES), F32)
     line = pltpu.VMEM((1, columns), F32)
 
-    sent, unit, norm = call(
-        select_kernel,
-        (
-            pltpu.VMEM((devices // 2, own, feat), BF16),
-            pltpu.VMEM((own, feat), F32),
-            pltpu.VMEM((own, LANES), F32),
-        ),
+    flags = pltpu.VMEM(patch_masks.shape, patch_masks.dtype)
+    feats = pltpu.VMEM(student_feats.shape, BF16)
+    sent, flags, feats = call(
+        teacher_kernel,
+        (pltpu.VMEM((devices // 2, own, feat), BF16), flags, feats),
         far(patch_masks),
         far(student_feats),
         far(teacher_feats),
         specs=[HBM] * 3,
-        scratch=[
-            pltpu.VMEM(patch_masks.shape, patch_masks.dtype),
-            pltpu.VMEM(student_feats.shape, BF16),
-            pltpu.VMEM(teacher_feats.shape, BF16),
-            pltpu.SemaphoreType.DMA((3,)),
-        ],
+        scratch=[feats, pltpu.SemaphoreType.DMA((3,))],
     )
     mine = exchange(sent.reshape(devices, each, feat)).reshape(half, feat)
     mine, teacher_weight = lax.optimization_barrier((mine, teacher_weight))
     other = near(swap(mine))
     mine = near(mine)
-    tea_w, tea_inv = call(
+    tea_w, tea_inv, unit, norm = call(
         norms_kernel,
-        (pltpu.VMEM(teacher_weight.shape, BF16), line),
+        (
+            pltpu.VMEM(teacher_weight.shape, BF16),
+            line,
+            pltpu.VMEM((own, feat), F32),
+            pltpu.VMEM((own, LANES), F32),
+        ),
+        flags,
+        feats,
         far(teacher_weight),
         flops=2 * feat * columns,
         moved=4 * feat * columns,
-        specs=[HBM],
+        specs=[VMEM, VMEM, HBM],
         scratch=[pltpu.SemaphoreType.DMA((len(chunks(columns)),))],
     )
     kernel, sent, hot = call(
         first_kernel,
-        (matrix, pltpu.VMEM((devices, each, feat + extra(2)), BF16), pltpu.VMEM((rows, 2 * half), BF16)),
+        (
+            matrix,
+            pltpu.VMEM((devices // 2, 2, held + -(-2 * rows // (QUAD * LANES)), QUAD, LANES), BF16),
+            pltpu.VMEM((rows, 2 * half), BF16),
+        ),
         mine,
         other,
         tea_w,
@@ -489,11 +527,11 @@
         moved=4 * big,
         exps=big,
     )
-    stu_mine = exchange(sent)
+    stu_mine = exchange(sent.reshape(devices, *sent.shape[2:]))
     stu_other = near(swap(stu_mine))
     stu_mine = near(stu_mine)
     (sent,) = call(
-        functools.partial(sweep_kernel, feat=feat),
+        functools.partial(sweep_kernel, held=held),
         (pltpu.VMEM((devices, tiles, LANES), F32),),
         stu_mine,
         kernel,
@@ -566,7 +604,7 @@
             pltpu.VMEM((feat, columns), F32),
             pltpu.VMEM((own, feat), F32),
             pltpu.VMEM((1, 1), F32),
-            pltpu.SemaphoreType.DMA((len(chunks(columns)) + 2,)),
+            pltpu.SemaphoreType.DMA((len(chunks(columns, 256)) + 2,)),
         ],
     )
     return loss.reshape(()), grad_weight, grad_rows

time: 71 us -> 70 us (0.986)
  blocking collectives: 54.3 us -> 53.4 us
    all_to_all x1, blocking collectives: 12.6 us -> 11.9 us  [shards(): stu_mine = exchange(sent.reshape(devices, *sent.shape[2:]))]
where the time goes in v6:
time: 70 us; the launch traced here: 69.8 us
  blocking collectives  53.4 us (76%)
  Pallas kernels  14.2 us (20%)
  starting transfers between devices  0.95 us (1%)
    all_to_all x2, blocking collectives, shards(): got = near(exchange(sent))  25.6 us
    all_to_all x1, blocking collectives, shards(): mine = exchange(sent.reshape(devices, each, feat)).reshape(half, feat)  16 us
    pallas_call x8, Pallas kernels, call(): pl.pallas_call(body, out_shape=outs, in_specs=specs or [VMEM] * len(args)...  14.2 us
    all_to_all x1, blocking collectives, shards(): stu_mine = exchange(sent.reshape(devices, *sent.shape[2:]))  11.9 us
  transfers between devices with their start and end apart: 3, of which 1 were waited for; matrix products, arithmetic and copies ran while one was open for 0% of the time, Pallas kernels for 5%

profile of v6, /device:TPU:0, one launch (start us, length us, event | category | flops | bytes accessed | tf_op | source)
XLA Modules:
  0.0 69.8 jit_solution(3409319909116067661)
XLA Ops:
  0.6 1.3 %shard_map.76 = (bf16[16,16,384]{2,1,0:T(8,128)(2,1)S(1)}, s32[1,128]{1,0:T(1,128)S(1)}, bf16[1,128,384]{2,1,0:T(8,128)(2,1)S(1)}) custom-call(s32[1,128]{1,0:T(1,128)} %mask_hbm.1, bf16[1,128,384]{2,1,0:T(8,128)(2,1)} %stu_hbm.1, bf16[1,128,384]{2,1,0:T(8,128)(2,1)} %tea_hbm.1), custom_call_target="tpu_custom_call" | custom-call | tf_op jit(solution)/shard_map/pallas_call | solution.py:27
  1.9 16.0 %all_to_all.20 = bf16[32,8,384]{2,1,0:T(8,128)(2,1)S(1)} all-to-all(bf16[32,8,384]{2,1,0:T(8,128)(2,1)S(1)} %bitcast.8), channel_id=1, replica_groups=mesh['img'=8,'proto'=4] {'img','proto'}, dimensions={0} | all-to-all | bytes 393216 | tf_op jit(solution)/shard_map/all_to_all | solution.py:494
  17.9 0.6 collective-permute-start
  18.5 2.0 %shard_map.77 = (bf16[384,4096]{1,0:T(8,128)(2,1)S(1)}, f32[1,4096]{1,0:T(1,128)S(1)}, f32[16,384]{1,0:T(8,128)S(1)}, f32[16,128]{1,0:T(8,128)S(1)}) custom-call(s32[1,128]{1,0:T(1,128)S(1)} %get-tuple-element.36.mask_ref, bf16[1,128,384]{2,1,0:T(8,128)(2,1)S(1)} %get-tuple-element.37.stu_ref, bf16[384,4096]{1,0:T(8,128)(2,1)} %tea_hbm.2), custom_call_target="tpu_custom_call" | custom-call | flops 3145728 | bytes 6291456 | tf_op jit(solution)/shard_map/pallas_call | solution.py:27
  20.5 0.0 collective-permute-done.other
  20.5 0.0 copy-start
  20.5 1.6 %shard_map.78 = (f32[160,4096]{1,0:T(8,128)S(1)}, bf16[16,2,7,4,128]{4,3,2,1,0:T(4,128)(2,1)S(1)}, bf16[160,512]{1,0:T(8,128)(2,1)S(1)}) custom-call(bf16[256,384]{1,0:T(8,128)(2,1)S(1)} %bitcast.5, bf16[256,384]{1,0:T(8,128)(2,1)S(1)} %collective-permute-done.other, bf16[384,4096]{1,0:T(8,128)(2,1)S(1)} %get-tuple-element.39.tea_w, ...), custom_call_target="tpu_custom_call" | custom-call | flops 503316480 | bytes 2621440 | tf_op jit(solution)/shard_map/pallas_call | solution.py:27
  22.2 11.9 %all_to_all.21.got.mine = bf16[32,7,4,128]{3,2,1,0:T(4,128)(2,1)S(1)} all-to-all(bf16[32,7,4,128]{3,2,1,0:T(4,128)(2,1)S(1)} %bitcast.7), channel_id=1, replica_groups=mesh['img'=8,'proto'=4] {'img','proto'}, dimensions={0} | all-to-all | bytes 458752 | tf_op jit(solution)/shard_map/all_to_all | solution.py:530
  34.0 0.2 collective-permute-start.1
  34.2 0.7 %shard_map.79 = f32[32,2,128]{2,1,0:T(2,128)S(1)} custom-call(bf16[32,7,4,128]{3,2,1,0:T(4,128)(2,1)S(1)} %all_to_all.21.got.mine, f32[160,4096]{1,0:T(8,128)S(1)} %get-tuple-element.43.kernel), custom_call_target="tpu_custom_call" | custom-call | flops 2621440 | bytes 2621440 | tf_op jit(solution)/shard_map/pallas_call | solution.py:27
  35.0 9.5 %all_to_all.22.got = f32[32,2,128]{2,1,0:T(2,128)S(1)} all-to-all(f32[32,2,128]{2,1,0:T(2,128)S(1)} %shard_map.79), channel_id=1, replica_groups=mesh['img'=8,'proto'=4] {'img','proto'}, dimensions={0} | all-to-all | bytes 65536 | tf_op jit(solution)/shard_map/all_to_all | solution.py:541
  44.4 0.0 collective-permute-done.1.other
  44.4 0.0 copy-done
  44.4 3.9 %shard_map.80 = (f32[1,4096]{1,0:T(1,128)S(1)}, f32[160,4096]{1,0:T(8,128)S(1)}, f32[160,4096]{1,0:T(8,128)S(1)}, bf16[384,160]{1,0:T(8,128)(2,1)S(1)}, f32[8,12...) custom-call(f32[32,2,128]{2,1,0:T(2,128)S(1)} %all_to_all.22.got, ...), custom_call_target="tpu_custom_call" | custom-call | flops 1509949440 | bytes 7864320 | tf_op jit(solution)/shard_map/pallas_call | solution.py:27
  48.3 0.2 collective-permute-start.2
  48.5 1.1 %shard_map.81 = (f32[160,4096]{1,0:T(8,128)S(1)}, f32[160,4096]{1,0:T(8,128)S(1)}, f32[16,160]{1,0:T(8,128)S(1)}, f32[160,128]{1,0:T(8,128)S(1)}) custom-call(f32[160,4096]{1,0:T(8,128)S(1)} %get-tuple-element.46.scaled, f32[160,4096]{1,0:T(8,128)S(1)} %get-tuple-element.47.logits, f32[1,4096]{1,0:T(1,128)S(1)} %get-tuple-element.48.inv, ...), custom_call_target="tpu_custom_call" | custom-call | flops 2621440 | bytes 10485760 | tf_op jit(solution)/shard_map/pallas_call | solution.py:27
  49.6 0.5 collective-permute-done.2.give
  50.1 0.1 shard_map.82
  50.2 16.1 %all_to_all.23.got = bf16[32,8,896]{2,1,0:T(8,128)(2,1)S(1)} all-to-all(bf16[32,8,896]{2,1,0:T(8,128)(2,1)S(1)} %shard_map.82), channel_id=1, replica_groups=mesh['img'=8,'proto'=4] {'img','proto'}, dimensions={0} | all-to-all | bytes 917504 | tf_op jit(solution)/shard_map/all_to_all | solution.py:581
  66.3 3.5 %shard_map.83 = (f32[384,4096]{1,0:T(8,128)}, f32[16,384]{1,0:T(8,128)}, f32[1,1]{1,0:T(1,128)}) custom-call(bf16[32,8,896]{2,1,0:T(8,128)(2,1)S(1)} %all_to_all.23.got, f32[160,4096]{1,0:T(8,128)S(1)} %get-tuple-element.56.pull, f32[160,4096]{1,0:T(8,128)S(1)} %get-tuple-element.57.push, f32[160,4096]{1,0:T(8,128)S(1)} %get-tuple-element.47.logits, ...), custom_call_target="tpu_custom_call" | custom-call | flops 503316480 | bytes 12582912 | tf_op jit(solution)/shard_map/pallas_call | solution.py:27
Async XLA Ops:
  17.9 2.6 %collective-permute-start = (bf16[256,384]{1,0:T(8,128)(2,1)S(1)}, bf16[256,384]{1,0:T(8,128)(2,1)S(1)}, u32[]{:S(2)}, u32[]{:S(2)}) collective-permute-start(bf16[256,384]{1,0:T(8,128)(2,1)S(1)} %bitcast.4), channel_id=1, source_target_pairs={{0,1},{1,0},{2,3},{3,2},{4,5},{5,4},{6,7},{7,6},{8,9},{9,8},{10,11... | collective-permute-start | bytes 589832 | tf_op jit(solution)/shard_map/ppermute | solution.py:496
  20.5 23.9 %copy-start = (bf16[384,4096]{1,0:T(8,128)(2,1)S(1)}, bf16[384,4096]{1,0:T(8,128)(2,1)}, u32[]{:S(2)}) copy-start(bf16[384,4096]{1,0:T(8,128)(2,1)} %stu_w.3) | copy-start | bytes 9437188
  34.0 10.4 %collective-permute-start.1 = (bf16[32,7,4,128]{3,2,1,0:T(4,128)(2,1)S(1)}, bf16[32,7,4,128]{3,2,1,0:T(4,128)(2,1)S(1)}, u32[]{:S(2)}, u32[]{:S(2)}) collective-permute-start(bf16[32,7,4,128]{3,2,1,0:T(4,128)(2,1)S(1)} %all_to_all.21.got.mine), channel_id=1, source_target_pairs={{0,1},{1,0},{2,3},{3,2},{4,5},{5,4},{6,7},{7,6},{8,9},{9,8},{10,11... | collective-permute-start | bytes 688136 | tf_op jit(solution)/shard_map/ppermute | solution.py:531
  48.3 1.8 %collective-permute-start.2 = (bf16[256,768]{1,0:T(8,128)(2,1)S(1)}, bf16[256,768]{1,0:T(8,128)(2,1)S(1)}, u32[]{:S(2)}, u32[]{:S(2)}) collective-permute-start(bf16[256,768]{1,0:T(8,128)(2,1)S(1)} %get-tuple-element.54), channel_id=1, source_target_pairs={{0,1},{1,0},{2,3},{3,2},{4,5},{5,4},{6,7},{7,6},{8,9},{9,8},{10,11... | collective-permute-start | bytes 1179656 | tf_op jit(solution)/shard_map/ppermute | solution.py:565

commit v7 on v6

--- a/solution.py
+++ b/solution.py
@@ -73,14 +73,15 @@
     return jnp.sum(part.T, axis=0, keepdims=True)[:, :rows]
 
 
-def lay_out(vectors, each, wide):
-    parts = []
-    for vector in vectors:
-        high = vector.astype(BF16).astype(F32)
-        parts += [high, vector - high]
-    tiles = tiles_of(jnp.concatenate(parts, axis=1))
-    tiles += [jnp.zeros((1, LANES), F32)] * (each * wide // LANES - len(tiles))
-    groups = [jnp.concatenate(tiles[g : g + each], axis=0) for g in range(0, len(tiles), each)]
+def split(vector):
+    high = vector.astype(BF16).astype(F32)
+    return [high, vector - high]
+
+
+def lay_out(vectors, lines, wide):
+    tiles = tiles_of(jnp.concatenate(vectors, axis=1))
+    tiles += [jnp.zeros((1, LANES), F32)] * (lines * wide // LANES - len(tiles))
+    groups = [jnp.concatenate(tiles[g : g + lines], axis=0) for g in range(0, len(tiles), lines)]
     return jnp.concatenate(groups, axis=1)
 
 
@@ -100,11 +101,6 @@
     return [jnp.broadcast_to(column(v * rows, (v + 1) * rows), (rows, LANES)) for v in range(count)]
 
 
-def read_pairs(got, start, rows, count):
-    parts = read_out(jnp.sum(got[:, :, start:].astype(F32), axis=0), rows, 2 * count)
-    return [parts[2 * v] + parts[2 * v + 1] for v in range(count)]
-
-
 def fold(x):
     return add_all([x[:, i : i + LANES] for i in range(0, x.shape[1], LANES)])
 
@@ -124,9 +120,11 @@
     return start
 
 
-def start_load(source, target, sems):
-    parts = chunks(target.shape[1])
-    copies = [pltpu.make_async_copy(source.at[:, at], target.at[:, at], sems.at[i]) for i, at in enumerate(parts)]
+def start_load(source, target, sems, first=0):
+    copies = []
+    for i, at in enumerate(chunks(target.shape[1])):
+        place = source.at[:, first + at.start : first + at.stop]
+        copies.append(pltpu.make_async_copy(place, target.at[:, at], sems.at[i]))
     for copy in copies:
         copy.start()
     return copies
@@ -154,26 +152,31 @@
     return (rows / norm).astype(BF16).astype(F32), norm, valid
 
 
-def teacher_kernel(mask_hbm, stu_hbm, tea_hbm, sent_out, mask_out, stu_out, tea_ref, sems):
+def teacher_kernel(mask_hbm, stu_hbm, tea_hbm, w_hbm, sent_out, mask_out, stu_out, early_w, tea_ref, sems, w_sems):
     pairs = ((mask_hbm, mask_out), (tea_hbm, tea_ref), (stu_hbm, stu_out))
     copies = [pltpu.make_async_copy(*pair, sems.at[i]) for i, pair in enumerate(pairs)]
     for copy in copies:
         copy.start()
+    loads = start_load(w_hbm, early_w, w_sems)
     for copy in copies[:2]:
         copy.wait()
     unit, _, valid = own_slots(mask_out, tea_ref, sent_out.shape[1])
     sent_out[...] = jnp.broadcast_to(jnp.where(valid, unit, EMPTY).astype(BF16)[None], sent_out.shape)
-    copies[2].wait()
-
-
-def norms_kernel(mask_ref, stu_ref, tea_hbm, tea_w, inv_out, unit_out, norm_out, sems):
-    copies = start_load(tea_hbm, tea_w, sems)
+    for copy in copies[2:] + loads:
+        copy.wait()
+
+
+def norms_kernel(mask_ref, stu_ref, early_w, w_hbm, late_w, inv_out, unit_out, norm_out, sems):
+    early = early_w.shape[1]
+    copies = start_load(w_hbm, late_w, sems, early)
     unit, norm, _ = own_slots(mask_ref, stu_ref, unit_out.shape[0])
     unit_out[...] = unit
     norm_out[...] = jnp.broadcast_to(norm, norm_out.shape)
-    for copy, at in zip(copies, chunks(tea_w.shape[1])):
+    for at in chunks(early):
+        inv_out[:, at] = inverse_norms(early_w[:, at])
+    for copy, at in zip(copies, chunks(late_w.shape[1])):
         copy.wait()
-        inv_out[:, at] = inverse_norms(tea_w[:, at])
+        inv_out[:, early + at.start : early + at.stop] = inverse_norms(late_w[:, at])
 
 
 def in_order(mine, other, h):
@@ -220,10 +223,10 @@
     return [(row, lane) for lane in range(0, feat, LANES) for row in range(0, each, QUAD)]
 
 
-def first_kernel(mine, other, tea_w, inv, unit, kernel_out, sent_out, hot_out):
+def first_kernel(mine, other, early_w, late_w, inv, unit, kernel_out, sent_out, hot_out):
     rows = kernel_out.shape[0]
     peers, _, groups, _, _ = sent_out.shape
-    feat = tea_w.shape[0]
+    feat = late_w.shape[0]
     packing([slot_flags(in_order(mine[:, :LANES], other[:, :LANES], h)) for h in range(2)], hot_out)
     x = pack_rows(hot_out, lambda a, b: mine[a:b], lambda a, b: other[a:b], mine.shape[0])
     each = unit.shape[0] // 2
@@ -232,16 +235,17 @@
             part = unit[h * each + row : h * each + row + QUAD, lane : lane + LANES]
             sent_out[:, h, g] = jnp.broadcast_to(part[None], (peers, QUAD, LANES)).astype(BF16)
 
-    def body(at, acc):
-        z = dot(x, tea_w[:, at], ((1,), (0,)))
-        k = jnp.exp(z * (inv[:, at] * (1.0 / TEACHER_TEMP)))
-        kernel_out[:, at] = k
-        c = 1.0 / jnp.sum(k, axis=0, keepdims=True)
-        return acc + fold(k * c)
-
-    acc = over_chunks(tea_w.shape[1], body, jnp.zeros((rows, LANES), F32))
+    acc = jnp.zeros((rows, LANES), F32)
+    for w, first in ((early_w, 0), (late_w, early_w.shape[1])):
+        for part in chunks(w.shape[1]):
+            at = slice(first + part.start, first + part.stop)
+            z = dot(x, w[:, part], ((1,), (0,)))
+            k = jnp.exp(z * (inv[:, at] * (1.0 / TEACHER_TEMP)))
+            kernel_out[:, at] = k
+            c = 1.0 / jnp.sum(k, axis=0, keepdims=True)
+            acc = acc + fold(k * c)
     held = len(quads(each, feat))
-    tiles = lay_out([to_row(acc)], QUAD, (groups - held) * LANES)
+    tiles = lay_out(split(to_row(acc)), QUAD, (groups - held) * LANES)
     for g in range(groups - held):
         tile = tiles[:, g * LANES : (g + 1) * LANES]
         for h in range(2):
@@ -286,12 +290,6 @@
     spot = q // each * half + me * each + q % each
     mark = (iota((own, 2 * half), 1) == spot).astype(BF16)
     own_out[...] = dot(mark, hot[...], ((1,), (1,)))
-
-
-def slots_of(got, feat):
-    devices, each, _ = got.shape
-    parts = got[:, :, :feat].astype(F32).reshape(devices // 2, 2, each, feat)
-    return jnp.sum(parts, axis=0).reshape(2 * each, feat)
 
 
 def sweep_kernel(got, kernel, sent_out, *, held):
@@ -394,10 +392,26 @@
 
 
 def fill_kernel(keep, give, sums, sent_out):
-    devices, each, wide = sent_out.shape
-    both = keep.shape[1]
-    sent_out[:, :, :both] = (keep[...] + give[...].astype(F32)).reshape(devices, each, both).astype(BF16)
-    sent_out[:, :, both:] = jnp.broadcast_to(sums[...][None], (devices, each, wide - both)).astype(BF16)
+    devices, groups, _, _ = sent_out.shape
+    half, both = keep.shape
+    each = half // devices
+    pair = keep[...] + give[...].astype(F32)
+    places = quads(each, both)
+    for g, (row, lane) in enumerate(places):
+        part = pair[:, lane : lane + LANES].reshape(devices, each, LANES)
+        sent_out[:, g] = part[:, row : row + QUAD].astype(BF16)
+    for g in range(len(places), groups):
+        at = (g - len(places)) * LANES
+        sent_out[:, g] = jnp.broadcast_to(sums[:, at : at + LANES][None], (devices, QUAD, LANES)).astype(BF16)
+
+
+def slots_of(got, each, both):
+    sums = [jnp.sum(got[:, :, g].astype(F32), axis=0) for g in range(len(quads(each, both)))]
+    deep = each // QUAD
+    lanes = [
+        jnp.concatenate([sums[g + i][h] for h in range(2) for i in range(deep)], axis=0) for g in range(0, len(sums), deep)
+    ]
+    return jnp.concatenate(lanes, axis=1)
 
 
 def final_kernel(
@@ -422,7 +436,10 @@
 ):
     rows, columns = pull.shape
     feat = xt.shape[0]
-    partition, total, cross = read_pairs(got, 2 * feat, rows, 3)
+    each = unit.shape[0] // 2
+    held = len(quads(each, 2 * feat))
+    sums = [jnp.sum(got[:, :, g].astype(F32), axis=(0, 1)) for g in range(held, got.shape[2])]
+    partition, total, cross = read_out(jnp.concatenate(sums, axis=1), rows, 3)
     parts = chunks(columns, 256)
     raise_by, lower_by = 1.0 / partition, 1.0 / total
     grow, shrink = spread(raise_by, parts[0].stop), spread(lower_by, parts[0].stop)
@@ -450,9 +467,9 @@
     loss_out[...] = loss[:, :1]
     send(loss_out, loss_hbm)
     factors = jnp.concatenate([raise_by, lower_by], axis=1) * spread(share * (rows / STUDENT_TEMP), 2 * LANES)
-    held = dot(own[...], factors, ((1,), (0,)), lax.Precision.HIGHEST)
-    sums = slots_of(got, 2 * feat)
-    full = sums[:, :feat] * held[:, :1] - sums[:, feat:] * held[:, LANES : LANES + 1]
+    scale = dot(own[...], factors, ((1,), (0,)), lax.Precision.HIGHEST)
+    sums = slots_of(got, each, 2 * feat)
+    full = sums[:, :feat] * scale[:, :1] - sums[:, feat:] * scale[:, LANES : LANES + 1]
     u = unit[...]
     rows_out[...] = (full - u * jnp.sum(u * full, axis=1, keepdims=True)) / norm[:, :1]
     send(rows_out, rows_hbm)
@@ -471,7 +488,7 @@
     half = each * devices
     rows = 2 * half * 5 // 16
     tiles = -(-rows // LANES)
-    extra = lambda parts: LANES * -(-parts * rows // (each * LANES))
+    spare = lambda parts: -(-parts * rows // (QUAD * LANES))
     held = len(quads(each, feat))
     big = rows * columns
     exchange = functools.partial(lax.all_to_all, axis_name=AXES, split_axis=0, concat_axis=0)
@@ -482,45 +499,50 @@
 
     flags = pltpu.VMEM(patch_masks.shape, patch_masks.dtype)
     feats = pltpu.VMEM(student_feats.shape, BF16)
-    sent, flags, feats = call(
+    early = columns * 3 // 8 // LANES * LANES
+    early_w, late_w = pltpu.VMEM((feat, early), BF16), pltpu.VMEM((feat, columns - early), BF16)
+    sent, flags, feats, early_w = call(
         teacher_kernel,
-        (pltpu.VMEM((devices // 2, own, feat), BF16), flags, feats),
+        (pltpu.VMEM((devices // 2, own, feat), BF16), flags, feats, early_w),
         far(patch_masks),
         far(student_feats),
         far(teacher_feats),
-        specs=[HBM] * 3,
-        scratch=[feats, pltpu.SemaphoreType.DMA((3,))],
+        far(teacher_weight),
+        specs=[HBM] * 4,
+        scratch=[feats, pltpu.SemaphoreType.DMA((3,)), pltpu.SemaphoreType.DMA((len(chunks(early)),))],
     )
     mine = exchange(sent.reshape(devices, each, feat)).reshape(half, feat)
     mine, teacher_weight = lax.optimization_barrier((mine, teacher_weight))
     other = near(swap(mine))
     mine = near(mine)
-    tea_w, tea_inv, unit, norm = call(
+    late_w, tea_inv, unit, norm = call(
         norms_kernel,
         (
-            pltpu.VMEM(teacher_weight.shape, BF16),
+            late_w,
             line,
             pltpu.VMEM((own, feat), F32),
             pltpu.VMEM((own, LANES), F32),
         ),
         flags,
         feats,
+        early_w,
         far(teacher_weight),
         flops=2 * feat * columns,
         moved=4 * feat * columns,
-        specs=[VMEM, VMEM, HBM],
-        scratch=[pltpu.SemaphoreType.DMA((len(chunks(columns)),))],
+        specs=[VMEM, VMEM, VMEM, HBM],
+        scratch=[pltpu.SemaphoreType.DMA((len(chunks(columns - early)),))],
     )
     kernel, sent, hot = call(
         first_kernel,
         (
             matrix,
-            pltpu.VMEM((devices // 2, 2, held + -(-2 * rows // (QUAD * LANES)), QUAD, LANES), BF16),
+            pltpu.VMEM((devices // 2, 2, held + spare(2), QUAD, LANES), BF16),
             pltpu.VMEM((rows, 2 * half), BF16),
         ),
         mine,
         other,
-        tea_w,
+        early_w,
+        late_w,
         tea_inv,
         unit,
         flops=2 * big * feat,
@@ -546,7 +568,7 @@
             matrix,
             matrix,
             pltpu.VMEM((feat, rows), BF16),
-            pltpu.VMEM((each, extra(6)), F32),
+            pltpu.VMEM((QUAD, spare(3) * LANES), F32),
             pltpu.VMEM((half, 2 * feat), F32),
             pltpu.VMEM((half, 2 * feat), BF16),
         ),
@@ -577,8 +599,10 @@
         exps=big,
     )
     keep, pull, push, own_hot, weight = lax.optimization_barrier((keep, pull, push, own_hot, weight))
-    (sent,) = call(fill_kernel, (pltpu.VMEM((devices, each, 2 * feat + extra(6)), BF16),), keep, give, sums)
-    got = near(exchange(sent))
+    payload = pltpu.VMEM((devices, 2 * held + spare(3), QUAD, LANES), BF16)
+    (sent,) = call(fill_kernel, (payload,), keep, give, sums)
+    got = exchange(sent)
+    got = near(got.reshape(devices // 2, 2, *got.shape[1:]))
     grad_weight, grad_rows, loss = call(
         final_kernel,
         (

time: 70 us -> 69.1 us (0.987)
    all_to_all x2 -> x1, blocking collectives: 25.6 us -> 9.48 us  [shards(): got = near(exchange(sent))]
    all_to_all x0 -> x1, blocking collectives: none -> 15.5 us  [shards(): got = exchange(sent)]
where the time goes in v7:
time: 69.1 us; the launch traced here: 68.8 us
  blocking collectives  52.8 us (76%)
  Pallas kernels  13.9 us (20%)
  starting transfers between devices  0.95 us (1%)
  between operations  0.7 us (1%)
    all_to_all x1, blocking collectives, shards(): mine = exchange(sent.reshape(devices, each, feat)).reshape(half, feat)  16 us
    all_to_all x1, blocking collectives, shards(): got = exchange(sent)  15.5 us
    pallas_call x8, Pallas kernels, call(): pl.pallas_call(body, out_shape=outs, in_specs=specs or [VMEM] * len(args)...  13.9 us
    all_to_all x1, blocking collectives, shards(): stu_mine = exchange(sent.reshape(devices, *sent.shape[2:]))  11.9 us
    all_to_all x1, blocking collectives, shards(): got = near(exchange(sent))  9.48 us
  transfers between devices with their start and end apart: 3, of which 1 were waited for; matrix products, arithmetic and copies ran while one was open for 0% of the time, Pallas kernels for 5%

profile of v7, /device:TPU:0, one launch (start us, length us, event | category | flops | bytes accessed | tf_op | source)
XLA Modules:
  0.0 68.8 jit_solution(5016398594885939227)
XLA Ops:
  0.6 1.5 %shard_map.76 = (bf16[16,16,384]{2,1,0:T(8,128)(2,1)S(1)}, s32[1,128]{1,0:T(1,128)S(1)}, bf16[1,128,384]{2,1,0:T(8,128)(2,1)S(1)}, bf16[384,1536]{1,0:T(8,128)(2,1)S(1)}) custom-call(s32[1,128]{1,0:T(1,128)} %mask_hbm.1, bf16[1,128,384]{2,1,0:T(8,128)(2,1)} %stu_hbm.1, bf16[1,128,384]{2,1,0:T(8,128)(2,1)} %tea_hbm.1, bf16[384,4096]{1,0:T(8,128)(2,1)} %w_hbm.2), custom_call_target="tpu_custom_call" | custom-call | tf_op jit(solution)/shard_map/pallas_call | solution.py:27
  2.1 16.0 %all_to_all.20 = bf16[32,8,384]{2,1,0:T(8,128)(2,1)S(1)} all-to-all(bf16[32,8,384]{2,1,0:T(8,128)(2,1)S(1)} %bitcast.10), channel_id=1, replica_groups=mesh['img'=8,'proto'=4] {'img','proto'}, dimensions={0} | all-to-all | bytes 393216 | tf_op jit(solution)/shard_map/all_to_all | solution.py:514
  18.1 0.6 collective-permute-start
  18.7 1.6 %shard_map.77 = (bf16[384,2560]{1,0:T(8,128)(2,1)S(1)}, f32[1,4096]{1,0:T(1,128)S(1)}, f32[16,384]{1,0:T(8,128)S(1)}, f32[16,128]{1,0:T(8,128)S(1)}) custom-call(s32[1,128]{1,0:T(1,128)S(1)} %get-tuple-element.38.mask_ref, bf16[1,128,384]{2,1,0:T(8,128)(2,1)S(1)} %get-tuple-element.39.stu_ref, bf16[384,1536]{1,0:T(8,128)(2,1)S(1)} %get-tuple-element.37.early_w, ...), custom_call_target="tpu_custom_call" | custom-call | flops 3145728 | bytes 6291456 | tf_op jit(solution)/shard_map/pallas_call | solution.py:27
  20.3 0.0 collective-permute-done.other
  20.3 0.0 copy-start
  20.3 1.6 %shard_map.78 = (f32[160,4096]{1,0:T(8,128)S(1)}, bf16[16,2,7,4,128]{4,3,2,1,0:T(4,128)(2,1)S(1)}, bf16[160,512]{1,0:T(8,128)(2,1)S(1)}) custom-call(bf16[256,384]{1,0:T(8,128)(2,1)S(1)} %bitcast.6, bf16[256,384]{1,0:T(8,128)(2,1)S(1)} %collective-permute-done.other, bf16[384,1536]{1,0:T(8,128)(2,1)S(1)} %get-tuple-element.37.early_w, ...), custom_call_target="tpu_custom_call" | custom-call | flops 503316480 | bytes 2621440 | tf_op jit(solution)/shard_map/pallas_call | solution.py:27
  21.9 11.9 %all_to_all.21.got.mine = bf16[32,7,4,128]{3,2,1,0:T(4,128)(2,1)S(1)} all-to-all(bf16[32,7,4,128]{3,2,1,0:T(4,128)(2,1)S(1)} %bitcast.9), channel_id=1, replica_groups=mesh['img'=8,'proto'=4] {'img','proto'}, dimensions={0} | all-to-all | bytes 458752 | tf_op jit(solution)/shard_map/all_to_all | solution.py:552
  33.7 0.2 collective-permute-start.1
  33.9 0.7 %shard_map.79 = f32[32,2,128]{2,1,0:T(2,128)S(1)} custom-call(bf16[32,7,4,128]{3,2,1,0:T(4,128)(2,1)S(1)} %all_to_all.21.got.mine, f32[160,4096]{1,0:T(8,128)S(1)} %get-tuple-element.45.kernel), custom_call_target="tpu_custom_call" | custom-call | flops 2621440 | bytes 2621440 | tf_op jit(solution)/shard_map/pallas_call | solution.py:27
  34.6 9.5 %all_to_all.22.got = f32[32,2,128]{2,1,0:T(2,128)S(1)} all-to-all(f32[32,2,128]{2,1,0:T(2,128)S(1)} %shard_map.79), channel_id=1, replica_groups=mesh['img'=8,'proto'=4] {'img','proto'}, dimensions={0} | all-to-all | bytes 65536 | tf_op jit(solution)/shard_map/all_to_all | solution.py:563
  44.1 0.0 collective-permute-done.1.other
  44.1 0.0 copy-done
  44.1 3.8 %shard_map.80 = (f32[1,4096]{1,0:T(1,128)S(1)}, f32[160,4096]{1,0:T(8,128)S(1)}, f32[160,4096]{1,0:T(8,128)S(1)}, bf16[384,160]{1,0:T(8,128)(2,1)S(1)}, f32[4,12...) custom-call(f32[32,2,128]{2,1,0:T(2,128)S(1)} %all_to_all.22.got, ...), custom_call_target="tpu_custom_call" | custom-call | flops 1509949440 | bytes 7864320 | tf_op jit(solution)/shard_map/pallas_call | solution.py:27
  48.0 0.2 collective-permute-start.2
  48.1 1.1 %shard_map.81 = (f32[160,4096]{1,0:T(8,128)S(1)}, f32[160,4096]{1,0:T(8,128)S(1)}, f32[16,160]{1,0:T(8,128)S(1)}, f32[160,128]{1,0:T(8,128)S(1)}) custom-call(f32[160,4096]{1,0:T(8,128)S(1)} %get-tuple-element.48.scaled, f32[160,4096]{1,0:T(8,128)S(1)} %get-tuple-element.49.logits, f32[1,4096]{1,0:T(1,128)S(1)} %get-tuple-element.50.inv, ...), custom_call_target="tpu_custom_call" | custom-call | flops 2621440 | bytes 10485760 | tf_op jit(solution)/shard_map/pallas_call | solution.py:27
  49.3 0.5 collective-permute-done.2.give
  49.8 0.2 shard_map.82
  49.9 15.5 %all_to_all.23 = bf16[32,13,4,128]{3,2,1,0:T(4,128)(2,1)S(1)} all-to-all(bf16[32,13,4,128]{3,2,1,0:T(4,128)(2,1)S(1)} %shard_map.82), channel_id=1, replica_groups=mesh['img'=8,'proto'=4] {'img','proto'}, dimensions={0} | all-to-all | bytes 851968 | tf_op jit(solution)/shard_map/all_to_all | solution.py:604
  65.4 3.4 %shard_map.83 = (f32[384,4096]{1,0:T(8,128)}, f32[16,384]{1,0:T(8,128)}, f32[1,1]{1,0:T(1,128)}) custom-call(bf16[16,2,13,4,128]{4,3,2,1,0:T(4,128)(2,1)S(1)} %bitcast.8, f32[160,4096]{1,0:T(8,128)S(1)} %get-tuple-element.58.pull, f32[160,4096]{1,0:T(8,128)S(1)} %get-tuple-element.59.push, f32[160,4096]{1,0:T(8,128)S(1)} %get-tuple-element.49.logits, ...), custom_call_target="tpu_custom_call" | custom-call | flops 503316480 | bytes 12582912 | tf_op jit(solution)/shard_map/pallas_call | solution.py:27
Async XLA Ops:
  18.1 2.2 %collective-permute-start = (bf16[256,384]{1,0:T(8,128)(2,1)S(1)}, bf16[256,384]{1,0:T(8,128)(2,1)S(1)}, u32[]{:S(2)}, u32[]{:S(2)}) collective-permute-start(bf16[256,384]{1,0:T(8,128)(2,1)S(1)} %bitcast.5), channel_id=1, source_target_pairs={{0,1},{1,0},{2,3},{3,2},{4,5},{5,4},{6,7},{7,6},{8,9},{9,8},{10,11... | collective-permute-start | bytes 589832 | tf_op jit(solution)/shard_map/ppermute | solution.py:516
  20.3 23.8 %copy-start = (bf16[384,4096]{1,0:T(8,128)(2,1)S(1)}, bf16[384,4096]{1,0:T(8,128)(2,1)}, u32[]{:S(2)}) copy-start(bf16[384,4096]{1,0:T(8,128)(2,1)} %stu_w.3) | copy-start | bytes 9437188
  33.7 10.4 %collective-permute-start.1 = (bf16[32,7,4,128]{3,2,1,0:T(4,128)(2,1)S(1)}, bf16[32,7,4,128]{3,2,1,0:T(4,128)(2,1)S(1)}, u32[]{:S(2)}, u32[]{:S(2)}) collective-permute-start(bf16[32,7,4,128]{3,2,1,0:T(4,128)(2,1)S(1)} %all_to_all.21.got.mine), channel_id=1, source_target_pairs={{0,1},{1,0},{2,3},{3,2},{4,5},{5,4},{6,7},{7,6},{8,9},{9,8},{10,11... | collective-permute-start | bytes 688136 | tf_op jit(solution)/shard_map/ppermute | solution.py:553
  48.0 1.8 %collective-permute-start.2 = (bf16[256,768]{1,0:T(8,128)(2,1)S(1)}, bf16[256,768]{1,0:T(8,128)(2,1)S(1)}, u32[]{:S(2)}, u32[]{:S(2)}) collective-permute-start(bf16[256,768]{1,0:T(8,128)(2,1)S(1)} %get-tuple-element.56), channel_id=1, source_target_pairs={{0,1},{1,0},{2,3},{3,2},{4,5},{5,4},{6,7},{7,6},{8,9},{9,8},{10,11... | collective-permute-start | bytes 1179656 | tf_op jit(solution)/shard_map/ppermute | solution.py:587

commit v8 on v7

--- a/solution.py
+++ b/solution.py
@@ -253,13 +253,13 @@
 
 
 def spots(hot, sums, start, stop):
-    return dot(hot[:, start:stop], sums, ((0,), (1,)))
+    return dot(hot[:, start:stop], sums, ((0,), (0,)))
 
 
 def halves(hot, sums, at, keep_out, give_out):
     half = keep_out.shape[0]
     odd = odd_half() == 1
-    lanes = slice(at, at + sums.shape[0])
+    lanes = slice(at, at + sums.shape[1])
     for start, stop in blocks(half):
         low, high = spots(hot, sums, start, stop), spots(hot, sums, half + start, half + stop)
         keep_out[start:stop, lanes] = jnp.where(odd, high, low)
@@ -323,8 +323,7 @@
     sums_out,
     keep_out,
     give_out,
-    pulls,
-    pushes,
+    stack,
 ):
     rows, columns = logits_out.shape
     feat = stu_w.shape[0]
@@ -354,24 +353,24 @@
         l = dot(x, w, ((1,), (0,))) * (n * (1.0 / STUDENT_TEMP))
         logits_out[:, at] = l
         p = jnp.exp(l)
-        pulls[:, at] = (p * n).astype(BF16)
+        stack[:rows, at] = (p * n).astype(BF16)
         return acc + fold(p)
 
     def sweep(at, acc):
         k = kernel[:, at]
         kc = k * (1.0 / jnp.sum(k * wide, axis=0, keepdims=True))
         scaled_out[:, at] = kc
-        pushes[:, at] = (kc * inv_out[:, at]).astype(BF16)
+        stack[rows:, at] = (kc * inv_out[:, at]).astype(BF16)
         return acc + fold(kc)
 
     zero = jnp.zeros((rows, LANES), F32)
     part = over_chunks(columns, student, zero)
-    pull = dot(stu_w[...], pulls[...], ((1,), (1,)))
     total = over_chunks(columns, sweep, zero)
-    push = dot(pushes[...], stu_w[...], ((1,), (1,))).T
+    sums = dot(stack[...], stu_w[...], ((1,), (1,)))
+    pull, push = sums[:rows], sums[rows:]
     halves(hot, pull.astype(BF16), 0, keep_out, give_out)
     halves(hot, push.astype(BF16), feat, keep_out, give_out)
-    cross = jnp.sum(push * xt, axis=0, keepdims=True) * (1.0 / STUDENT_TEMP)
+    cross = to_row(fold(push * x.astype(F32))) * (1.0 / STUDENT_TEMP)
     sums_out[...] = lay_out([to_row(part), to_row(total), cross], *sums_out.shape)
 
 
@@ -581,7 +580,7 @@
         flops=6 * big * feat,
         moved=12 * big,
         exps=big,
-        scratch=[pltpu.VMEM((rows, columns), BF16), pltpu.VMEM((rows, columns), BF16)],
+        scratch=[pltpu.VMEM((2 * rows, columns), BF16)],
         limit=22 + half // 112,
     )
     give = near(swap(give))

time: 69.1 us -> 68.7 us (level)
  no operation moved by 1% of the time
where the time goes in v8:
time: 68.7 us; the launch traced here: 68.5 us
  blocking collectives  52.8 us (77%)
  Pallas kernels  13.5 us (20%)
  starting transfers between devices  0.95 us (1%)
  between operations  0.7 us (1%)
    all_to_all x1, blocking collectives, shards(): mine = exchange(sent.reshape(devices, each, feat)).reshape(half, feat)  16 us
    all_to_all x1, blocking collectives, shards(): got = exchange(sent)  15.5 us
    pallas_call x8, Pallas kernels, call(): pl.pallas_call(body, out_shape=outs, in_specs=specs or [VMEM] * len(args)...  13.5 us
    all_to_all x1, blocking collectives, shards(): stu_mine = exchange(sent.reshape(devices, *sent.shape[2:]))  11.9 us
    all_to_all x1, blocking collectives, shards(): got = near(exchange(sent))  9.48 us
  transfers between devices with their start and end apart: 3, of which 1 were waited for; matrix products, arithmetic and copies ran while one was open for 0% of the time, Pallas kernels for 5%

profile of v8, /device:TPU:0, one launch (start us, length us, event | category | flops | bytes accessed | tf_op | source)
XLA Modules:
  0.0 68.5 jit_solution(10844923528606637742)
XLA Ops:
  0.6 1.5 %shard_map.76 = (bf16[16,16,384]{2,1,0:T(8,128)(2,1)S(1)}, s32[1,128]{1,0:T(1,128)S(1)}, bf16[1,128,384]{2,1,0:T(8,128)(2,1)S(1)}, bf16[384,1536]{1,0:T(8,128)(2,1)S(1)}) custom-call(s32[1,128]{1,0:T(1,128)} %mask_hbm.1, bf16[1,128,384]{2,1,0:T(8,128)(2,1)} %stu_hbm.1, bf16[1,128,384]{2,1,0:T(8,128)(2,1)} %tea_hbm.1, bf16[384,4096]{1,0:T(8,128)(2,1)} %w_hbm.2), custom_call_target="tpu_custom_call" | custom-call | tf_op jit(solution)/shard_map/pallas_call | solution.py:27
  2.1 16.0 %all_to_all.20 = bf16[32,8,384]{2,1,0:T(8,128)(2,1)S(1)} all-to-all(bf16[32,8,384]{2,1,0:T(8,128)(2,1)S(1)} %bitcast.10), channel_id=1, replica_groups=mesh['img'=8,'proto'=4] {'img','proto'}, dimensions={0} | all-to-all | bytes 393216 | tf_op jit(solution)/shard_map/all_to_all | solution.py:513
  18.1 0.6 collective-permute-start
  18.7 1.6 %shard_map.77 = (bf16[384,2560]{1,0:T(8,128)(2,1)S(1)}, f32[1,4096]{1,0:T(1,128)S(1)}, f32[16,384]{1,0:T(8,128)S(1)}, f32[16,128]{1,0:T(8,128)S(1)}) custom-call(s32[1,128]{1,0:T(1,128)S(1)} %get-tuple-element.38.mask_ref, bf16[1,128,384]{2,1,0:T(8,128)(2,1)S(1)} %get-tuple-element.39.stu_ref, bf16[384,1536]{1,0:T(8,128)(2,1)S(1)} %get-tuple-element.37.early_w, ...), custom_call_target="tpu_custom_call" | custom-call | flops 3145728 | bytes 6291456 | tf_op jit(solution)/shard_map/pallas_call | solution.py:27
  20.3 0.0 collective-permute-done.other
  20.3 0.0 copy-start
  20.3 1.6 %shard_map.78 = (f32[160,4096]{1,0:T(8,128)S(1)}, bf16[16,2,7,4,128]{4,3,2,1,0:T(4,128)(2,1)S(1)}, bf16[160,512]{1,0:T(8,128)(2,1)S(1)}) custom-call(bf16[256,384]{1,0:T(8,128)(2,1)S(1)} %bitcast.6, bf16[256,384]{1,0:T(8,128)(2,1)S(1)} %collective-permute-done.other, bf16[384,1536]{1,0:T(8,128)(2,1)S(1)} %get-tuple-element.37.early_w, ...), custom_call_target="tpu_custom_call" | custom-call | flops 503316480 | bytes 2621440 | tf_op jit(solution)/shard_map/pallas_call | solution.py:27
  21.9 11.9 %all_to_all.21.got.mine = bf16[32,7,4,128]{3,2,1,0:T(4,128)(2,1)S(1)} all-to-all(bf16[32,7,4,128]{3,2,1,0:T(4,128)(2,1)S(1)} %bitcast.9), channel_id=1, replica_groups=mesh['img'=8,'proto'=4] {'img','proto'}, dimensions={0} | all-to-all | bytes 458752 | tf_op jit(solution)/shard_map/all_to_all | solution.py:551
  33.7 0.2 collective-permute-start.1
  33.9 0.7 %shard_map.79 = f32[32,2,128]{2,1,0:T(2,128)S(1)} custom-call(bf16[32,7,4,128]{3,2,1,0:T(4,128)(2,1)S(1)} %all_to_all.21.got.mine, f32[160,4096]{1,0:T(8,128)S(1)} %get-tuple-element.45.kernel), custom_call_target="tpu_custom_call" | custom-call | flops 2621440 | bytes 2621440 | tf_op jit(solution)/shard_map/pallas_call | solution.py:27
  34.6 9.5 %all_to_all.22.got = f32[32,2,128]{2,1,0:T(2,128)S(1)} all-to-all(f32[32,2,128]{2,1,0:T(2,128)S(1)} %shard_map.79), channel_id=1, replica_groups=mesh['img'=8,'proto'=4] {'img','proto'}, dimensions={0} | all-to-all | bytes 65536 | tf_op jit(solution)/shard_map/all_to_all | solution.py:562
  44.1 0.0 collective-permute-done.1.other
  44.1 0.0 copy-done
  44.1 3.5 %shard_map.80 = (f32[1,4096]{1,0:T(1,128)S(1)}, f32[160,4096]{1,0:T(8,128)S(1)}, f32[160,4096]{1,0:T(8,128)S(1)}, bf16[384,160]{1,0:T(8,128)(2,1)S(1)}, f32[4,12...) custom-call(f32[32,2,128]{2,1,0:T(2,128)S(1)} %all_to_all.22.got, ...), custom_call_target="tpu_custom_call" | custom-call | flops 1509949440 | bytes 7864320 | tf_op jit(solution)/shard_map/pallas_call | solution.py:27
  47.6 0.2 collective-permute-start.2
  47.8 1.1 %shard_map.81 = (f32[160,4096]{1,0:T(8,128)S(1)}, f32[160,4096]{1,0:T(8,128)S(1)}, f32[16,160]{1,0:T(8,128)S(1)}, f32[160,128]{1,0:T(8,128)S(1)}) custom-call(f32[160,4096]{1,0:T(8,128)S(1)} %get-tuple-element.48.scaled, f32[160,4096]{1,0:T(8,128)S(1)} %get-tuple-element.49.logits, f32[1,4096]{1,0:T(1,128)S(1)} %get-tuple-element.50.inv, ...), custom_call_target="tpu_custom_call" | custom-call | flops 2621440 | bytes 10485760 | tf_op jit(solution)/shard_map/pallas_call | solution.py:27
  48.9 0.5 collective-permute-done.2.give
  49.4 0.2 shard_map.82
  49.6 15.5 %all_to_all.23 = bf16[32,13,4,128]{3,2,1,0:T(4,128)(2,1)S(1)} all-to-all(bf16[32,13,4,128]{3,2,1,0:T(4,128)(2,1)S(1)} %shard_map.82), channel_id=1, replica_groups=mesh['img'=8,'proto'=4] {'img','proto'}, dimensions={0} | all-to-all | bytes 851968 | tf_op jit(solution)/shard_map/all_to_all | solution.py:603
  65.1 3.4 %shard_map.83 = (f32[384,4096]{1,0:T(8,128)}, f32[16,384]{1,0:T(8,128)}, f32[1,1]{1,0:T(1,128)}) custom-call(bf16[16,2,13,4,128]{4,3,2,1,0:T(4,128)(2,1)S(1)} %bitcast.8, f32[160,4096]{1,0:T(8,128)S(1)} %get-tuple-element.58.pull, f32[160,4096]{1,0:T(8,128)S(1)} %get-tuple-element.59.push, f32[160,4096]{1,0:T(8,128)S(1)} %get-tuple-element.49.logits, ...), custom_call_target="tpu_custom_call" | custom-call | flops 503316480 | bytes 12582912 | tf_op jit(solution)/shard_map/pallas_call | solution.py:27
Async XLA Ops:
  18.1 2.2 %collective-permute-start = (bf16[256,384]{1,0:T(8,128)(2,1)S(1)}, bf16[256,384]{1,0:T(8,128)(2,1)S(1)}, u32[]{:S(2)}, u32[]{:S(2)}) collective-permute-start(bf16[256,384]{1,0:T(8,128)(2,1)S(1)} %bitcast.5), channel_id=1, source_target_pairs={{0,1},{1,0},{2,3},{3,2},{4,5},{5,4},{6,7},{7,6},{8,9},{9,8},{10,11... | collective-permute-start | bytes 589832 | tf_op jit(solution)/shard_map/ppermute | solution.py:515
  20.3 23.8 %copy-start = (bf16[384,4096]{1,0:T(8,128)(2,1)S(1)}, bf16[384,4096]{1,0:T(8,128)(2,1)}, u32[]{:S(2)}) copy-start(bf16[384,4096]{1,0:T(8,128)(2,1)} %stu_w.3) | copy-start | bytes 9437188
  33.7 10.4 %collective-permute-start.1 = (bf16[32,7,4,128]{3,2,1,0:T(4,128)(2,1)S(1)}, bf16[32,7,4,128]{3,2,1,0:T(4,128)(2,1)S(1)}, u32[]{:S(2)}, u32[]{:S(2)}) collective-permute-start(bf16[32,7,4,128]{3,2,1,0:T(4,128)(2,1)S(1)} %all_to_all.21.got.mine), channel_id=1, source_target_pairs={{0,1},{1,0},{2,3},{3,2},{4,5},{5,4},{6,7},{7,6},{8,9},{9,8},{10,11... | collective-permute-start | bytes 688136 | tf_op jit(solution)/shard_map/ppermute | solution.py:552
  47.6 1.8 %collective-permute-start.2 = (bf16[256,768]{1,0:T(8,128)(2,1)S(1)}, bf16[256,768]{1,0:T(8,128)(2,1)S(1)}, u32[]{:S(2)}, u32[]{:S(2)}) collective-permute-start(bf16[256,768]{1,0:T(8,128)(2,1)S(1)} %get-tuple-element.56), channel_id=1, source_target_pairs={{0,1},{1,0},{2,3},{3,2},{4,5},{5,4},{6,7},{7,6},{8,9},{9,8},{10,11... | collective-permute-start | bytes 1179656 | tf_op jit(solution)/shard_map/ppermute | solution.py:586

commit v9 on v8

--- a/solution.py
+++ b/solution.py
@@ -250,20 +250,6 @@
         tile = tiles[:, g * LANES : (g + 1) * LANES]
         for h in range(2):
             sent_out[:, h, held + g] = jnp.broadcast_to(tile[None], (peers, QUAD, LANES)).astype(BF16)
-
-
-def spots(hot, sums, start, stop):
-    return dot(hot[:, start:stop], sums, ((0,), (0,)))
-
-
-def halves(hot, sums, at, keep_out, give_out):
-    half = keep_out.shape[0]
-    odd = odd_half() == 1
-    lanes = slice(at, at + sums.shape[1])
-    for start, stop in blocks(half):
-        low, high = spots(hot, sums, start, stop), spots(hot, sums, half + start, half + stop)
-        keep_out[start:stop, lanes] = jnp.where(odd, high, low)
-        give_out[start:stop, lanes] = jnp.where(odd, low, high).astype(BF16)
 
 
 def row_weights(mine, other, hot, own_out, weight_out, protos):
@@ -320,14 +306,14 @@
     logits_out,
     scaled_out,
     xt_out,
-    sums_out,
+    vectors_out,
     keep_out,
     give_out,
     stack,
 ):
     rows, columns = logits_out.shape
     feat = stu_w.shape[0]
-    half = keep_out.shape[0]
+    half = hot.shape[1] // 2
     each = half // lax.axis_size(AXES)
 
     def reader(ref):
@@ -367,11 +353,11 @@
     part = over_chunks(columns, student, zero)
     total = over_chunks(columns, sweep, zero)
     sums = dot(stack[...], stu_w[...], ((1,), (1,)))
-    pull, push = sums[:rows], sums[rows:]
-    halves(hot, pull.astype(BF16), 0, keep_out, give_out)
-    halves(hot, push.astype(BF16), feat, keep_out, give_out)
-    cross = to_row(fold(push * x.astype(F32))) * (1.0 / STUDENT_TEMP)
-    sums_out[...] = lay_out([to_row(part), to_row(total), cross], *sums_out.shape)
+    for part_of, lanes in ((sums[:rows], slice(0, feat)), (sums[rows:], slice(feat, 2 * feat))):
+        keep_out[:, lanes] = part_of
+        give_out[:, lanes] = part_of.astype(BF16)
+    cross = to_row(fold(sums[rows:] * x.astype(F32))) * (1.0 / STUDENT_TEMP)
+    vectors_out[...] = lay_out([to_row(part), to_row(total), cross], *vectors_out.shape)
 
 
 def prepare_kernel(
@@ -390,18 +376,22 @@
     over_chunks(columns, body, 0)
 
 
-def fill_kernel(keep, give, sums, sent_out):
+def fill_kernel(keep, give, hot, vectors, sent_out):
     devices, groups, _, _ = sent_out.shape
-    half, both = keep.shape
+    half, both = hot.shape[1] // 2, keep.shape[1]
     each = half // devices
-    pair = keep[...] + give[...].astype(F32)
+    pair = (keep[...] + give[...].astype(F32)).astype(BF16)
     places = quads(each, both)
-    for g, (row, lane) in enumerate(places):
-        part = pair[:, lane : lane + LANES].reshape(devices, each, LANES)
-        sent_out[:, g] = part[:, row : row + QUAD].astype(BF16)
+    for start, stop in blocks(half):
+        own = jnp.where(odd_half() == 1, hot[:, half + start : half + stop], hot[:, start:stop])
+        slots = dot(own, pair, ((0,), (0,)))
+        peers = slice(start // each, stop // each)
+        for g, (row, lane) in enumerate(places):
+            part = slots[:, lane : lane + LANES].reshape((stop - start) // each, each, LANES)
+            sent_out[peers, g] = part[:, row : row + QUAD].astype(BF16)
     for g in range(len(places), groups):
         at = (g - len(places)) * LANES
-        sent_out[:, g] = jnp.broadcast_to(sums[:, at : at + LANES][None], (devices, QUAD, LANES)).astype(BF16)
+        sent_out[:, g] = jnp.broadcast_to(vectors[:, at : at + LANES][None], (devices, QUAD, LANES)).astype(BF16)
 
 
 def slots_of(got, each, both):
@@ -568,8 +558,8 @@
             matrix,
             pltpu.VMEM((feat, rows), BF16),
             pltpu.VMEM((QUAD, spare(3) * LANES), F32),
-            pltpu.VMEM((half, 2 * feat), F32),
-            pltpu.VMEM((half, 2 * feat), BF16),
+            pltpu.VMEM((rows, 2 * feat), F32),
+            pltpu.VMEM((rows, 2 * feat), BF16),
         ),
         got,
         kernel,
@@ -599,7 +589,7 @@
     )
     keep, pull, push, own_hot, weight = lax.optimization_barrier((keep, pull, push, own_hot, weight))
     payload = pltpu.VMEM((devices, 2 * held + spare(3), QUAD, LANES), BF16)
-    (sent,) = call(fill_kernel, (payload,), keep, give, sums)
+    (sent,) = call(fill_kernel, (payload,), keep, give, hot, sums)
     got = exchange(sent)
     got = near(got.reshape(devices // 2, 2, *got.shape[1:]))
     grad_weight, grad_rows, loss = call(

time: 68.7 us -> 68.7 us (level)
  no operation moved by 1% of the time
where the time goes in v9:
time: 68.7 us; the launch traced here: 68.5 us
  blocking collectives  52.8 us (77%)
  Pallas kernels  13.7 us (20%)
  starting transfers between devices  0.9 us (1%)
  between operations  0.7 us (1%)
    all_to_all x1, blocking collectives, shards(): mine = exchange(sent.reshape(devices, each, feat)).reshape(half, feat)  16 us
    all_to_all x1, blocking collectives, shards(): got = exchange(sent)  15.5 us
    pallas_call x8, Pallas kernels, call(): pl.pallas_call(body, out_shape=outs, in_specs=specs or [VMEM] * len(args)...  13.7 us
    all_to_all x1, blocking collectives, shards(): stu_mine = exchange(sent.reshape(devices, *sent.shape[2:]))  11.9 us
    all_to_all x1, blocking collectives, shards(): got = near(exchange(sent))  9.48 us
  transfers between devices with their start and end apart: 3, of which 1 were waited for; matrix products, arithmetic and copies ran while one was open for 0% of the time, Pallas kernels for 5%

profile of v9, /device:TPU:0, one launch (start us, length us, event | category | flops | bytes accessed | tf_op | source)
XLA Modules:
  0.0 68.5 jit_solution(5558141332528665508)
XLA Ops:
  0.6 1.5 %shard_map.76 = (bf16[16,16,384]{2,1,0:T(8,128)(2,1)S(1)}, s32[1,128]{1,0:T(1,128)S(1)}, bf16[1,128,384]{2,1,0:T(8,128)(2,1)S(1)}, bf16[384,1536]{1,0:T(8,128)(2,1)S(1)}) custom-call(s32[1,128]{1,0:T(1,128)} %mask_hbm.1, bf16[1,128,384]{2,1,0:T(8,128)(2,1)} %stu_hbm.1, bf16[1,128,384]{2,1,0:T(8,128)(2,1)} %tea_hbm.1, bf16[384,4096]{1,0:T(8,128)(2,1)} %w_hbm.2), custom_call_target="tpu_custom_call" | custom-call | tf_op jit(solution)/shard_map/pallas_call | solution.py:27
  2.1 16.0 %all_to_all.20 = bf16[32,8,384]{2,1,0:T(8,128)(2,1)S(1)} all-to-all(bf16[32,8,384]{2,1,0:T(8,128)(2,1)S(1)} %bitcast.10), channel_id=1, replica_groups=mesh['img'=8,'proto'=4] {'img','proto'}, dimensions={0} | all-to-all | bytes 393216 | tf_op jit(solution)/shard_map/all_to_all | solution.py:503
  18.1 0.6 collective-permute-start
  18.7 1.6 %shard_map.77 = (bf16[384,2560]{1,0:T(8,128)(2,1)S(1)}, f32[1,4096]{1,0:T(1,128)S(1)}, f32[16,384]{1,0:T(8,128)S(1)}, f32[16,128]{1,0:T(8,128)S(1)}) custom-call(s32[1,128]{1,0:T(1,128)S(1)} %get-tuple-element.38.mask_ref, bf16[1,128,384]{2,1,0:T(8,128)(2,1)S(1)} %get-tuple-element.39.stu_ref, bf16[384,1536]{1,0:T(8,128)(2,1)S(1)} %get-tuple-element.37.early_w, ...), custom_call_target="tpu_custom_call" | custom-call | flops 3145728 | bytes 6291456 | tf_op jit(solution)/shard_map/pallas_call | solution.py:27
  20.3 0.0 collective-permute-done.other
  20.3 0.0 copy-start
  20.3 1.6 %shard_map.78 = (f32[160,4096]{1,0:T(8,128)S(1)}, bf16[16,2,7,4,128]{4,3,2,1,0:T(4,128)(2,1)S(1)}, bf16[160,512]{1,0:T(8,128)(2,1)S(1)}) custom-call(bf16[256,384]{1,0:T(8,128)(2,1)S(1)} %bitcast.6, bf16[256,384]{1,0:T(8,128)(2,1)S(1)} %collective-permute-done.other, bf16[384,1536]{1,0:T(8,128)(2,1)S(1)} %get-tuple-element.37.early_w, ...), custom_call_target="tpu_custom_call" | custom-call | flops 503316480 | bytes 2621440 | tf_op jit(solution)/shard_map/pallas_call | solution.py:27
  21.9 11.9 %all_to_all.21.got.mine = bf16[32,7,4,128]{3,2,1,0:T(4,128)(2,1)S(1)} all-to-all(bf16[32,7,4,128]{3,2,1,0:T(4,128)(2,1)S(1)} %bitcast.9), channel_id=1, replica_groups=mesh['img'=8,'proto'=4] {'img','proto'}, dimensions={0} | all-to-all | bytes 458752 | tf_op jit(solution)/shard_map/all_to_all | solution.py:541
  33.8 0.2 collective-permute-start.1
  33.9 0.7 %shard_map.79 = f32[32,2,128]{2,1,0:T(2,128)S(1)} custom-call(bf16[32,7,4,128]{3,2,1,0:T(4,128)(2,1)S(1)} %all_to_all.21.got.mine, f32[160,4096]{1,0:T(8,128)S(1)} %get-tuple-element.45.kernel), custom_call_target="tpu_custom_call" | custom-call | flops 2621440 | bytes 2621440 | tf_op jit(solution)/shard_map/pallas_call | solution.py:27
  34.7 9.5 %all_to_all.22.got = f32[32,2,128]{2,1,0:T(2,128)S(1)} all-to-all(f32[32,2,128]{2,1,0:T(2,128)S(1)} %shard_map.79), channel_id=1, replica_groups=mesh['img'=8,'proto'=4] {'img','proto'}, dimensions={0} | all-to-all | bytes 65536 | tf_op jit(solution)/shard_map/all_to_all | solution.py:552
  44.1 0.0 collective-permute-done.1.other
  44.1 0.0 copy-done
  44.1 3.5 %shard_map.80 = (f32[1,4096]{1,0:T(1,128)S(1)}, f32[160,4096]{1,0:T(8,128)S(1)}, f32[160,4096]{1,0:T(8,128)S(1)}, bf16[384,160]{1,0:T(8,128)(2,1)S(1)}, f32[4,12...) custom-call(f32[32,2,128]{2,1,0:T(2,128)S(1)} %all_to_all.22.got, ...), custom_call_target="tpu_custom_call" | custom-call | flops 1509949440 | bytes 7864320 | tf_op jit(solution)/shard_map/pallas_call | solution.py:27
  47.7 0.1 collective-permute-start.2
  47.8 1.1 %shard_map.81 = (f32[160,4096]{1,0:T(8,128)S(1)}, f32[160,4096]{1,0:T(8,128)S(1)}, f32[16,160]{1,0:T(8,128)S(1)}, f32[160,128]{1,0:T(8,128)S(1)}) custom-call(f32[160,4096]{1,0:T(8,128)S(1)} %get-tuple-element.48.scaled, f32[160,4096]{1,0:T(8,128)S(1)} %get-tuple-element.49.logits, f32[1,4096]{1,0:T(1,128)S(1)} %get-tuple-element.50.inv, ...), custom_call_target="tpu_custom_call" | custom-call | flops 2621440 | bytes 10485760 | tf_op jit(solution)/shard_map/pallas_call | solution.py:27
  48.9 0.3 collective-permute-done.2.give
  49.2 0.3 shard_map.82
  49.5 15.5 %all_to_all.23 = bf16[32,13,4,128]{3,2,1,0:T(4,128)(2,1)S(1)} all-to-all(bf16[32,13,4,128]{3,2,1,0:T(4,128)(2,1)S(1)} %shard_map.82), channel_id=1, replica_groups=mesh['img'=8,'proto'=4] {'img','proto'}, dimensions={0} | all-to-all | bytes 851968 | tf_op jit(solution)/shard_map/all_to_all | solution.py:593
  65.0 3.4 %shard_map.83 = (f32[384,4096]{1,0:T(8,128)}, f32[16,384]{1,0:T(8,128)}, f32[1,1]{1,0:T(1,128)}) custom-call(bf16[16,2,13,4,128]{4,3,2,1,0:T(4,128)(2,1)S(1)} %bitcast.8, f32[160,4096]{1,0:T(8,128)S(1)} %get-tuple-element.58.pull, f32[160,4096]{1,0:T(8,128)S(1)} %get-tuple-element.59.push, f32[160,4096]{1,0:T(8,128)S(1)} %get-tuple-element.49.logits, ...), custom_call_target="tpu_custom_call" | custom-call | flops 503316480 | bytes 12582912 | tf_op jit(solution)/shard_map/pallas_call | solution.py:27
Async XLA Ops:
  18.1 2.2 %collective-permute-start = (bf16[256,384]{1,0:T(8,128)(2,1)S(1)}, bf16[256,384]{1,0:T(8,128)(2,1)S(1)}, u32[]{:S(2)}, u32[]{:S(2)}) collective-permute-start(bf16[256,384]{1,0:T(8,128)(2,1)S(1)} %bitcast.5), channel_id=1, source_target_pairs={{0,1},{1,0},{2,3},{3,2},{4,5},{5,4},{6,7},{7,6},{8,9},{9,8},{10,11... | collective-permute-start | bytes 589832 | tf_op jit(solution)/shard_map/ppermute | solution.py:505
  20.3 23.9 %copy-start = (bf16[384,4096]{1,0:T(8,128)(2,1)S(1)}, bf16[384,4096]{1,0:T(8,128)(2,1)}, u32[]{:S(2)}) copy-start(bf16[384,4096]{1,0:T(8,128)(2,1)} %stu_w.3) | copy-start | bytes 9437188
  33.8 10.4 %collective-permute-start.1 = (bf16[32,7,4,128]{3,2,1,0:T(4,128)(2,1)S(1)}, bf16[32,7,4,128]{3,2,1,0:T(4,128)(2,1)S(1)}, u32[]{:S(2)}, u32[]{:S(2)}) collective-permute-start(bf16[32,7,4,128]{3,2,1,0:T(4,128)(2,1)S(1)} %all_to_all.21.got.mine), channel_id=1, source_target_pairs={{0,1},{1,0},{2,3},{3,2},{4,5},{5,4},{6,7},{7,6},{8,9},{9,8},{10,11... | collective-permute-start | bytes 688136 | tf_op jit(solution)/shard_map/ppermute | solution.py:542
  47.7 1.5 %collective-permute-start.2 = (bf16[160,768]{1,0:T(8,128)(2,1)S(1)}, bf16[160,768]{1,0:T(8,128)(2,1)S(1)}, u32[]{:S(2)}, u32[]{:S(2)}) collective-permute-start(bf16[160,768]{1,0:T(8,128)(2,1)S(1)} %get-tuple-element.56), channel_id=1, source_target_pairs={{0,1},{1,0},{2,3},{3,2},{4,5},{5,4},{6,7},{7,6},{8,9},{9,8},{10,11... | collective-permute-start | bytes 737288 | tf_op jit(solution)/shard_map/ppermute | solution.py:576

commit v10 on v9

--- a/solution.py
+++ b/solution.py
@@ -245,7 +245,7 @@
             c = 1.0 / jnp.sum(k, axis=0, keepdims=True)
             acc = acc + fold(k * c)
     held = len(quads(each, feat))
-    tiles = lay_out(split(to_row(acc)), QUAD, (groups - held) * LANES)
+    tiles = lay_out(split(widen(to_row(acc))), QUAD, (groups - held) * LANES)
     for g in range(groups - held):
         tile = tiles[:, g * LANES : (g + 1) * LANES]
         for h in range(2):
@@ -281,8 +281,9 @@
 def sweep_kernel(got, kernel, sent_out, *, held):
     rows, columns = kernel.shape
     sums = [jnp.sum(got[:, g].astype(F32), axis=0) for g in range(held, got.shape[1])]
-    high, low = read_out(jnp.concatenate(sums, axis=1), rows, 2)
-    total = high + low
+    width = -(-rows // LANES) * LANES
+    high, low = read_out(jnp.concatenate(sums, axis=1), width, 2)
+    total = (high + low)[:rows]
     wide = spread(1.0 / total, chunks(columns)[0].stop)
 
     def body(at, acc):
@@ -334,8 +335,7 @@
 
     def student(at, acc):
         w = stu_w[:, at]
-        n = inverse_norms(w)
-        inv_out[:, at] = n
+        n = inv_out[:, at]
         l = dot(x, w, ((1,), (0,))) * (n * (1.0 / STUDENT_TEMP))
         logits_out[:, at] = l
         p = jnp.exp(l)
@@ -346,12 +346,14 @@
         k = kernel[:, at]
         kc = k * (1.0 / jnp.sum(k * wide, axis=0, keepdims=True))
         scaled_out[:, at] = kc
-        stack[rows:, at] = (kc * inv_out[:, at]).astype(BF16)
+        n = inverse_norms(stu_w[:, at])
+        inv_out[:, at] = n
+        stack[rows:, at] = (kc * n).astype(BF16)
         return acc + fold(kc)
 
     zero = jnp.zeros((rows, LANES), F32)
+    total = over_chunks(columns, sweep, zero)
     part = over_chunks(columns, student, zero)
-    total = over_chunks(columns, sweep, zero)
     sums = dot(stack[...], stu_w[...], ((1,), (1,)))
     for part_of, lanes in ((sums[:rows], slice(0, feat)), (sums[rows:], slice(feat, 2 * feat))):
         keep_out[:, lanes] = part_of
@@ -525,7 +527,7 @@
         first_kernel,
         (
             matrix,
-            pltpu.VMEM((devices // 2, 2, held + spare(2), QUAD, LANES), BF16),
+            pltpu.VMEM((devices // 2, 2, held + -(-2 * tiles // QUAD), QUAD, LANES), BF16),
             pltpu.VMEM((rows, 2 * half), BF16),
         ),
         mine,

time: 68.7 us -> 68.5 us (level)
  no operation moved by 1% of the time
where the time goes in v10:
time: 68.5 us; the launch traced here: 68.3 us
  blocking collectives  52.8 us (77%)
  Pallas kernels  13.6 us (20%)
  starting transfers between devices  0.9 us (1%)
  between operations  0.7 us (1%)
    all_to_all x1, blocking collectives, shards(): mine = exchange(sent.reshape(devices, each, feat)).reshape(half, feat)  16 us
    all_to_all x1, blocking collectives, shards(): got = exchange(sent)  15.5 us
    pallas_call x8, Pallas kernels, call(): pl.pallas_call(body, out_shape=outs, in_specs=specs or [VMEM] * len(args)...  13.6 us
    all_to_all x1, blocking collectives, shards(): stu_mine = exchange(sent.reshape(devices, *sent.shape[2:]))  11.9 us
    all_to_all x1, blocking collectives, shards(): got = near(exchange(sent))  9.48 us
  transfers between devices with their start and end apart: 3, of which 1 were waited for; matrix products, arithmetic and copies ran while one was open for 0% of the time, Pallas kernels for 5%

profile of v10, /device:TPU:0, one launch (start us, length us, event | category | flops | bytes accessed | tf_op | source)
XLA Modules:
  0.0 68.3 jit_solution(9923969530694774425)
XLA Ops:
  0.6 1.5 %shard_map.76 = (bf16[16,16,384]{2,1,0:T(8,128)(2,1)S(1)}, s32[1,128]{1,0:T(1,128)S(1)}, bf16[1,128,384]{2,1,0:T(8,128)(2,1)S(1)}, bf16[384,1536]{1,0:T(8,128)(2,1)S(1)}) custom-call(s32[1,128]{1,0:T(1,128)} %mask_hbm.1, bf16[1,128,384]{2,1,0:T(8,128)(2,1)} %stu_hbm.1, bf16[1,128,384]{2,1,0:T(8,128)(2,1)} %tea_hbm.1, bf16[384,4096]{1,0:T(8,128)(2,1)} %w_hbm.2), custom_call_target="tpu_custom_call" | custom-call | tf_op jit(solution)/shard_map/pallas_call | solution.py:27
  2.1 16.0 %all_to_all.20 = bf16[32,8,384]{2,1,0:T(8,128)(2,1)S(1)} all-to-all(bf16[32,8,384]{2,1,0:T(8,128)(2,1)S(1)} %bitcast.10), channel_id=1, replica_groups=mesh['img'=8,'proto'=4] {'img','proto'}, dimensions={0} | all-to-all | bytes 393216 | tf_op jit(solution)/shard_map/all_to_all | solution.py:505
  18.1 0.6 collective-permute-start
  18.7 1.6 %shard_map.77 = (bf16[384,2560]{1,0:T(8,128)(2,1)S(1)}, f32[1,4096]{1,0:T(1,128)S(1)}, f32[16,384]{1,0:T(8,128)S(1)}, f32[16,128]{1,0:T(8,128)S(1)}) custom-call(s32[1,128]{1,0:T(1,128)S(1)} %get-tuple-element.38.mask_ref, bf16[1,128,384]{2,1,0:T(8,128)(2,1)S(1)} %get-tuple-element.39.stu_ref, bf16[384,1536]{1,0:T(8,128)(2,1)S(1)} %get-tuple-element.37.early_w, ...), custom_call_target="tpu_custom_call" | custom-call | flops 3145728 | bytes 6291456 | tf_op jit(solution)/shard_map/pallas_call | solution.py:27
  20.3 0.0 collective-permute-done.other
  20.3 0.0 copy-start
  20.3 1.5 %shard_map.78 = (f32[160,4096]{1,0:T(8,128)S(1)}, bf16[16,2,7,4,128]{4,3,2,1,0:T(4,128)(2,1)S(1)}, bf16[160,512]{1,0:T(8,128)(2,1)S(1)}) custom-call(bf16[256,384]{1,0:T(8,128)(2,1)S(1)} %bitcast.6, bf16[256,384]{1,0:T(8,128)(2,1)S(1)} %collective-permute-done.other, bf16[384,1536]{1,0:T(8,128)(2,1)S(1)} %get-tuple-element.37.early_w, ...), custom_call_target="tpu_custom_call" | custom-call | flops 503316480 | bytes 2621440 | tf_op jit(solution)/shard_map/pallas_call | solution.py:27
  21.8 11.9 %all_to_all.21.got.mine = bf16[32,7,4,128]{3,2,1,0:T(4,128)(2,1)S(1)} all-to-all(bf16[32,7,4,128]{3,2,1,0:T(4,128)(2,1)S(1)} %bitcast.9), channel_id=1, replica_groups=mesh['img'=8,'proto'=4] {'img','proto'}, dimensions={0} | all-to-all | bytes 458752 | tf_op jit(solution)/shard_map/all_to_all | solution.py:543
  33.7 0.2 collective-permute-start.1
  33.9 0.7 %shard_map.79 = f32[32,2,128]{2,1,0:T(2,128)S(1)} custom-call(bf16[32,7,4,128]{3,2,1,0:T(4,128)(2,1)S(1)} %all_to_all.21.got.mine, f32[160,4096]{1,0:T(8,128)S(1)} %get-tuple-element.45.kernel), custom_call_target="tpu_custom_call" | custom-call | flops 2621440 | bytes 2621440 | tf_op jit(solution)/shard_map/pallas_call | solution.py:27
  34.6 9.5 %all_to_all.22.got = f32[32,2,128]{2,1,0:T(2,128)S(1)} all-to-all(f32[32,2,128]{2,1,0:T(2,128)S(1)} %shard_map.79), channel_id=1, replica_groups=mesh['img'=8,'proto'=4] {'img','proto'}, dimensions={0} | all-to-all | bytes 65536 | tf_op jit(solution)/shard_map/all_to_all | solution.py:554
  44.0 0.0 collective-permute-done.1.other
  44.0 0.0 copy-done
  44.1 3.5 %shard_map.80 = (f32[1,4096]{1,0:T(1,128)S(1)}, f32[160,4096]{1,0:T(8,128)S(1)}, f32[160,4096]{1,0:T(8,128)S(1)}, bf16[384,160]{1,0:T(8,128)(2,1)S(1)}, f32[4,12...) custom-call(f32[32,2,128]{2,1,0:T(2,128)S(1)} %all_to_all.22.got, ...), custom_call_target="tpu_custom_call" | custom-call | flops 1509949440 | bytes 7864320 | tf_op jit(solution)/shard_map/pallas_call | solution.py:27
  47.5 0.1 collective-permute-start.2
  47.6 1.1 %shard_map.81 = (f32[160,4096]{1,0:T(8,128)S(1)}, f32[160,4096]{1,0:T(8,128)S(1)}, f32[16,160]{1,0:T(8,128)S(1)}, f32[160,128]{1,0:T(8,128)S(1)}) custom-call(f32[160,4096]{1,0:T(8,128)S(1)} %get-tuple-element.48.scaled, f32[160,4096]{1,0:T(8,128)S(1)} %get-tuple-element.49.logits, f32[1,4096]{1,0:T(1,128)S(1)} %get-tuple-element.50.inv, ...), custom_call_target="tpu_custom_call" | custom-call | flops 2621440 | bytes 10485760 | tf_op jit(solution)/shard_map/pallas_call | solution.py:27
  48.8 0.3 collective-permute-done.2.give
  49.0 0.3 shard_map.82
  49.4 15.5 %all_to_all.23 = bf16[32,13,4,128]{3,2,1,0:T(4,128)(2,1)S(1)} all-to-all(bf16[32,13,4,128]{3,2,1,0:T(4,128)(2,1)S(1)} %shard_map.82), channel_id=1, replica_groups=mesh['img'=8,'proto'=4] {'img','proto'}, dimensions={0} | all-to-all | bytes 851968 | tf_op jit(solution)/shard_map/all_to_all | solution.py:595
  64.9 3.4 %shard_map.83 = (f32[384,4096]{1,0:T(8,128)}, f32[16,384]{1,0:T(8,128)}, f32[1,1]{1,0:T(1,128)}) custom-call(bf16[16,2,13,4,128]{4,3,2,1,0:T(4,128)(2,1)S(1)} %bitcast.8, f32[160,4096]{1,0:T(8,128)S(1)} %get-tuple-element.58.pull, f32[160,4096]{1,0:T(8,128)S(1)} %get-tuple-element.59.push, f32[160,4096]{1,0:T(8,128)S(1)} %get-tuple-element.49.logits, ...), custom_call_target="tpu_custom_call" | custom-call | flops 503316480 | bytes 12582912 | tf_op jit(solution)/shard_map/pallas_call | solution.py:27
Async XLA Ops:
  18.1 2.2 %collective-permute-start = (bf16[256,384]{1,0:T(8,128)(2,1)S(1)}, bf16[256,384]{1,0:T(8,128)(2,1)S(1)}, u32[]{:S(2)}, u32[]{:S(2)}) collective-permute-start(bf16[256,384]{1,0:T(8,128)(2,1)S(1)} %bitcast.5), channel_id=1, source_target_pairs={{0,1},{1,0},{2,3},{3,2},{4,5},{5,4},{6,7},{7,6},{8,9},{9,8},{10,11... | collective-permute-start | bytes 589832 | tf_op jit(solution)/shard_map/ppermute | solution.py:507
  20.3 23.8 %copy-start = (bf16[384,4096]{1,0:T(8,128)(2,1)S(1)}, bf16[384,4096]{1,0:T(8,128)(2,1)}, u32[]{:S(2)}) copy-start(bf16[384,4096]{1,0:T(8,128)(2,1)} %stu_w.3) | copy-start | bytes 9437188
  33.7 10.4 %collective-permute-start.1 = (bf16[32,7,4,128]{3,2,1,0:T(4,128)(2,1)S(1)}, bf16[32,7,4,128]{3,2,1,0:T(4,128)(2,1)S(1)}, u32[]{:S(2)}, u32[]{:S(2)}) collective-permute-start(bf16[32,7,4,128]{3,2,1,0:T(4,128)(2,1)S(1)} %all_to_all.21.got.mine), channel_id=1, source_target_pairs={{0,1},{1,0},{2,3},{3,2},{4,5},{5,4},{6,7},{7,6},{8,9},{9,8},{10,11... | collective-permute-start | bytes 688136 | tf_op jit(solution)/shard_map/ppermute | solution.py:544
  47.5 1.5 %collective-permute-start.2 = (bf16[160,768]{1,0:T(8,128)(2,1)S(1)}, bf16[160,768]{1,0:T(8,128)(2,1)S(1)}, u32[]{:S(2)}, u32[]{:S(2)}) collective-permute-start(bf16[160,768]{1,0:T(8,128)(2,1)S(1)} %get-tuple-element.56), channel_id=1, source_target_pairs={{0,1},{1,0},{2,3},{3,2},{4,5},{5,4},{6,7},{7,6},{8,9},{9,8},{10,11... | collective-permute-start | bytes 737288 | tf_op jit(solution)/shard_map/ppermute | solution.py:578

commit v11 on v10

--- a/solution.py
+++ b/solution.py
@@ -166,9 +166,10 @@
         copy.wait()
 
 
-def norms_kernel(mask_ref, stu_ref, early_w, w_hbm, late_w, inv_out, unit_out, norm_out, sems):
+def norms_kernel(mine, mask_ref, stu_ref, early_w, w_hbm, late_w, inv_out, unit_out, norm_out, hot_out, sems):
     early = early_w.shape[1]
     copies = start_load(w_hbm, late_w, sems, early)
+    packing([slot_flags(mine[:, :LANES])] * 2, hot_out)
     unit, norm, _ = own_slots(mask_ref, stu_ref, unit_out.shape[0])
     unit_out[...] = unit
     norm_out[...] = jnp.broadcast_to(norm, norm_out.shape)
@@ -223,12 +224,11 @@
     return [(row, lane) for lane in range(0, feat, LANES) for row in range(0, each, QUAD)]
 
 
-def first_kernel(mine, other, early_w, late_w, inv, unit, kernel_out, sent_out, hot_out):
+def first_kernel(mine, other, early_w, late_w, inv, unit, hot, kernel_out, sent_out):
     rows = kernel_out.shape[0]
     peers, _, groups, _, _ = sent_out.shape
     feat = late_w.shape[0]
-    packing([slot_flags(in_order(mine[:, :LANES], other[:, :LANES], h)) for h in range(2)], hot_out)
-    x = pack_rows(hot_out, lambda a, b: mine[a:b], lambda a, b: other[a:b], mine.shape[0])
+    x = pack_rows(hot, lambda a, b: mine[a:b], lambda a, b: other[a:b], mine.shape[0])
     each = unit.shape[0] // 2
     for h in range(2):
         for g, (row, lane) in enumerate(quads(each, feat)):
@@ -363,10 +363,14 @@
 
 
 def prepare_kernel(
-    scaled, logits, inv, mine, other, hot, pull_out, push_out, own_out, weight_out, *, scale, protos
+    scaled, logits, inv, mine, other, hot, pull_out, push_out, own_out, weight_out, spots_out, *, scale, protos
 ):
     rows, columns = scaled.shape
     row_weights(mine, other, hot, own_out, weight_out, protos)
+    half = spots_out.shape[0]
+    for start, stop in blocks(half):
+        own = jnp.where(odd_half() == 1, hot[:, half + start : half + stop], hot[:, start:stop])
+        spots_out[start:stop] = own.astype(F32).T.astype(BF16)
     factor = spread(weight_out[...] * (rows / STUDENT_TEMP), chunks(columns)[0].stop)
 
     def body(at, _):
@@ -380,13 +384,12 @@
 
 def fill_kernel(keep, give, hot, vectors, sent_out):
     devices, groups, _, _ = sent_out.shape
-    half, both = hot.shape[1] // 2, keep.shape[1]
+    half, both = hot.shape[0], keep.shape[1]
     each = half // devices
     pair = (keep[...] + give[...].astype(F32)).astype(BF16)
     places = quads(each, both)
     for start, stop in blocks(half):
-        own = jnp.where(odd_half() == 1, hot[:, half + start : half + stop], hot[:, start:stop])
-        slots = dot(own, pair, ((0,), (0,)))
+        slots = dot(hot[start:stop], pair, ((1,), (0,)))
         peers = slice(start // each, stop // each)
         for g, (row, lane) in enumerate(places):
             part = slots[:, lane : lane + LANES].reshape((stop - start) // each, each, LANES)
@@ -475,6 +478,7 @@
     assert images == 1 and protos % 2 == 0
     columns = student_weight.shape[1]
     own = patches // 2 // protos
+    assert patches // 8 % own == 0
     each = own // 2
     half = each * devices
     rows = 2 * half * 5 // 16
@@ -506,29 +510,30 @@
     mine, teacher_weight = lax.optimization_barrier((mine, teacher_weight))
     other = near(swap(mine))
     mine = near(mine)
-    late_w, tea_inv, unit, norm = call(
+    late_w, tea_inv, unit, norm, hot = call(
         norms_kernel,
         (
             late_w,
             line,
             pltpu.VMEM((own, feat), F32),
             pltpu.VMEM((own, LANES), F32),
+            pltpu.VMEM((rows, 2 * half), BF16),
         ),
+        mine,
         flags,
         feats,
         early_w,
         far(teacher_weight),
         flops=2 * feat * columns,
         moved=4 * feat * columns,
-        specs=[VMEM, VMEM, VMEM, HBM],
+        specs=[VMEM, VMEM, VMEM, VMEM, HBM],
         scratch=[pltpu.SemaphoreType.DMA((len(chunks(columns - early)),))],
     )
-    kernel, sent, hot = call(
+    kernel, sent = call(
         first_kernel,
         (
             matrix,
             pltpu.VMEM((devices // 2, 2, held + -(-2 * tiles // QUAD), QUAD, LANES), BF16),
-            pltpu.VMEM((rows, 2 * half), BF16),
         ),
         mine,
         other,
@@ -536,6 +541,7 @@
         late_w,
         tea_inv,
         unit,
+        hot,
         flops=2 * big * feat,
         moved=4 * big,
         exps=big,
@@ -576,9 +582,9 @@
         limit=22 + half // 112,
     )
     give = near(swap(give))
-    pull, push, own_hot, weight = call(
+    pull, push, own_hot, weight, spots = call(
         functools.partial(prepare_kernel, scale=columns * devices * GRAD_SCALE, protos=protos),
-        (matrix, matrix, pltpu.VMEM((own, rows), F32), column),
+        (matrix, matrix, pltpu.VMEM((own, rows), F32), column, pltpu.VMEM((half, rows), BF16)),
         scaled,
         logits,
         stu_inv,
@@ -591,7 +597,7 @@
     )
     keep, pull, push, own_hot, weight = lax.optimization_barrier((keep, pull, push, own_hot, weight))
     payload = pltpu.VMEM((devices, 2 * held + spare(3), QUAD, LANES), BF16)
-    (sent,) = call(fill_kernel, (payload,), keep, give, hot, sums)
+    (sent,) = call(fill_kernel, (payload,), keep, give, spots, sums)
     got = exchange(sent)
     got = near(got.reshape(devices // 2, 2, *got.shape[1:]))
     grad_weight, grad_rows, loss = call(

time: 68.5 us -> 68.2 us (level)
  no operation moved by 1% of the time
where the time goes in v11:
time: 68.2 us; the launch traced here: 68 us
  blocking collectives  52.8 us (77%)
  Pallas kernels  13.3 us (20%)
  starting transfers between devices  0.9 us (1%)
  between operations  0.7 us (1%)
    all_to_all x1, blocking collectives, shards(): mine = exchange(sent.reshape(devices, each, feat)).reshape(half, feat)  16 us
    all_to_all x1, blocking collectives, shards(): got = exchange(sent)  15.5 us
    pallas_call x8, Pallas kernels, call(): pl.pallas_call(body, out_shape=outs, in_specs=specs or [VMEM] * len(args)...  13.3 us
    all_to_all x1, blocking collectives, shards(): stu_mine = exchange(sent.reshape(devices, *sent.shape[2:]))  11.9 us
    all_to_all x1, blocking collectives, shards(): got = near(exchange(sent))  9.48 us
  transfers between devices with their start and end apart: 3, of which 1 were waited for; matrix products, arithmetic and copies ran while one was open for 0% of the time, Pallas kernels for 5%

profile of v11, /device:TPU:0, one launch (start us, length us, event | category | flops | bytes accessed | tf_op | source)
XLA Modules:
  0.0 68.0 jit_solution(15263008725693471854)
XLA Ops:
  0.6 1.5 %shard_map.76 = (bf16[16,16,384]{2,1,0:T(8,128)(2,1)S(1)}, s32[1,128]{1,0:T(1,128)S(1)}, bf16[1,128,384]{2,1,0:T(8,128)(2,1)S(1)}, bf16[384,1536]{1,0:T(8,128)(2,1)S(1)}) custom-call(s32[1,128]{1,0:T(1,128)} %mask_hbm.1, bf16[1,128,384]{2,1,0:T(8,128)(2,1)} %stu_hbm.1, bf16[1,128,384]{2,1,0:T(8,128)(2,1)} %tea_hbm.1, bf16[384,4096]{1,0:T(8,128)(2,1)} %w_hbm.2), custom_call_target="tpu_custom_call" | custom-call | tf_op jit(solution)/shard_map/pallas_call | solution.py:27
  2.1 16.0 %all_to_all.20 = bf16[32,8,384]{2,1,0:T(8,128)(2,1)S(1)} all-to-all(bf16[32,8,384]{2,1,0:T(8,128)(2,1)S(1)} %bitcast.11), channel_id=1, replica_groups=mesh['img'=8,'proto'=4] {'img','proto'}, dimensions={0} | all-to-all | bytes 393216 | tf_op jit(solution)/shard_map/all_to_all | solution.py:509
  18.1 0.6 collective-permute-start
  18.7 1.7 %shard_map.77 = (bf16[384,2560]{1,0:T(8,128)(2,1)S(1)}, f32[1,4096]{1,0:T(1,128)S(1)}, f32[16,384]{1,0:T(8,128)S(1)}, f32[16,128]{1,0:T(8,128)S(1)}, bf16[160,512]{1,0:T(8,128)(2,1)S(1)}) custom-call(bf16[256,384]{1,0:T(8,128)(2,1)S(1)} %bitcast.6, s32[1,128]{1,0:T(1,128)S(1)} %get-tuple-element.39.mask_ref, ...), custom_call_target="tpu_custom_call" | custom-call | flops 3145728 | bytes 6291456 | tf_op jit(solution)/shard_map/pallas_call | solution.py:27
  20.3 0.0 collective-permute-done.other
  20.3 1.2 %shard_map.78 = (f32[160,4096]{1,0:T(8,128)S(1)}, bf16[16,2,7,4,128]{4,3,2,1,0:T(4,128)(2,1)S(1)}) custom-call(bf16[256,384]{1,0:T(8,128)(2,1)S(1)} %bitcast.7, bf16[256,384]{1,0:T(8,128)(2,1)S(1)} %collective-permute-done.other, bf16[384,1536]{1,0:T(8,128)(2,1)S(1)} %get-tuple-element.38.early_w, bf16[384,2560]{1,0:T(8,128)(2,1)S(1)} %get-tuple-element.42.late_w, ...), custom_call_target="tpu_custom_call" | custom-call | flops 503316480 | bytes 2621440 | tf_op jit(solution)/shard_map/pallas_call | solution.py:27
  21.6 0.0 copy-start
  21.6 11.9 %all_to_all.21.got.mine = bf16[32,7,4,128]{3,2,1,0:T(4,128)(2,1)S(1)} all-to-all(bf16[32,7,4,128]{3,2,1,0:T(4,128)(2,1)S(1)} %bitcast.10), channel_id=1, replica_groups=mesh['img'=8,'proto'=4] {'img','proto'}, dimensions={0} | all-to-all | bytes 458752 | tf_op jit(solution)/shard_map/all_to_all | solution.py:549
  33.4 0.2 collective-permute-start.1
  33.6 0.7 %shard_map.79 = f32[32,2,128]{2,1,0:T(2,128)S(1)} custom-call(bf16[32,7,4,128]{3,2,1,0:T(4,128)(2,1)S(1)} %all_to_all.21.got.mine, f32[160,4096]{1,0:T(8,128)S(1)} %get-tuple-element.47.kernel), custom_call_target="tpu_custom_call" | custom-call | flops 2621440 | bytes 2621440 | tf_op jit(solution)/shard_map/pallas_call | solution.py:27
  34.3 9.5 %all_to_all.22.got = f32[32,2,128]{2,1,0:T(2,128)S(1)} all-to-all(f32[32,2,128]{2,1,0:T(2,128)S(1)} %shard_map.79), channel_id=1, replica_groups=mesh['img'=8,'proto'=4] {'img','proto'}, dimensions={0} | all-to-all | bytes 65536 | tf_op jit(solution)/shard_map/all_to_all | solution.py:560
  43.8 0.0 collective-permute-done.1.other
  43.8 0.0 copy-done
  43.8 3.4 %shard_map.80 = (f32[1,4096]{1,0:T(1,128)S(1)}, f32[160,4096]{1,0:T(8,128)S(1)}, f32[160,4096]{1,0:T(8,128)S(1)}, bf16[384,160]{1,0:T(8,128)(2,1)S(1)}, f32[4,12...) custom-call(f32[32,2,128]{2,1,0:T(2,128)S(1)} %all_to_all.22.got, ...), custom_call_target="tpu_custom_call" | custom-call | flops 1509949440 | bytes 7864320 | tf_op jit(solution)/shard_map/pallas_call | solution.py:27
  47.3 0.1 collective-permute-start.2
  47.4 1.1 %shard_map.81 = (f32[160,4096]{1,0:T(8,128)S(1)}, f32[160,4096]{1,0:T(8,128)S(1)}, f32[16,160]{1,0:T(8,128)S(1)}, f32[160,128]{1,0:T(8,128)S(1)}, bf16[256,160]{1,0:T(8,128)(2,1)S(1)}) custom-call(f32[160,4096]{1,0:T(8,128)S(1)} %get-tuple-element.49.scaled, f32[160,4096]{1,0:T(8,128)S(1)} %get-tuple-element.50.logits, f32[1,4096]{1,0:T(1,128)S(1)} %get-tuple-element.51.inv, ...), custom_call_target="tpu_custom_call" | custom-call | flops 2621440 | bytes 10485760 | tf_op jit(solution)/shard_map/pallas_call | solution.py:27
  48.5 0.3 collective-permute-done.2.give
  48.8 0.3 shard_map.82
  49.1 15.5 %all_to_all.23 = bf16[32,13,4,128]{3,2,1,0:T(4,128)(2,1)S(1)} all-to-all(bf16[32,13,4,128]{3,2,1,0:T(4,128)(2,1)S(1)} %shard_map.82), channel_id=1, replica_groups=mesh['img'=8,'proto'=4] {'img','proto'}, dimensions={0} | all-to-all | bytes 851968 | tf_op jit(solution)/shard_map/all_to_all | solution.py:601
  64.5 3.4 %shard_map.83 = (f32[384,4096]{1,0:T(8,128)}, f32[16,384]{1,0:T(8,128)}, f32[1,1]{1,0:T(1,128)}) custom-call(bf16[16,2,13,4,128]{4,3,2,1,0:T(4,128)(2,1)S(1)} %bitcast.9, f32[160,4096]{1,0:T(8,128)S(1)} %get-tuple-element.60.pull, f32[160,4096]{1,0:T(8,128)S(1)} %get-tuple-element.61.push, f32[160,4096]{1,0:T(8,128)S(1)} %get-tuple-element.50.logits, ...), custom_call_target="tpu_custom_call" | custom-call | flops 503316480 | bytes 12582912 | tf_op jit(solution)/shard_map/pallas_call | solution.py:27
Async XLA Ops:
  18.1 2.3 %collective-permute-start = (bf16[256,384]{1,0:T(8,128)(2,1)S(1)}, bf16[256,384]{1,0:T(8,128)(2,1)S(1)}, u32[]{:S(2)}, u32[]{:S(2)}) collective-permute-start(bf16[256,384]{1,0:T(8,128)(2,1)S(1)} %bitcast.5), channel_id=1, source_target_pairs={{0,1},{1,0},{2,3},{3,2},{4,5},{5,4},{6,7},{7,6},{8,9},{9,8},{10,11... | collective-permute-start | bytes 589832 | tf_op jit(solution)/shard_map/ppermute | solution.py:511
  21.6 22.2 %copy-start = (bf16[384,4096]{1,0:T(8,128)(2,1)S(1)}, bf16[384,4096]{1,0:T(8,128)(2,1)}, u32[]{:S(2)}) copy-start(bf16[384,4096]{1,0:T(8,128)(2,1)} %stu_w.3) | copy-start | bytes 9437188
  33.4 10.4 %collective-permute-start.1 = (bf16[32,7,4,128]{3,2,1,0:T(4,128)(2,1)S(1)}, bf16[32,7,4,128]{3,2,1,0:T(4,128)(2,1)S(1)}, u32[]{:S(2)}, u32[]{:S(2)}) collective-permute-start(bf16[32,7,4,128]{3,2,1,0:T(4,128)(2,1)S(1)} %all_to_all.21.got.mine), channel_id=1, source_target_pairs={{0,1},{1,0},{2,3},{3,2},{4,5},{5,4},{6,7},{7,6},{8,9},{9,8},{10,11... | collective-permute-start | bytes 688136 | tf_op jit(solution)/shard_map/ppermute | solution.py:550
  47.3 1.5 %collective-permute-start.2 = (bf16[160,768]{1,0:T(8,128)(2,1)S(1)}, bf16[160,768]{1,0:T(8,128)(2,1)S(1)}, u32[]{:S(2)}, u32[]{:S(2)}) collective-permute-start(bf16[160,768]{1,0:T(8,128)(2,1)S(1)} %get-tuple-element.57), channel_id=1, source_target_pairs={{0,1},{1,0},{2,3},{3,2},{4,5},{5,4},{6,7},{7,6},{8,9},{9,8},{10,11... | collective-permute-start | bytes 737288 | tf_op jit(solution)/shard_map/ppermute | solution.py:584

commit v12 on v11

--- a/solution.py
+++ b/solution.py
@@ -293,7 +293,7 @@
 
     acc = over_chunks(columns, body, jnp.zeros((rows, LANES), F32))
     tiles = jnp.concatenate(tiles_of(to_row(acc)), axis=0)
-    sent_out[...] = jnp.broadcast_to(tiles[None], sent_out.shape)
+    sent_out[...] = jnp.broadcast_to(tiles[None], sent_out.shape).astype(BF16)
 
 
 def student_kernel(
@@ -330,7 +330,7 @@
     x = pack_rows(hot, reader(mine), reader(other), half)
     xt = x.astype(F32).T
     xt_out[...] = xt.astype(BF16)
-    (total,) = read_out(jnp.sum(got[...], axis=0), rows, 1)
+    (total,) = read_out(jnp.sum(got[...].astype(F32), axis=0), rows, 1)
     wide = spread(1.0 / total, chunks(columns)[0].stop)
 
     def student(at, acc):
@@ -551,7 +551,7 @@
     stu_mine = near(stu_mine)
     (sent,) = call(
         functools.partial(sweep_kernel, held=held),
-        (pltpu.VMEM((devices, tiles, LANES), F32),),
+        (pltpu.VMEM((devices, tiles, LANES), BF16),),
         stu_mine,
         kernel,
         flops=4 * big,

time: 68.2 us -> 68.1 us (level)
  no operation moved by 1% of the time
where the time goes in v12:
time: 68.1 us; the launch traced here: 67.8 us
  blocking collectives  52.7 us (77%)
  Pallas kernels  13.3 us (20%)
  starting transfers between devices  0.79 us (1%)
  between operations  0.71 us (1%)
    all_to_all x1, blocking collectives, shards(): mine = exchange(sent.reshape(devices, each, feat)).reshape(half, feat)  16 us
    all_to_all x1, blocking collectives, shards(): got = exchange(sent)  15.5 us
    pallas_call x8, Pallas kernels, call(): pl.pallas_call(body, out_shape=outs, in_specs=specs or [VMEM] * len(args)...  13.3 us
    all_to_all x1, blocking collectives, shards(): stu_mine = exchange(sent.reshape(devices, *sent.shape[2:]))  11.9 us
    all_to_all x1, blocking collectives, shards(): got = near(exchange(sent))  9.38 us
  transfers between devices with their start and end apart: 3, of which 1 were waited for; matrix products, arithmetic and copies ran while one was open for 0% of the time, Pallas kernels for 5%

profile of v12, /device:TPU:0, one launch (start us, length us, event | category | flops | bytes accessed | tf_op | source)
XLA Modules:
  0.0 67.8 jit_solution(5264671548374246097)
XLA Ops:
  0.6 1.5 %shard_map.76 = (bf16[16,16,384]{2,1,0:T(8,128)(2,1)S(1)}, s32[1,128]{1,0:T(1,128)S(1)}, bf16[1,128,384]{2,1,0:T(8,128)(2,1)S(1)}, bf16[384,1536]{1,0:T(8,128)(2,1)S(1)}) custom-call(s32[1,128]{1,0:T(1,128)} %mask_hbm.1, bf16[1,128,384]{2,1,0:T(8,128)(2,1)} %stu_hbm.1, bf16[1,128,384]{2,1,0:T(8,128)(2,1)} %tea_hbm.1, bf16[384,4096]{1,0:T(8,128)(2,1)} %w_hbm.2), custom_call_target="tpu_custom_call" | custom-call | tf_op jit(solution)/shard_map/pallas_call | solution.py:27
  2.1 16.0 %all_to_all.20 = bf16[32,8,384]{2,1,0:T(8,128)(2,1)S(1)} all-to-all(bf16[32,8,384]{2,1,0:T(8,128)(2,1)S(1)} %bitcast.11), channel_id=1, replica_groups=mesh['img'=8,'proto'=4] {'img','proto'}, dimensions={0} | all-to-all | bytes 393216 | tf_op jit(solution)/shard_map/all_to_all | solution.py:509
  18.1 0.6 collective-permute-start
  18.7 1.7 %shard_map.77 = (bf16[384,2560]{1,0:T(8,128)(2,1)S(1)}, f32[1,4096]{1,0:T(1,128)S(1)}, f32[16,384]{1,0:T(8,128)S(1)}, f32[16,128]{1,0:T(8,128)S(1)}, bf16[160,512]{1,0:T(8,128)(2,1)S(1)}) custom-call(bf16[256,384]{1,0:T(8,128)(2,1)S(1)} %bitcast.6, s32[1,128]{1,0:T(1,128)S(1)} %get-tuple-element.39.mask_ref, ...), custom_call_target="tpu_custom_call" | custom-call | flops 3145728 | bytes 6291456 | tf_op jit(solution)/shard_map/pallas_call | solution.py:27
  20.3 0.0 collective-permute-done.other
  20.3 0.0 copy-start
  20.4 1.2 %shard_map.78 = (f32[160,4096]{1,0:T(8,128)S(1)}, bf16[16,2,7,4,128]{4,3,2,1,0:T(4,128)(2,1)S(1)}) custom-call(bf16[256,384]{1,0:T(8,128)(2,1)S(1)} %bitcast.7, bf16[256,384]{1,0:T(8,128)(2,1)S(1)} %collective-permute-done.other, bf16[384,1536]{1,0:T(8,128)(2,1)S(1)} %get-tuple-element.38.early_w, bf16[384,2560]{1,0:T(8,128)(2,1)S(1)} %get-tuple-element.42.late_w, ...), custom_call_target="tpu_custom_call" | custom-call | flops 503316480 | bytes 2621440 | tf_op jit(solution)/shard_map/pallas_call | solution.py:27
  21.6 11.9 %all_to_all.21.got.mine = bf16[32,7,4,128]{3,2,1,0:T(4,128)(2,1)S(1)} all-to-all(bf16[32,7,4,128]{3,2,1,0:T(4,128)(2,1)S(1)} %bitcast.10), channel_id=1, replica_groups=mesh['img'=8,'proto'=4] {'img','proto'}, dimensions={0} | all-to-all | bytes 458752 | tf_op jit(solution)/shard_map/all_to_all | solution.py:549
  33.4 0.2 collective-permute-start.1
  33.6 0.7 %shard_map.79 = bf16[32,2,128]{2,1,0:T(2,128)(2,1)S(1)} custom-call(bf16[32,7,4,128]{3,2,1,0:T(4,128)(2,1)S(1)} %all_to_all.21.got.mine, f32[160,4096]{1,0:T(8,128)S(1)} %get-tuple-element.47.kernel), custom_call_target="tpu_custom_call" | custom-call | flops 2621440 | bytes 2621440 | tf_op jit(solution)/shard_map/pallas_call | solution.py:27
  34.3 9.4 %all_to_all.22.got = bf16[32,2,128]{2,1,0:T(2,128)(2,1)S(1)} all-to-all(bf16[32,2,128]{2,1,0:T(2,128)(2,1)S(1)} %shard_map.79), channel_id=1, replica_groups=mesh['img'=8,'proto'=4] {'img','proto'}, dimensions={0} | all-to-all | bytes 32768 | tf_op jit(solution)/shard_map/all_to_all | solution.py:560
  43.7 0.0 collective-permute-done.1.other
  43.7 0.0 copy-done
  43.7 3.4 %shard_map.80 = (f32[1,4096]{1,0:T(1,128)S(1)}, f32[160,4096]{1,0:T(8,128)S(1)}, f32[160,4096]{1,0:T(8,128)S(1)}, bf16[384,160]{1,0:T(8,128)(2,1)S(1)}, f32[4,12...) custom-call(bf16[32,2,128]{2,1,0:T(2,128)(2,1)S(1)} %all_to_all.22.got, ...), custom_call_target="tpu_custom_call" | custom-call | flops 1509949440 | bytes 7864320 | tf_op jit(solution)/shard_map/pallas_call | solution.py:27
  47.1 0.0 collective-permute-start.2
  47.2 1.1 %shard_map.81 = (f32[160,4096]{1,0:T(8,128)S(1)}, f32[160,4096]{1,0:T(8,128)S(1)}, f32[16,160]{1,0:T(8,128)S(1)}, f32[160,128]{1,0:T(8,128)S(1)}, bf16[256,160]{1,0:T(8,128)(2,1)S(1)}) custom-call(f32[160,4096]{1,0:T(8,128)S(1)} %get-tuple-element.49.scaled, f32[160,4096]{1,0:T(8,128)S(1)} %get-tuple-element.50.logits, f32[1,4096]{1,0:T(1,128)S(1)} %get-tuple-element.51.inv, ...), custom_call_target="tpu_custom_call" | custom-call | flops 2621440 | bytes 10485760 | tf_op jit(solution)/shard_map/pallas_call | solution.py:27
  48.3 0.4 collective-permute-done.2.give
  48.7 0.3 shard_map.82
  48.9 15.5 %all_to_all.23 = bf16[32,13,4,128]{3,2,1,0:T(4,128)(2,1)S(1)} all-to-all(bf16[32,13,4,128]{3,2,1,0:T(4,128)(2,1)S(1)} %shard_map.82), channel_id=1, replica_groups=mesh['img'=8,'proto'=4] {'img','proto'}, dimensions={0} | all-to-all | bytes 851968 | tf_op jit(solution)/shard_map/all_to_all | solution.py:601
  64.4 3.4 %shard_map.83 = (f32[384,4096]{1,0:T(8,128)}, f32[16,384]{1,0:T(8,128)}, f32[1,1]{1,0:T(1,128)}) custom-call(bf16[16,2,13,4,128]{4,3,2,1,0:T(4,128)(2,1)S(1)} %bitcast.9, f32[160,4096]{1,0:T(8,128)S(1)} %get-tuple-element.60.pull, f32[160,4096]{1,0:T(8,128)S(1)} %get-tuple-element.61.push, f32[160,4096]{1,0:T(8,128)S(1)} %get-tuple-element.50.logits, ...), custom_call_target="tpu_custom_call" | custom-call | flops 503316480 | bytes 12582912 | tf_op jit(solution)/shard_map/pallas_call | solution.py:27
Async XLA Ops:
  18.1 2.3 %collective-permute-start = (bf16[256,384]{1,0:T(8,128)(2,1)S(1)}, bf16[256,384]{1,0:T(8,128)(2,1)S(1)}, u32[]{:S(2)}, u32[]{:S(2)}) collective-permute-start(bf16[256,384]{1,0:T(8,128)(2,1)S(1)} %bitcast.5), channel_id=1, source_target_pairs={{0,1},{1,0},{2,3},{3,2},{4,5},{5,4},{6,7},{7,6},{8,9},{9,8},{10,11... | collective-permute-start | bytes 589832 | tf_op jit(solution)/shard_map/ppermute | solution.py:511
  20.3 23.4 %copy-start = (bf16[384,4096]{1,0:T(8,128)(2,1)S(1)}, bf16[384,4096]{1,0:T(8,128)(2,1)}, u32[]{:S(2)}) copy-start(bf16[384,4096]{1,0:T(8,128)(2,1)} %stu_w.3) | copy-start | bytes 9437188
  33.4 10.3 %collective-permute-start.1 = (bf16[32,7,4,128]{3,2,1,0:T(4,128)(2,1)S(1)}, bf16[32,7,4,128]{3,2,1,0:T(4,128)(2,1)S(1)}, u32[]{:S(2)}, u32[]{:S(2)}) collective-permute-start(bf16[32,7,4,128]{3,2,1,0:T(4,128)(2,1)S(1)} %all_to_all.21.got.mine), channel_id=1, source_target_pairs={{0,1},{1,0},{2,3},{3,2},{4,5},{5,4},{6,7},{7,6},{8,9},{9,8},{10,11... | collective-permute-start | bytes 688136 | tf_op jit(solution)/shard_map/ppermute | solution.py:550
  47.1 1.5 %collective-permute-start.2 = (bf16[160,768]{1,0:T(8,128)(2,1)S(1)}, bf16[160,768]{1,0:T(8,128)(2,1)S(1)}, u32[]{:S(2)}, u32[]{:S(2)}) collective-permute-start(bf16[160,768]{1,0:T(8,128)(2,1)S(1)} %get-tuple-element.57), channel_id=1, source_target_pairs={{0,1},{1,0},{2,3},{3,2},{4,5},{5,4},{6,7},{7,6},{8,9},{9,8},{10,11... | collective-permute-start | bytes 737288 | tf_op jit(solution)/shard_map/ppermute | solution.py:584

commit v13 on v11

--- a/solution.py
+++ b/solution.py
@@ -352,8 +352,8 @@
         return acc + fold(kc)
 
     zero = jnp.zeros((rows, LANES), F32)
-    total = over_chunks(columns, sweep, zero)
-    part = over_chunks(columns, student, zero)
+    both = lambda at, accs: (sweep(at, accs[0]), student(at, accs[1]))
+    total, part = over_chunks(columns, both, (zero, zero))
     sums = dot(stack[...], stu_w[...], ((1,), (1,)))
     for part_of, lanes in ((sums[:rows], slice(0, feat)), (sums[rows:], slice(feat, 2 * feat))):
         keep_out[:, lanes] = part_of

time: 68.2 us -> 68.2 us (level)
  no operation moved by 1% of the time
where the time goes in v13:
time: 68.2 us; the launch traced here: 68 us
  blocking collectives  52.8 us (77%)
  Pallas kernels  13.3 us (20%)
  starting transfers between devices  0.9 us (1%)
  between operations  0.7 us (1%)
    all_to_all x1, blocking collectives, shards(): mine = exchange(sent.reshape(devices, each, feat)).reshape(half, feat)  16 us
    all_to_all x1, blocking collectives, shards(): got = exchange(sent)  15.5 us
    pallas_call x8, Pallas kernels, call(): pl.pallas_call(body, out_shape=outs, in_specs=specs or [VMEM] * len(args)...  13.3 us
    all_to_all x1, blocking collectives, shards(): stu_mine = exchange(sent.reshape(devices, *sent.shape[2:]))  11.9 us
    all_to_all x1, blocking collectives, shards(): got = near(exchange(sent))  9.48 us
  transfers between devices with their start and end apart: 3, of which 1 were waited for; matrix products, arithmetic and copies ran while one was open for 0% of the time, Pallas kernels for 5%

profile of v13, /device:TPU:0, one launch (start us, length us, event | category | flops | bytes accessed | tf_op | source)
XLA Modules:
  0.0 68.0 jit_solution(5216924891596641409)
XLA Ops:
  0.6 1.5 %shard_map.76 = (bf16[16,16,384]{2,1,0:T(8,128)(2,1)S(1)}, s32[1,128]{1,0:T(1,128)S(1)}, bf16[1,128,384]{2,1,0:T(8,128)(2,1)S(1)}, bf16[384,1536]{1,0:T(8,128)(2,1)S(1)}) custom-call(s32[1,128]{1,0:T(1,128)} %mask_hbm.1, bf16[1,128,384]{2,1,0:T(8,128)(2,1)} %stu_hbm.1, bf16[1,128,384]{2,1,0:T(8,128)(2,1)} %tea_hbm.1, bf16[384,4096]{1,0:T(8,128)(2,1)} %w_hbm.2), custom_call_target="tpu_custom_call" | custom-call | tf_op jit(solution)/shard_map/pallas_call | solution.py:27
  2.1 16.0 %all_to_all.20 = bf16[32,8,384]{2,1,0:T(8,128)(2,1)S(1)} all-to-all(bf16[32,8,384]{2,1,0:T(8,128)(2,1)S(1)} %bitcast.11), channel_id=1, replica_groups=mesh['img'=8,'proto'=4] {'img','proto'}, dimensions={0} | all-to-all | bytes 393216 | tf_op jit(solution)/shard_map/all_to_all | solution.py:509
  18.1 0.6 collective-permute-start
  18.7 1.7 %shard_map.77 = (bf16[384,2560]{1,0:T(8,128)(2,1)S(1)}, f32[1,4096]{1,0:T(1,128)S(1)}, f32[16,384]{1,0:T(8,128)S(1)}, f32[16,128]{1,0:T(8,128)S(1)}, bf16[160,512]{1,0:T(8,128)(2,1)S(1)}) custom-call(bf16[256,384]{1,0:T(8,128)(2,1)S(1)} %bitcast.6, s32[1,128]{1,0:T(1,128)S(1)} %get-tuple-element.39.mask_ref, ...), custom_call_target="tpu_custom_call" | custom-call | flops 3145728 | bytes 6291456 | tf_op jit(solution)/shard_map/pallas_call | solution.py:27
  20.3 0.0 collective-permute-done.other
  20.3 1.2 %shard_map.78 = (f32[160,4096]{1,0:T(8,128)S(1)}, bf16[16,2,7,4,128]{4,3,2,1,0:T(4,128)(2,1)S(1)}) custom-call(bf16[256,384]{1,0:T(8,128)(2,1)S(1)} %bitcast.7, bf16[256,384]{1,0:T(8,128)(2,1)S(1)} %collective-permute-done.other, bf16[384,1536]{1,0:T(8,128)(2,1)S(1)} %get-tuple-element.38.early_w, bf16[384,2560]{1,0:T(8,128)(2,1)S(1)} %get-tuple-element.42.late_w, ...), custom_call_target="tpu_custom_call" | custom-call | flops 503316480 | bytes 2621440 | tf_op jit(solution)/shard_map/pallas_call | solution.py:27
  21.6 0.0 copy-start
  21.6 11.9 %all_to_all.21.got.mine = bf16[32,7,4,128]{3,2,1,0:T(4,128)(2,1)S(1)} all-to-all(bf16[32,7,4,128]{3,2,1,0:T(4,128)(2,1)S(1)} %bitcast.10), channel_id=1, replica_groups=mesh['img'=8,'proto'=4] {'img','proto'}, dimensions={0} | all-to-all | bytes 458752 | tf_op jit(solution)/shard_map/all_to_all | solution.py:549
  33.4 0.2 collective-permute-start.1
  33.6 0.7 %shard_map.79 = f32[32,2,128]{2,1,0:T(2,128)S(1)} custom-call(bf16[32,7,4,128]{3,2,1,0:T(4,128)(2,1)S(1)} %all_to_all.21.got.mine, f32[160,4096]{1,0:T(8,128)S(1)} %get-tuple-element.47.kernel), custom_call_target="tpu_custom_call" | custom-call | flops 2621440 | bytes 2621440 | tf_op jit(solution)/shard_map/pallas_call | solution.py:27
  34.3 9.5 %all_to_all.22.got = f32[32,2,128]{2,1,0:T(2,128)S(1)} all-to-all(f32[32,2,128]{2,1,0:T(2,128)S(1)} %shard_map.79), channel_id=1, replica_groups=mesh['img'=8,'proto'=4] {'img','proto'}, dimensions={0} | all-to-all | bytes 65536 | tf_op jit(solution)/shard_map/all_to_all | solution.py:560
  43.8 0.0 collective-permute-done.1.other
  43.8 0.0 copy-done
  43.8 3.4 %shard_map.80 = (f32[1,4096]{1,0:T(1,128)S(1)}, f32[160,4096]{1,0:T(8,128)S(1)}, f32[160,4096]{1,0:T(8,128)S(1)}, bf16[384,160]{1,0:T(8,128)(2,1)S(1)}, f32[4,12...) custom-call(f32[32,2,128]{2,1,0:T(2,128)S(1)} %all_to_all.22.got, ...), custom_call_target="tpu_custom_call" | custom-call | flops 1509949440 | bytes 7864320 | tf_op jit(solution)/shard_map/pallas_call | solution.py:27
  47.2 0.1 collective-permute-start.2
  47.4 1.1 %shard_map.81 = (f32[160,4096]{1,0:T(8,128)S(1)}, f32[160,4096]{1,0:T(8,128)S(1)}, f32[16,160]{1,0:T(8,128)S(1)}, f32[160,128]{1,0:T(8,128)S(1)}, bf16[256,160]{1,0:T(8,128)(2,1)S(1)}) custom-call(f32[160,4096]{1,0:T(8,128)S(1)} %get-tuple-element.49.scaled, f32[160,4096]{1,0:T(8,128)S(1)} %get-tuple-element.50.logits, f32[1,4096]{1,0:T(1,128)S(1)} %get-tuple-element.51.inv, ...), custom_call_target="tpu_custom_call" | custom-call | flops 2621440 | bytes 10485760 | tf_op jit(solution)/shard_map/pallas_call | solution.py:27
  48.5 0.3 collective-permute-done.2.give
  48.8 0.3 shard_map.82
  49.0 15.5 %all_to_all.23 = bf16[32,13,4,128]{3,2,1,0:T(4,128)(2,1)S(1)} all-to-all(bf16[32,13,4,128]{3,2,1,0:T(4,128)(2,1)S(1)} %shard_map.82), channel_id=1, replica_groups=mesh['img'=8,'proto'=4] {'img','proto'}, dimensions={0} | all-to-all | bytes 851968 | tf_op jit(solution)/shard_map/all_to_all | solution.py:601
  64.5 3.4 %shard_map.83 = (f32[384,4096]{1,0:T(8,128)}, f32[16,384]{1,0:T(8,128)}, f32[1,1]{1,0:T(1,128)}) custom-call(bf16[16,2,13,4,128]{4,3,2,1,0:T(4,128)(2,1)S(1)} %bitcast.9, f32[160,4096]{1,0:T(8,128)S(1)} %get-tuple-element.60.pull, f32[160,4096]{1,0:T(8,128)S(1)} %get-tuple-element.61.push, f32[160,4096]{1,0:T(8,128)S(1)} %get-tuple-element.50.logits, ...), custom_call_target="tpu_custom_call" | custom-call | flops 503316480 | bytes 12582912 | tf_op jit(solution)/shard_map/pallas_call | solution.py:27
Async XLA Ops:
  18.1 2.3 %collective-permute-start = (bf16[256,384]{1,0:T(8,128)(2,1)S(1)}, bf16[256,384]{1,0:T(8,128)(2,1)S(1)}, u32[]{:S(2)}, u32[]{:S(2)}) collective-permute-start(bf16[256,384]{1,0:T(8,128)(2,1)S(1)} %bitcast.5), channel_id=1, source_target_pairs={{0,1},{1,0},{2,3},{3,2},{4,5},{5,4},{6,7},{7,6},{8,9},{9,8},{10,11... | collective-permute-start | bytes 589832 | tf_op jit(solution)/shard_map/ppermute | solution.py:511
  21.6 22.2 %copy-start = (bf16[384,4096]{1,0:T(8,128)(2,1)S(1)}, bf16[384,4096]{1,0:T(8,128)(2,1)}, u32[]{:S(2)}) copy-start(bf16[384,4096]{1,0:T(8,128)(2,1)} %stu_w.3) | copy-start | bytes 9437188
  33.4 10.4 %collective-permute-start.1 = (bf16[32,7,4,128]{3,2,1,0:T(4,128)(2,1)S(1)}, bf16[32,7,4,128]{3,2,1,0:T(4,128)(2,1)S(1)}, u32[]{:S(2)}, u32[]{:S(2)}) collective-permute-start(bf16[32,7,4,128]{3,2,1,0:T(4,128)(2,1)S(1)} %all_to_all.21.got.mine), channel_id=1, source_target_pairs={{0,1},{1,0},{2,3},{3,2},{4,5},{5,4},{6,7},{7,6},{8,9},{9,8},{10,11... | collective-permute-start | bytes 688136 | tf_op jit(solution)/shard_map/ppermute | solution.py:550
  47.2 1.5 %collective-permute-start.2 = (bf16[160,768]{1,0:T(8,128)(2,1)S(1)}, bf16[160,768]{1,0:T(8,128)(2,1)S(1)}, u32[]{:S(2)}, u32[]{:S(2)}) collective-permute-start(bf16[160,768]{1,0:T(8,128)(2,1)S(1)} %get-tuple-element.57), channel_id=1, source_target_pairs={{0,1},{1,0},{2,3},{3,2},{4,5},{5,4},{6,7},{7,6},{8,9},{9,8},{10,11... | collective-permute-start | bytes 737288 | tf_op jit(solution)/shard_map/ppermute | solution.py:584
